TPU v7x, 32 devices: a whole 2x2x4 slice. The times are simulated.
32 devices in a mesh: phase: 4 (over y, x), ctx: 8 (over z, core).
Axes of the slice: x: 2, y: 2, z: 4, core: 2. Of those that a mesh axis runs over, the one named last changes fastest.
Arguments:
- hidden: bfloat16 [4, 1024, 4096], P('phase', 'ctx'), may hold values from -6 to 6
- queries: bfloat16 [4, 1024, 2048], P('phase', 'ctx'), may hold values from -400 to 400
- key_value_weight: bfloat16 [4, 4096, 1024], P('phase'), may hold values from -0.09375 to 0.09375
- doc_ids: int32 [4, 1024], P('phase'), may hold values from 0 to 7, never falling along the last dimension, each value on 1 to 768 neighbouring positions
- scored: int32 [4, 1024], P('phase', 'ctx'), may hold values 0 or 1
Outputs:
- passed: bfloat16 [4, 1024, 2048], P('phase', 'ctx')
Inputs may be any that keep to these rules, and one draw needn't show every extreme that they name: doc_ids never fall along a sequence; one document spans exactly 768 tokens.
All inputs are finite; a program needn't handle non-finite values. No bound on the sum of `scored` on one device may be relied on, other than what follows from the above.
Results may differ from a plain program's by a relative error of at most 0.008.
The roundings to bfloat16 on the way count: a program that leaves them out, or rounds other values in their place, can miss the bound.
Values may be sent and summed in bfloat16 or wider, within the bound.
No kernel may reach another device: no remote copies, remote signals or barrier semaphores. Data moves between devices by JAX's collectives and lax.ppermute only.
A program may use at most 128 MiB of HBM per device.

v0:
```python
import math

import jax
import jax.numpy as jnp
from jax import lax
from jax.sharding import PartitionSpec as P

QUERY_HEADS = 16
KEY_VALUE_HEADS = 4
HEAD_SIZE = 128


rope_base = 500000.0


def from_behind(block, axis, distance):
    devices = range(lax.axis_size(axis))
    route = [((i - distance) % len(devices), i) for i in devices]
    return lax.ppermute(block, axis, route)


def apply_rotary(key_heads, token_positions):
    half_dim = key_heads.shape[-1] // 2
    frequency = rope_base ** (-jnp.arange(half_dim, dtype=jnp.float32) * 2.0 / key_heads.shape[-1])
    angles = token_positions.astype(jnp.float32)[:, None] * frequency[None, :]
    cosine_part = jnp.cos(angles)[:, None, :]
    sine_part = jnp.sin(angles)[:, None, :]
    lower_half = key_heads[..., :half_dim]
    upper_half = key_heads[..., half_dim:]
    return jnp.concatenate(
        [
            lower_half * cosine_part - upper_half * sine_part,
            upper_half * cosine_part + lower_half * sine_part,
        ],
        axis=-1,
    )


def per_device(hidden, queries, key_value_weight, doc_ids, scored):
    count_of_rows = hidden.shape[1]
    first_row = lax.axis_index("ctx") * count_of_rows
    token_positions = first_row + jnp.arange(count_of_rows, dtype=jnp.int32)
    wide = hidden[0].astype(jnp.float32)
    normed = (wide * lax.rsqrt(jnp.mean(wide * wide, axis=-1, keepdims=True) + 1e-05)).astype(
        jnp.bfloat16
    )
    projected_rows = jnp.dot(normed, key_value_weight[0], preferred_element_type=jnp.float32)
    key_value_width = KEY_VALUE_HEADS * HEAD_SIZE
    key_matrix = (
        apply_rotary(
            projected_rows[:, :key_value_width].reshape(count_of_rows, KEY_VALUE_HEADS, HEAD_SIZE),
            token_positions,
        )
        .astype(jnp.bfloat16)
        .reshape(count_of_rows, key_value_width)
    )
    value_matrix = projected_rows[:, key_value_width:].astype(jnp.bfloat16)
    query_group_width = QUERY_HEADS // KEY_VALUE_HEADS
    query_head_count = queries[0].reshape(
        count_of_rows, KEY_VALUE_HEADS, query_group_width, HEAD_SIZE
    )
    sequence_docs = doc_ids[0]
    own_docs = lax.dynamic_slice_in_dim(sequence_docs, first_row, count_of_rows, 0)
    score_scale = 1.0 / math.sqrt(HEAD_SIZE)
    stacked = jnp.concatenate([key_matrix, value_matrix], axis=1)
    collected_rows = lax.all_gather(stacked, "ctx", axis=0, tiled=True)
    sequence_length = collected_rows.shape[0]
    every_key_row = collected_rows[:, :key_value_width].reshape(
        sequence_length, KEY_VALUE_HEADS, HEAD_SIZE
    )
    every_value_row = collected_rows[:, key_value_width:].reshape(
        sequence_length, KEY_VALUE_HEADS, HEAD_SIZE
    )
    head_outputs = []
    for key_value_head in range(KEY_VALUE_HEADS):
        key_part = every_key_row[:, key_value_head : key_value_head + 1]
        key_count = key_part.shape[0]
        scores = (
            jnp.einsum(
                "qhgd,khd->hgqk",
                query_head_count[:, key_value_head : key_value_head + 1],
                key_part,
                preferred_element_type=jnp.float32,
            )
            * score_scale
        )
        key_pos = jnp.arange(key_count, dtype=jnp.int32)
        allowed = (key_pos[None, :] <= token_positions[:, None]) & (
            sequence_docs[None, :] == own_docs[:, None]
        )
        scores = jnp.where(allowed[None, None], scores, jnp.float32(-1e30))
        row_max = jnp.max(scores, axis=-1, keepdims=True)
        expo = jnp.exp(scores - row_max)
        total = jnp.sum(expo, axis=-1)
        weights = expo.astype(jnp.bfloat16)
        summed = jnp.einsum(
            "hgqk,khd->hgqd",
            weights,
            every_value_row[:, key_value_head : key_value_head + 1],
            preferred_element_type=jnp.float32,
        )
        head_outputs.append(summed / total[..., None])
    attended = jnp.transpose(jnp.concatenate(head_outputs, axis=0), (2, 0, 1, 3))
    flat = (
        attended.reshape(count_of_rows, QUERY_HEADS * HEAD_SIZE)
        * scored[0].astype(jnp.float32)[:, None]
    )
    outgoing = flat.astype(jnp.bfloat16)[None]
    return from_behind(outgoing, "phase", 1)


def solution(mesh):
    placed = (
        P("phase", "ctx", None),
        P("phase", "ctx", None),
        P("phase", None, None),
        P("phase", None),
        P("phase", "ctx"),
    )
    return jax.shard_map(
        per_device, mesh=mesh, in_specs=placed, out_specs=P("phase", "ctx", None), check_vma=False
    )
```

profile of v0, /device:TPU:0, one launch (start us, length us, event | category | flops | bytes accessed | tf_op | source)
XLA Modules:
  0.0 79.1 jit_solution(17514824225343585779)
XLA Ops:
  6.5 0.0 all-gather.2.cloned.1.call-start
  6.5 1.5 %fusion.2 = f32[128]{0:T(128)S(1)} fusion(bf16[1,128,4096]{2,1,0:T(8,128)(2,1)} %param.5), kind=kLoop, calls=%fused_computation.4 | loop fusion | flops 1572736 | bytes 1049088 | tf_op jit(solution)/shard_map/reduce_sum | solution.py:44
  8.1 5.0 %fusion = f32[128,1024]{1,0:T(8,128)S(1)} fusion(bf16[1,4096,1024]{2,1,0:T(8,128)(2,1)} %param.7, bf16[1,128,4096]{2,1,0:T(8,128)(2,1)} %param.5, f32[128]{0:T(128)S(1)} %add_rsqrt_fusion), kind=kOutput, calls=%fused_computation | convolution fusion | flops 1075314688 | bytes 9961984 | tf_op jit(solution)/shard_map/dot_general | solution.py:47
  13.1 0.0 copy-start
  13.2 0.0 copy-start.2
  13.2 0.0 copy-start.3
  13.2 0.1 reshape.293
  13.3 0.3 multiply_cosine_fusion
  13.6 0.3 subtract_convert_fusion
  13.9 0.2 pad_maximum_fusion.2
  14.1 0.8 pad_maximum_fusion.1
  14.9 0.0 all-gather.2.cloned.1.call-update
  14.9 0.0 copy-done
  14.9 1.0 %copy.20 = bf16[1,128,2048]{1,2,0:T(8,128)(2,1)} copy(bf16[1,128,2048]{2,1,0:T(8,128)(2,1)S(1)} %copy-done) | data formatting | bytes 1048576 | tf_op args[1]
  15.9 0.0 copy-done.2
  15.9 0.0 copy-done.3
  15.9 0.2 fusion.31
  16.1 30.7 %all-gather.2.cloned.1.call-done = bf16[1024,1024]{1,0:T(8,128)(2,1)} async-done(((bf16[128,1024]{1,0:T(8,128)(2,1)}), bf16[1024,1024]{1,0:T(8,128)(2,1)}) %all-gather.2.cloned.1.call-update) | async-done | bytes 2097168 | tf_op jit(solution)/shard_map/all_gather | solution.py:66
  46.9 1.7 %fusion.33 = (bf16[1024,512]{1,0:T(8,128)(2,1)S(1)}, bf16[1024,512]{1,0:T(8,128)(2,1)S(1)}) fusion(bf16[1024,1024]{1,0:T(8,128)(2,1)} %all-gather.2.cloned.1.call-done), kind=kLoop, calls=%fused_computation.70 | loop fusion | bytes 4194304 | tf_op jit(solution)/shard_map/slice | solution.py:71
  48.5 0.5 copy.41
  49.1 0.3 reshape.294
  49.4 0.0 copy-start.1
  49.4 1.6 %fusion.34 = (bf16[1024,1,128]{2,1,0:T(2,128)(2,1)S(1)}, bf16[1024,1,128]{2,1,0:T(2,128)(2,1)S(1)}, bf16[1024,1,128]{2,1,0:T(2,128)(2,1)S(1)}, bf16[1024,1,128]{2,1,0:T(2,128)(2,1)S(1)}) fusion(bf16[1024,4,128]{2,1,0:T(4,128)(2,1)S(1)} %reshape.294), kind=kLoop, calls=%fused_computation.71 | loop fusion | bytes 2097152 | tf_op jit(solution)/shard_map/slice | solution.py:76
  51.0 0.0 copy-done.1
  51.0 0.4 fusion.38
  51.4 0.4 fusion.36
  51.8 0.3 fusion.4
  52.1 0.5 fusion.15
  52.6 0.3 fusion.8
  52.9 0.5 fusion.13
  53.5 0.4 fusion.37
  53.9 0.3 fusion.6
  54.2 0.5 fusion.14
  54.7 0.4 fusion.35
  55.1 0.3 fusion.10
  55.4 0.5 fusion.12
  55.9 0.1 pad_maximum_fusion
  56.0 0.3 copy.36
  56.4 0.1 multiply_convert_fusion
  56.5 1.5 %collective-permute-start = (bf16[1,128,2048]{2,1,0:T(8,128)(2,1)S(1)}, bf16[1,128,2048]{2,1,0:T(8,128)(2,1)S(1)}, u32[]{:S(2)}, u32[]{:S(2)}) collective-permute-start(bf16[1,128,2048]{2,1,0:T(8,128)(2,1)S(1)} %multiply_convert_fusion), channel_id=1, source_target_pairs={{24,0},{0,8},{8,16},{16,24},{25,1},{1,9},{9,17},{17,25},{26,2},{2,... | collective-permute-start | bytes 1572872 | tf_op jit(solution)/shard_map/ppermute | solution.py:19
  58.0 13.5 %collective-permute-done = bf16[1,128,2048]{2,1,0:T(8,128)(2,1)S(1)} collective-permute-done((bf16[1,128,2048]{2,1,0:T(8,128)(2,1)S(1)}, bf16[1,128,2048]{2,1,0:T(8,128)(2,1)S(1)}, u32[]{:S(2)}, u32[]{:S(2)}) %collective-permute-start) | collective-permute-done | bytes 524320 | tf_op jit(solution)/shard_map/ppermute | solution.py:19
  71.5 0.8 %copy.70 = bf16[1,128,2048]{2,1,0:T(8,128)(2,1)} copy(bf16[1,128,2048]{2,1,0:T(8,128)(2,1)S(1)} %collective-permute-done) | data formatting | bytes 1048576
  (8 shorter events, 0.1 us)
Async XLA Ops:
  6.5 40.3 %all-gather.2.cloned.1.call-start = ((), (), s32[]{:S(2)}) async-start(), calls=%async_computation | async-start | bytes 2359296 | tf_op jit(solution)/shard_map/all_gather | solution.py:66
  13.1 1.8 %copy-start = (bf16[1,128,2048]{2,1,0:T(8,128)(2,1)S(1)}, bf16[1,128,2048]{2,1,0:T(8,128)(2,1)}, u32[]{:S(2)}) copy-start(bf16[1,128,2048]{2,1,0:T(8,128)(2,1)} %param.6) | copy-start | bytes 1572868
  13.2 2.8 %copy-start.2 = (s32[1,1024]{1,0:T(1,128)S(1)}, s32[1,1024]{1,0:T(1,128)}, u32[]{:S(2)}) copy-start(s32[1,1024]{1,0:T(1,128)} %param.8) | copy-start | bytes 12292
  13.2 2.7 %copy-start.3 = (s32[1,128]{1,0:T(1,128)S(1)}, s32[1,128]{1,0:T(1,128)}, u32[]{:S(2)}) copy-start(s32[1,128]{1,0:T(1,128)} %param.9) | copy-start | bytes 1540
  49.4 1.6 %copy-start.1 = (bf16[1,128,2048]{1,2,0:T(8,128)(2,1)S(1)}, bf16[1,128,2048]{1,2,0:T(8,128)(2,1)}, u32[]{:S(2)}) copy-start(bf16[1,128,2048]{1,2,0:T(8,128)(2,1)} %copy.20) | copy-start | bytes 1572868
  56.5 15.0 %collective-permute-start = (bf16[1,128,2048]{2,1,0:T(8,128)(2,1)S(1)}, bf16[1,128,2048]{2,1,0:T(8,128)(2,1)S(1)}, u32[]{:S(2)}, u32[]{:S(2)}) collective-permute-start(bf16[1,128,2048]{2,1,0:T(8,128)(2,1)S(1)} %multiply_convert_fusion), channel_id=1, source_target_pairs={{24,0},{0,8},{8,16},{16,24},{25,1},{1,9},{9,17},{17,25},{26,2},{2,... | collective-permute-start | bytes 1572872 | tf_op jit(solution)/shard_map/ppermute | solution.py:19
Sparse Core Ops, SparseCore 0:
  15.0 31.7 all-gather.1
where the time goes:
time: 79.3 us; the launch traced here: 79.1 us
  waiting for transfers between devices  44.2 us (56%)
  between operations  13.6 us (17%)
  matrix products  8.73 us (11%)
  local copies, waits for them, and re-layouts  6.35 us (8%)
  other arithmetic  4.67 us (6%)
  starting transfers between devices  1.52 us (2%)
    all_gather x1, waiting for transfers between devices, per_device(): collected_rows = lax.all_gather(stacked, 'ctx', axis=0, tiled=True)  30.7 us
    ppermute x1, waiting for transfers between devices, from_behind(): return lax.ppermute(block, axis, route)  13.5 us
    dot_general x1, matrix products, per_device(): jnp.dot(normed, key_value_weight[0], preferred_element_type=jnp.float32)  5.02 us
    dot_general x4, matrix products, per_device(): jnp.einsum('hgqk,khd->hgqd', weights, every_value_row[:, key_value_head:k...  1.98 us
    unnamed x11, local copies, waits for them, and re-layouts  1.84 us
    dot_general x4, matrix products, per_device(): jnp.einsum('qhgd,khd->hgqk', query_head_count[:, key_value_head:key_value...  1.74 us
    slice x1, local copies, waits for them, and re-layouts, per_device(): collected_rows[:, key_value_width:]  1.68 us
  transfers between devices with their start and end apart: 2, of which 2 were waited for; matrix products, arithmetic and copies ran while one was open for 2% of the time, Pallas kernels for 0%

commit v1 on v0

--- a/solution.py
+++ b/solution.py
@@ -1,14 +1,21 @@
+import functools
 import math
 
 import jax
 import jax.numpy as jnp
+import numpy as np
 from jax import lax
+from jax.experimental import pallas as pl
+from jax.experimental.pallas import tpu as pltpu
 from jax.sharding import PartitionSpec as P
 
 QUERY_HEADS = 16
 KEY_VALUE_HEADS = 4
 HEAD_SIZE = 128
-
+GROUP = QUERY_HEADS // KEY_VALUE_HEADS
+GROUP_WIDTH = GROUP * HEAD_SIZE
+PAIR_WIDTH = 2 * HEAD_SIZE
+MASKED = -1e30
 
 rope_base = 500000.0
 
@@ -36,7 +43,7 @@
     )
 
 
-def per_device(hidden, queries, key_value_weight, doc_ids, scored):
+def gathered_everywhere(hidden, queries, key_value_weight, doc_ids, scored):
     count_of_rows = hidden.shape[1]
     first_row = lax.axis_index("ctx") * count_of_rows
     token_positions = first_row + jnp.arange(count_of_rows, dtype=jnp.int32)
@@ -55,10 +62,7 @@
         .reshape(count_of_rows, key_value_width)
     )
     value_matrix = projected_rows[:, key_value_width:].astype(jnp.bfloat16)
-    query_group_width = QUERY_HEADS // KEY_VALUE_HEADS
-    query_head_count = queries[0].reshape(
-        count_of_rows, KEY_VALUE_HEADS, query_group_width, HEAD_SIZE
-    )
+    query_head_count = queries[0].reshape(count_of_rows, KEY_VALUE_HEADS, GROUP, HEAD_SIZE)
     sequence_docs = doc_ids[0]
     own_docs = lax.dynamic_slice_in_dim(sequence_docs, first_row, count_of_rows, 0)
     score_scale = 1.0 / math.sqrt(HEAD_SIZE)
@@ -88,7 +92,7 @@
         allowed = (key_pos[None, :] <= token_positions[:, None]) & (
             sequence_docs[None, :] == own_docs[:, None]
         )
-        scores = jnp.where(allowed[None, None], scores, jnp.float32(-1e30))
+        scores = jnp.where(allowed[None, None], scores, jnp.float32(MASKED))
         row_max = jnp.max(scores, axis=-1, keepdims=True)
         expo = jnp.exp(scores - row_max)
         total = jnp.sum(expo, axis=-1)
@@ -109,6 +113,296 @@
     return from_behind(outgoing, "phase", 1)
 
 
+def rotary_table(positions):
+    half = HEAD_SIZE // 2
+    frequency = (rope_base ** (-np.arange(half) * 2.0 / HEAD_SIZE)).astype(np.float32)
+    angles = (np.arange(positions, dtype=np.float32)[:, None] * frequency[None, :]).astype(np.float64)
+    cosine, sine = np.cos(angles), np.sin(angles)
+    return np.concatenate([cosine, cosine, -sine, sine], axis=1).astype(np.float32)
+
+
+def project_kernel(
+    blocks,
+    hidden,
+    table,
+    queries,
+    weight,
+    keep_a,
+    keep_b,
+    give,
+    q_a,
+    q_a_give,
+    q_b,
+    q_b_give,
+    weight_store,
+    normed,
+    weight_sems,
+    query_sems,
+):
+    core = lax.rem(lax.axis_index("ctx"), 2)
+    depth = weight.shape[1] // blocks
+    copies = []
+    for i in range(blocks):
+        copy = pltpu.make_async_copy(
+            weight.at[0, pl.ds(i * depth, depth), :], weight_store.at[i], weight_sems.at[i]
+        )
+        copy.start()
+        copies.append(copy)
+    first = core * (2 * GROUP_WIDTH)
+    second = (1 - core) * (2 * GROUP_WIDTH)
+    cuts = []
+    for i, (start, target) in enumerate(
+        (
+            (first, q_a),
+            (second, q_a_give),
+            (first + GROUP_WIDTH, q_b),
+            (second + GROUP_WIDTH, q_b_give),
+        )
+    ):
+        cut = pltpu.make_async_copy(
+            queries.at[0, :, pl.ds(pl.multiple_of(start, GROUP_WIDTH), GROUP_WIDTH)],
+            target,
+            query_sems.at[i],
+        )
+        cut.start()
+        cuts.append(cut)
+    wide = hidden[0].astype(jnp.float32)
+    scale = lax.rsqrt(jnp.mean(wide * wide, axis=-1, keepdims=True) + 1e-05)
+    normed[...] = (wide * scale).astype(jnp.bfloat16)
+    total = None
+    for i in range(blocks):
+        copies[i].wait()
+        part = jnp.dot(
+            normed[:, i * depth : (i + 1) * depth],
+            weight_store[i],
+            preferred_element_type=jnp.float32,
+        )
+        total = part if total is None else total + part
+    cosine, sine = table[:, :HEAD_SIZE], table[:, HEAD_SIZE:]
+    pairs = []
+    for head in range(KEY_VALUE_HEADS):
+        key = total[:, head * HEAD_SIZE : (head + 1) * HEAD_SIZE]
+        key = key * cosine + pltpu.roll(key, HEAD_SIZE // 2, 1) * sine
+        at = (KEY_VALUE_HEADS + head) * HEAD_SIZE
+        value = total[:, at : at + HEAD_SIZE]
+        pairs.append(jnp.concatenate([key, value], axis=1).astype(jnp.bfloat16))
+
+    for mine in range(2):
+
+        @pl.when(core == mine)
+        def _():
+            keep_a[...] = pairs[2 * mine]
+            keep_b[...] = pairs[2 * mine + 1]
+            give[:, :PAIR_WIDTH] = pairs[2 * (1 - mine)]
+            give[:, PAIR_WIDTH:] = pairs[2 * (1 - mine) + 1]
+
+    for cut in cuts:
+        cut.wait()
+
+
+def project(hidden, queries, weight, table):
+    rows, width = hidden.shape[1], hidden.shape[2]
+    columns = weight.shape[2]
+    blocks = 8
+    pair = jax.ShapeDtypeStruct((rows, PAIR_WIDTH), jnp.bfloat16)
+    cut = jax.ShapeDtypeStruct((rows, GROUP_WIDTH), jnp.bfloat16)
+    vmem = pl.BlockSpec(memory_space=pltpu.VMEM)
+    hbm = pl.BlockSpec(memory_space=pl.ANY)
+    return pl.pallas_call(
+        functools.partial(project_kernel, blocks),
+        grid=(1,),
+        out_shape=(
+            pair,
+            pair,
+            jax.ShapeDtypeStruct((rows, 2 * PAIR_WIDTH), jnp.bfloat16),
+            cut,
+            cut,
+            cut,
+            cut,
+        ),
+        in_specs=[
+            vmem,
+            pl.BlockSpec((rows, 2 * HEAD_SIZE), lambda i: (lax.axis_index("ctx"), 0)),
+            hbm,
+            hbm,
+        ],
+        out_specs=(vmem, vmem, vmem, hbm, hbm, hbm, hbm),
+        scratch_shapes=[
+            pltpu.VMEM((blocks, width // blocks, columns), jnp.bfloat16),
+            pltpu.VMEM((rows, width), jnp.bfloat16),
+            pltpu.SemaphoreType.DMA((blocks,)),
+            pltpu.SemaphoreType.DMA((4,)),
+        ],
+        compiler_params=pltpu.CompilerParams(vmem_limit_bytes=40 * 2**20),
+        cost_estimate=pl.CostEstimate(
+            flops=2 * rows * width * columns,
+            bytes_accessed=2 * (width * columns + rows * width),
+            transcendentals=0,
+        ),
+        name="project",
+    )(hidden, table, queries, weight)
+
+
+def attend_kernel(q_own, q_other, kv_0, kv_1, kv_2, kv_3, docs, out_own, out_other, bias):
+    rows = q_own.shape[0]
+    place = lax.axis_index("ctx")
+    chip, core = place // 2, lax.rem(place, 2)
+    cores = (core, 1 - core)
+    row_at = lax.broadcasted_iota(jnp.int32, (rows, rows), 0)
+    key_at = lax.broadcasted_iota(jnp.int32, (rows, rows), 1)
+
+    def docs_of(device):
+        start = pl.multiple_of(device * rows, rows)
+        row = docs[:, pl.ds(start, rows)].astype(jnp.float32)
+        return jnp.broadcast_to(row, (rows, rows))
+
+    for a in range(2):
+        query_docs = docs_of(2 * chip + cores[a]).T
+        for back in range(4):
+            for b in range(2):
+                block = chip - back
+                key_docs = docs_of(2 * jnp.maximum(block, 0) + cores[b])
+                key_docs = jnp.where(block >= 0, key_docs, -1.0)
+                allowed = query_docs == key_docs
+                if back == 0:
+                    allowed &= cores[a] * rows + row_at >= cores[b] * rows + key_at
+                at = (2 * back + b) * rows
+                bias[a * rows : (a + 1) * rows, at : at + rows] = jnp.where(allowed, 0.0, MASKED)
+
+    blocks = (kv_0, kv_1, kv_2, kv_3)
+    factor = math.log2(math.e) / math.sqrt(HEAD_SIZE)
+    for head in range(GROUP):
+        at = head * HEAD_SIZE
+        q = jnp.concatenate([q_own[:, at : at + HEAD_SIZE], q_other[:, at : at + HEAD_SIZE]], axis=0)
+        scores = []
+        for back, kv in enumerate(blocks):
+            part = lax.dot_general(
+                q,
+                kv[:, :HEAD_SIZE],
+                (((1,), (1,)), ((), ())),
+                preferred_element_type=jnp.float32,
+            )
+            scores.append(part + bias[:, 2 * back * rows : 2 * (back + 1) * rows])
+        scores = jnp.concatenate(scores, axis=1)
+        row_max = jnp.max(scores, axis=-1, keepdims=True)
+        expo = jnp.exp2((scores - row_max) * factor)
+        total = jnp.sum(expo, axis=-1, keepdims=True)
+        weights = expo.astype(jnp.bfloat16)
+        summed = None
+        for back, kv in enumerate(blocks):
+            part = jnp.dot(
+                weights[:, 2 * back * rows : 2 * (back + 1) * rows],
+                kv[:, HEAD_SIZE:],
+                preferred_element_type=jnp.float32,
+            )
+            summed = part if summed is None else summed + part
+        result = (summed / total).astype(jnp.bfloat16)
+        out_own[:, at : at + HEAD_SIZE] = result[:rows]
+        out_other[:, at : at + HEAD_SIZE] = result[rows:]
+
+
+def attend(q_own, q_other, blocks, docs):
+    rows = q_own.shape[0]
+    vmem = pl.BlockSpec(memory_space=pltpu.VMEM)
+    out = jax.ShapeDtypeStruct((rows, GROUP_WIDTH), jnp.bfloat16)
+    work = GROUP * 2 * rows * 8 * rows
+    return pl.pallas_call(
+        attend_kernel,
+        out_shape=(out, out),
+        in_specs=[vmem] * 7,
+        out_specs=(vmem, vmem),
+        scratch_shapes=[pltpu.VMEM((2 * rows, 8 * rows), jnp.float32)],
+        compiler_params=pltpu.CompilerParams(vmem_limit_bytes=40 * 2**20),
+        cost_estimate=pl.CostEstimate(
+            flops=4 * work * HEAD_SIZE, bytes_accessed=2**20, transcendentals=work
+        ),
+        name="attend",
+    )(q_own, q_other, *blocks, docs)
+
+
+def assemble_kernel(a_own, a_other, b_own, b_other, notes, out):
+    rows = a_own.shape[0]
+    core = lax.rem(lax.axis_index("ctx"), 2)
+    kept = notes[:, notes.shape[1] - rows :].astype(jnp.float32)
+    kept = jnp.broadcast_to(kept, (rows, rows)).T
+
+    def put(at, part):
+        for i in range(GROUP):
+            cut = part[:, i * HEAD_SIZE : (i + 1) * HEAD_SIZE].astype(jnp.float32) * kept
+            out[0, :, at + i * HEAD_SIZE : at + (i + 1) * HEAD_SIZE] = cut.astype(jnp.bfloat16)
+
+    for mine in range(2):
+
+        @pl.when(core == mine)
+        def _():
+            put(2 * mine * GROUP_WIDTH, a_own)
+            put((2 * mine + 1) * GROUP_WIDTH, b_own)
+            put(2 * (1 - mine) * GROUP_WIDTH, a_other)
+            put((2 * (1 - mine) + 1) * GROUP_WIDTH, b_other)
+
+
+def assemble(a_own, a_other, b_own, b_other, notes):
+    rows = a_own.shape[0]
+    vmem = pl.BlockSpec(memory_space=pltpu.VMEM)
+    return pl.pallas_call(
+        assemble_kernel,
+        out_shape=jax.ShapeDtypeStruct((1, rows, QUERY_HEADS * HEAD_SIZE), jnp.bfloat16),
+        in_specs=[vmem] * 5,
+        out_specs=vmem,
+        name="assemble",
+    )(a_own, a_other, b_own, b_other, notes)
+
+
+def up(block, chips, first=0):
+    count = lax.axis_size("ctx")
+    route = [(i, i + 2 * chips) for i in range(2 * first, count - 2 * chips)]
+    return lax.ppermute(block, "ctx", route)
+
+
+def across(block):
+    return lax.ppermute(block, "ctx", [(i, i ^ 1) for i in range(lax.axis_size("ctx"))])
+
+
+def onward(block, cross=0):
+    sections, count = lax.axis_size("phase"), lax.axis_size("ctx")
+    route = [
+        (p * count + c, (p + 1) % sections * count + (c ^ cross))
+        for p in range(sections)
+        for c in range(count)
+    ]
+    return lax.ppermute(block, ("phase", "ctx"), route)
+
+
+def behind(block):
+    one = up(block, 1)
+    two = up(one, 1, 1)
+    three = up(one, 2, 1)
+    return one, two, three
+
+
+def relayed(hidden, queries, key_value_weight, doc_ids, scored):
+    table = jnp.asarray(rotary_table(doc_ids.shape[1]))
+    notes = onward(jnp.concatenate([doc_ids, scored], axis=1))
+    keep_a, keep_b, give, q_a, q_a_give, q_b, q_b_give = project(
+        hidden, queries, key_value_weight, table
+    )
+    taken = across(give)
+    block_a = jnp.concatenate([keep_a, taken[:, :PAIR_WIDTH]], axis=0)
+    block_b = jnp.concatenate([keep_b, taken[:, PAIR_WIDTH:]], axis=0)
+    far_a = behind(block_a)
+    block_b = onward(block_b)
+    q_a_other = across(q_a_give)
+    q_b_own = onward(q_b)
+    q_b_other = onward(q_b_give, 1)
+    far_b = behind(block_b)
+    a_own, a_other = attend(q_a, q_a_other, (block_a,) + far_a, doc_ids)
+    a_own = onward(a_own)
+    a_other = onward(a_other, 1)
+    b_own, b_other = attend(q_b_own, q_b_other, (block_b,) + far_b, notes)
+    b_other = across(b_other)
+    return assemble(a_own, a_other, b_own, b_other, notes)
+
+
 def solution(mesh):
     placed = (
         P("phase", "ctx", None),
@@ -117,6 +411,7 @@
         P("phase", None),
         P("phase", "ctx"),
     )
+    plan = relayed if mesh.shape["ctx"] == 8 else gathered_everywhere
     return jax.shard_map(
-        per_device, mesh=mesh, in_specs=placed, out_specs=P("phase", "ctx", None), check_vma=False
-    )
+        plan, mesh=mesh, in_specs=placed, out_specs=P("phase", "ctx", None), check_vma=False
+    )

time: 79.3 us -> 48.7 us (0.61)
  the two profiles are of different devices: /device:TPU:0 before, /device:TPU:25 now
where the time goes in v1:
time: 48.7 us; the launch traced here: 48.3 us
  starting transfers between devices  17.4 us (36%)
  waiting for transfers between devices  13.1 us (27%)
  Pallas kernels  9.46 us (19%)
  local copies, waits for them, and re-layouts  8.21 us (17%)
    ppermute x6, starting transfers between devices, onward(): return lax.ppermute(block, ('phase', 'ctx'), route)  8.25 us
    unnamed x22, local copies, waits for them, and re-layouts  8.2 us
    ppermute x6, starting transfers between devices, up(): return lax.ppermute(block, 'ctx', route)  7.72 us
    ppermute x6, waiting for transfers between devices, onward(): return lax.ppermute(block, ('phase', 'ctx'), route)  7.03 us
    ppermute x6, waiting for transfers between devices, up(): return lax.ppermute(block, 'ctx', route)  5.04 us
    pallas_call x2, Pallas kernels, attend(): pl.pallas_call(attend_kernel, out_shape=(out, out), in_specs=[vmem] * 7,...  4.44 us
    pallas_call x1, Pallas kernels, project(): pl.pallas_call(functools.partial(project_kernel, blocks), grid=(1,), out_...  2.91 us
    pallas_call x1, Pallas kernels, assemble(): pl.pallas_call(assemble_kernel, out_shape=jax.ShapeDtypeStruct((1, rows,...  2.12 us
  transfers between devices with their start and end apart: 15, of which 7 were waited for; matrix products, arithmetic and copies ran while one was open for 0% of the time, Pallas kernels for 9%

profile of v1, /device:TPU:25, one launch (start us, length us, event | category | flops | bytes accessed | tf_op | source)
XLA Modules:
  0.0 48.3 jit_solution(4965479132281917328)
XLA Ops:
  0.0 0.0 copy-start
  0.0 3.4 %copy-done = bf16[1,4096,1024]{2,1,0:T(8,128)(2,1)S(1)} copy-done((bf16[1,4096,1024]{2,1,0:T(8,128)(2,1)S(1)}, bf16[1,4096,1024]{2,1,0:T(8,128)(2,1)}, u32[]{:S(2)}) %copy-start) | copy-done | bytes 8388632
  3.4 0.0 copy-start.1
  3.4 1.2 %copy-done.1 = bf16[1,128,4096]{2,1,0:T(8,128)(2,1)S(1)} copy-done((bf16[1,128,4096]{2,1,0:T(8,128)(2,1)S(1)}, bf16[1,128,4096]{2,1,0:T(8,128)(2,1)}, u32[]{:S(2)}) %copy-start.1) | copy-done | bytes 1048600
  4.6 0.0 copy-start.2
  4.6 1.2 %copy-done.2 = f32[1024,256]{1,0:T(8,128)S(1)} copy-done((f32[1024,256]{1,0:T(8,128)S(1)}, f32[1024,256]{1,0:T(8,128)}, u32[]{:S(2)}) %copy-start.2) | copy-done | bytes 1048600
  5.8 1.0 %copy-done.3 = bf16[1,128,2048]{2,1,0:T(8,128)(2,1)S(1)} copy-done((bf16[1,128,2048]{2,1,0:T(8,128)(2,1)S(1)}, bf16[1,128,2048]{2,1,0:T(8,128)(2,1)}, u32[]{:S(2)}) %copy-start.3) | copy-done | bytes 524312
  6.9 2.9 %project.1 = (bf16[128,256]{1,0:T(8,128)(2,1)S(1)}, bf16[128,256]{1,0:T(8,128)(2,1)S(1)}, bf16[128,512]{1,0:T(8,128)(2,1)S(1)}, bf16[128,512]{1,0:T(8,128)(2,1)S...) custom-call(bf16[1,128,4096]{2,1,0:T(8,128)(2,1)S(1)} %copy-done.1, ...), custom_call_target="tpu_custom_call" | custom-call | flops 1073741824 | bytes 9437184 | tf_op jit(solution)/shard_map/project/pallas_call | solution.py:211
  9.8 0.7 %collective-permute-start.1 = (bf16[128,512]{1,0:T(8,128)(2,1)S(1)}, bf16[128,512]{1,0:T(8,128)(2,1)S(1)}, u32[]{:S(2)}, u32[]{:S(2)}) collective-permute-start(bf16[128,512]{1,0:T(8,128)(2,1)S(1)} %get-tuple-element.19), channel_id=1, source_target_pairs={{0,1},{1,0},{2,3},{3,2},{4,5},{5,4},{6,7},{7,6},{8,9},{9,8},{10,11... | collective-permute-start | bytes 393224 | tf_op jit(solution)/shard_map/ppermute | solution.py:363
  10.5 1.0 %collective-permute-done.1 = bf16[128,512]{1,0:T(8,128)(2,1)S(1)} collective-permute-done((bf16[128,512]{1,0:T(8,128)(2,1)S(1)}, bf16[128,512]{1,0:T(8,128)(2,1)S(1)}, u32[]{:S(2)}, u32[]{:S(2)}) %collective-permute-start.1) | collective-permute-done | bytes 131104 | tf_op jit(solution)/shard_map/ppermute | solution.py:363
  11.5 1.3 %collective-permute-start.9 = (bf16[256,256]{1,0:T(8,128)(2,1)S(1)}, bf16[256,256]{1,0:T(8,128)(2,1)S(1)}, u32[]{:S(2)}, u32[]{:S(2)}) collective-permute-start(bf16[256,256]{1,0:T(8,128)(2,1)S(1)} %pad_maximum_fusion.1), channel_id=1, source_target_pairs={{0,8},{1,9},{2,10},{3,11},{4,12},{5,13},{6,14},{7,15},{8,16},{9,17... | collective-permute-start | bytes 393224 | tf_op jit(solution)/shard_map/ppermute | solution.py:373
  12.8 1.3 %collective-permute-start.2 = (bf16[256,256]{1,0:T(8,128)(2,1)S(1)}, bf16[256,256]{1,0:T(8,128)(2,1)S(1)}, u32[]{:S(2)}, u32[]{:S(2)}) collective-permute-start(bf16[256,256]{1,0:T(8,128)(2,1)S(1)} %pad_maximum_fusion.kv_0), channel_id=1, source_target_pairs={{0,2},{1,3},{2,4},{3,5},{4,6},{5,7},{8,10},{9,11},{10,12},{11,13},... | collective-permute-start | bytes 393224 | tf_op jit(solution)/shard_map/ppermute | solution.py:359
  14.1 0.7 %collective-permute-start = (bf16[128,512]{1,0:T(8,128)(2,1)S(1)}, bf16[128,512]{1,0:T(8,128)(2,1)S(1)}, u32[]{:S(2)}, u32[]{:S(2)}) collective-permute-start(bf16[128,512]{1,0:T(8,128)(2,1)S(1)} %get-tuple-element.17), channel_id=1, source_target_pairs={{0,1},{1,0},{2,3},{3,2},{4,5},{5,4},{6,7},{7,6},{8,9},{9,8},{10,11... | collective-permute-start | bytes 393224 | tf_op jit(solution)/shard_map/ppermute | solution.py:363
  14.8 2.4 %collective-permute-done.9.kv_0 = bf16[256,256]{1,0:T(8,128)(2,1)S(1)} collective-permute-done((bf16[256,256]{1,0:T(8,128)(2,1)S(1)}, bf16[256,256]{1,0:T(8,128)(2,1)S(1)}, u32[]{:S(2)}, u32[]{:S(2)}) %collective-permute-start.9) | collective-permute-done | bytes 131104 | tf_op jit(solution)/shard_map/ppermute | solution.py:373
  17.2 1.3 %collective-permute-start.10 = (bf16[256,256]{1,0:T(8,128)(2,1)S(1)}, bf16[256,256]{1,0:T(8,128)(2,1)S(1)}, u32[]{:S(2)}, u32[]{:S(2)}) collective-permute-start(bf16[256,256]{1,0:T(8,128)(2,1)S(1)} %collective-permute-done.9.kv_0), channel_id=1, source_target_pairs={{0,2},{1,3},{2,4},{3,5},{4,6},{5,7},{8,10},{9,11},{10,12},{11,13},... | collective-permute-start | bytes 393224 | tf_op jit(solution)/shard_map/ppermute | solution.py:359
  18.5 0.6 %collective-permute-done.2.kv_1 = bf16[256,256]{1,0:T(8,128)(2,1)S(1)} collective-permute-done((bf16[256,256]{1,0:T(8,128)(2,1)S(1)}, bf16[256,256]{1,0:T(8,128)(2,1)S(1)}, u32[]{:S(2)}, u32[]{:S(2)}) %collective-permute-start.2) | collective-permute-done | bytes 131104 | tf_op jit(solution)/shard_map/ppermute | solution.py:359
  19.1 1.3 %collective-permute-start.3 = (bf16[256,256]{1,0:T(8,128)(2,1)S(1)}, bf16[256,256]{1,0:T(8,128)(2,1)S(1)}, u32[]{:S(2)}, u32[]{:S(2)}) collective-permute-start(bf16[256,256]{1,0:T(8,128)(2,1)S(1)} %collective-permute-done.2.kv_1), channel_id=1, source_target_pairs={{2,4},{3,5},{4,6},{5,7},{10,12},{11,13},{12,14},{13,15},{18,20},{1... | collective-permute-start | bytes 393224 | tf_op jit(solution)/shard_map/ppermute | solution.py:359
  20.4 1.3 %collective-permute-start.7 = (bf16[128,512]{1,0:T(8,128)(2,1)S(1)}, bf16[128,512]{1,0:T(8,128)(2,1)S(1)}, u32[]{:S(2)}, u32[]{:S(2)}) collective-permute-start(bf16[128,512]{1,0:T(8,128)(2,1)S(1)} %get-tuple-element.22), channel_id=1, source_target_pairs={{0,8},{1,9},{2,10},{3,11},{4,12},{5,13},{6,14},{7,15},{8,16},{9,17... | collective-permute-start | bytes 393224 | tf_op jit(solution)/shard_map/ppermute | solution.py:373
  21.7 2.9 %collective-permute-start.8 = (bf16[128,512]{1,0:T(8,128)(2,1)S(1)}, bf16[128,512]{1,0:T(8,128)(2,1)S(1)}, u32[]{:S(2)}, u32[]{:S(2)}) collective-permute-start(bf16[128,512]{1,0:T(8,128)(2,1)S(1)} %get-tuple-element.23), channel_id=1, source_target_pairs={{0,9},{1,8},{2,11},{3,10},{4,13},{5,12},{6,15},{7,14},{8,17},{9,16... | collective-permute-start | bytes 393224 | tf_op jit(solution)/shard_map/ppermute | solution.py:373
  24.6 0.0 collective-permute-done.q_other
  24.6 1.3 %collective-permute-start.4 = (bf16[256,256]{1,0:T(8,128)(2,1)S(1)}, bf16[256,256]{1,0:T(8,128)(2,1)S(1)}, u32[]{:S(2)}, u32[]{:S(2)}) collective-permute-start(bf16[256,256]{1,0:T(8,128)(2,1)S(1)} %collective-permute-done.2.kv_1), channel_id=1, source_target_pairs={{2,6},{3,7},{10,14},{11,15},{18,22},{19,23},{26,30},{27,31}} | collective-permute-start | bytes 393224 | tf_op jit(solution)/shard_map/ppermute | solution.py:359
  25.9 0.0 collective-permute-done.10.kv_1
  25.9 1.3 %collective-permute-start.11 = (bf16[256,256]{1,0:T(8,128)(2,1)S(1)}, bf16[256,256]{1,0:T(8,128)(2,1)S(1)}, u32[]{:S(2)}, u32[]{:S(2)}) collective-permute-start(bf16[256,256]{1,0:T(8,128)(2,1)S(1)} %collective-permute-done.10.kv_1), channel_id=1, source_target_pairs={{2,4},{3,5},{4,6},{5,7},{10,12},{11,13},{12,14},{13,15},{18,20},{1... | collective-permute-start | bytes 393224 | tf_op jit(solution)/shard_map/ppermute | solution.py:359
  27.2 0.0 collective-permute-done.3.kv_2
  27.2 1.3 %collective-permute-start.12 = (bf16[256,256]{1,0:T(8,128)(2,1)S(1)}, bf16[256,256]{1,0:T(8,128)(2,1)S(1)}, u32[]{:S(2)}, u32[]{:S(2)}) collective-permute-start(bf16[256,256]{1,0:T(8,128)(2,1)S(1)} %collective-permute-done.10.kv_1), channel_id=1, source_target_pairs={{2,6},{3,7},{10,14},{11,15},{18,22},{19,23},{26,30},{27,31}} | collective-permute-start | bytes 393224 | tf_op jit(solution)/shard_map/ppermute | solution.py:359
  28.5 0.0 copy-done.6
  28.5 0.0 copy-done.10
  28.5 4.4 %collective-permute-done.4.kv_3 = bf16[256,256]{1,0:T(8,128)(2,1)S(1)} collective-permute-done((bf16[256,256]{1,0:T(8,128)(2,1)S(1)}, bf16[256,256]{1,0:T(8,128)(2,1)S(1)}, u32[]{:S(2)}, u32[]{:S(2)}) %collective-permute-start.4) | collective-permute-done | bytes 131104 | tf_op jit(solution)/shard_map/ppermute | solution.py:359
  32.9 0.8 %collective-permute-start.13 = (s32[1,1152]{1,0:T(1,128)S(1)}, s32[1,1152]{1,0:T(1,128)S(1)}, u32[]{:S(2)}, u32[]{:S(2)}) collective-permute-start(s32[1,1152]{1,0:T(1,128)S(1)} %pad_add_fusion), channel_id=1, source_target_pairs={{0,8},{1,9},{2,10},{3,11},{4,12},{5,13},{6,14},{7,15},{8,16},{9,17... | collective-permute-start | bytes 13832 | tf_op jit(solution)/shard_map/ppermute | solution.py:373
  33.7 2.2 %attend.2 = (bf16[128,512]{1,0:T(8,128)(2,1)S(1)}, bf16[128,512]{1,0:T(8,128)(2,1)S(1)}) custom-call(bf16[128,512]{1,0:T(8,128)(2,1)S(1)} %get-tuple-element.16.q_own, bf16[128,512]{1,0:T(8,128)(2,1)S(1)} %collective-permute-done.q_other, bf16[256,256]{1,0:T(8,128)(2,1)S(1)} %pad_maximum_fusion.kv_0, bf16[256,256]{1,0:T(8,128)(2,1)S(1)} %collective-permute-done.2.kv_1, ...), custom_call_target="tpu_custom_call" | custom-call | flops 536870912 | bytes 1048576 | tf_op jit(solution)/shard_map/attend/pallas_call | solution.py:309
  36.0 0.6 %collective-permute-done.13.docs.notes = s32[1,1152]{1,0:T(1,128)S(1)} collective-permute-done((s32[1,1152]{1,0:T(1,128)S(1)}, s32[1,1152]{1,0:T(1,128)S(1)}, u32[]{:S(2)}, u32[]{:S(2)}) %collective-permute-start.13) | collective-permute-done | bytes 4640 | tf_op jit(solution)/shard_map/ppermute | solution.py:373
  36.6 0.2 collective-permute-start.5
  36.8 0.0 collective-permute-done.7.q_own
  36.8 1.8 %collective-permute-start.6 = (bf16[128,512]{1,0:T(8,128)(2,1)S(1)}, bf16[128,512]{1,0:T(8,128)(2,1)S(1)}, u32[]{:S(2)}, u32[]{:S(2)}) collective-permute-start(bf16[128,512]{1,0:T(8,128)(2,1)S(1)} %get-tuple-element.21), channel_id=1, source_target_pairs={{0,9},{1,8},{2,11},{3,10},{4,13},{5,12},{6,15},{7,14},{8,17},{9,16... | collective-permute-start | bytes 393224 | tf_op jit(solution)/shard_map/ppermute | solution.py:373
  38.6 0.0 collective-permute-done.8.q_other
  38.6 0.0 collective-permute-done.11.kv_2
  38.6 0.0 collective-permute-done.12.kv_3
  38.6 2.2 %attend.3 = (bf16[128,512]{1,0:T(8,128)(2,1)S(1)}, bf16[128,512]{1,0:T(8,128)(2,1)S(1)}) custom-call(bf16[128,512]{1,0:T(8,128)(2,1)S(1)} %collective-permute-done.7.q_own, bf16[128,512]{1,0:T(8,128)(2,1)S(1)} %collective-permute-done.8.q_other, bf16[256,256]{1,0:T(8,128)(2,1)S(1)} %collective-permute-done.9.kv_0, ...), custom_call_target="tpu_custom_call" | custom-call | flops 536870912 | bytes 1048576 | tf_op jit(solution)/shard_map/attend/pallas_call | solution.py:309
  40.8 0.6 %copy-done.4 = bf16[128,512]{1,0:T(8,128)(2,1)} copy-done((bf16[128,512]{1,0:T(8,128)(2,1)}, bf16[128,512]{1,0:T(8,128)(2,1)S(1)}, u32[]{:S(2)}) %copy-start.4) | copy-done | bytes 131096
  41.5 0.0 collective-permute-start.14
  41.5 0.9 %collective-permute-done.5.a_own = bf16[128,512]{1,0:T(8,128)(2,1)S(1)} collective-permute-done((bf16[128,512]{1,0:T(8,128)(2,1)S(1)}, bf16[128,512]{1,0:T(8,128)(2,1)S(1)}, u32[]{:S(2)}, u32[]{:S(2)}) %collective-permute-start.5) | collective-permute-done | bytes 131104 | tf_op jit(solution)/shard_map/ppermute | solution.py:373
  42.4 3.1 %collective-permute-done.6.a_other = bf16[128,512]{1,0:T(8,128)(2,1)S(1)} collective-permute-done((bf16[128,512]{1,0:T(8,128)(2,1)S(1)}, bf16[128,512]{1,0:T(8,128)(2,1)S(1)}, u32[]{:S(2)}, u32[]{:S(2)}) %collective-permute-start.6) | collective-permute-done | bytes 131104 | tf_op jit(solution)/shard_map/ppermute | solution.py:373
  45.5 0.0 collective-permute-done.14.b_other
  45.5 0.0 copy-done.5
  45.5 0.0 copy-done.7
  45.5 0.6 %copy-done.8 = bf16[128,512]{1,0:T(8,128)(2,1)} copy-done((bf16[128,512]{1,0:T(8,128)(2,1)}, bf16[128,512]{1,0:T(8,128)(2,1)S(1)}, u32[]{:S(2)}) %copy-start.8) | copy-done | bytes 131096
  46.2 0.0 copy-done.9
  46.2 2.1 %assemble.1 = bf16[1,128,2048]{2,1,0:T(8,128)(2,1)} custom-call(bf16[128,512]{1,0:T(8,128)(2,1)} %copy-done.7, bf16[128,512]{1,0:T(8,128)(2,1)} %copy-done.8, bf16[128,512]{1,0:T(8,128)(2,1)} %copy-done.4, bf16[128,512]{1,0:T(8,128)(2,1)} %copy-done.9, s32[1,1152]{1,0:T(1,128)} %copy-done.5), custom_call_target="tpu_custom_call" | custom-call | tf_op jit(solution)/shard_map/assemble/pallas_call | solution.py:347
  (12 shorter events, 0.0 us)
Async XLA Ops:
  0.0 3.4 %copy-start = (bf16[1,4096,1024]{2,1,0:T(8,128)(2,1)S(1)}, bf16[1,4096,1024]{2,1,0:T(8,128)(2,1)}, u32[]{:S(2)}) copy-start(bf16[1,4096,1024]{2,1,0:T(8,128)(2,1)} %weight.1) | copy-start | bytes 25165828
  3.4 1.2 %copy-start.1 = (bf16[1,128,4096]{2,1,0:T(8,128)(2,1)S(1)}, bf16[1,128,4096]{2,1,0:T(8,128)(2,1)}, u32[]{:S(2)}) copy-start(bf16[1,128,4096]{2,1,0:T(8,128)(2,1)} %hidden.1) | copy-start | bytes 3145732
  4.6 1.2 %copy-start.2 = (f32[1024,256]{1,0:T(8,128)S(1)}, f32[1024,256]{1,0:T(8,128)}, u32[]{:S(2)}) copy-start(f32[1024,256]{1,0:T(8,128)} %constant.2.clone.table) | copy-start | bytes 3145732
  5.8 1.0 %copy-start.3 = (bf16[1,128,2048]{2,1,0:T(8,128)(2,1)S(1)}, bf16[1,128,2048]{2,1,0:T(8,128)(2,1)}, u32[]{:S(2)}) copy-start(bf16[1,128,2048]{2,1,0:T(8,128)(2,1)} %queries.1) | copy-start | bytes 1572868
  6.9 21.6 %copy-start.6 = (s32[1,1024]{1,0:T(1,128)S(1)}, s32[1,1024]{1,0:T(1,128)}, u32[]{:S(2)}) copy-start(s32[1,1024]{1,0:T(1,128)} %docs.1) | copy-start | bytes 12292
  6.9 21.6 %copy-start.10 = (s32[1,128]{1,0:T(1,128)S(1)}, s32[1,128]{1,0:T(1,128)}, u32[]{:S(2)}) copy-start(s32[1,128]{1,0:T(1,128)} %param.10) | copy-start | bytes 1540
  9.8 1.7 %collective-permute-start.1 = (bf16[128,512]{1,0:T(8,128)(2,1)S(1)}, bf16[128,512]{1,0:T(8,128)(2,1)S(1)}, u32[]{:S(2)}, u32[]{:S(2)}) collective-permute-start(bf16[128,512]{1,0:T(8,128)(2,1)S(1)} %get-tuple-element.19), channel_id=1, source_target_pairs={{0,1},{1,0},{2,3},{3,2},{4,5},{5,4},{6,7},{7,6},{8,9},{9,8},{10,11... | collective-permute-start | bytes 393224 | tf_op jit(solution)/shard_map/ppermute | solution.py:363
  11.5 5.7 %collective-permute-start.9 = (bf16[256,256]{1,0:T(8,128)(2,1)S(1)}, bf16[256,256]{1,0:T(8,128)(2,1)S(1)}, u32[]{:S(2)}, u32[]{:S(2)}) collective-permute-start(bf16[256,256]{1,0:T(8,128)(2,1)S(1)} %pad_maximum_fusion.1), channel_id=1, source_target_pairs={{0,8},{1,9},{2,10},{3,11},{4,12},{5,13},{6,14},{7,15},{8,16},{9,17... | collective-permute-start | bytes 393224 | tf_op jit(solution)/shard_map/ppermute | solution.py:373
  12.8 6.3 %collective-permute-start.2 = (bf16[256,256]{1,0:T(8,128)(2,1)S(1)}, bf16[256,256]{1,0:T(8,128)(2,1)S(1)}, u32[]{:S(2)}, u32[]{:S(2)}) collective-permute-start(bf16[256,256]{1,0:T(8,128)(2,1)S(1)} %pad_maximum_fusion.kv_0), channel_id=1, source_target_pairs={{0,2},{1,3},{2,4},{3,5},{4,6},{5,7},{8,10},{9,11},{10,12},{11,13},... | collective-permute-start | bytes 393224 | tf_op jit(solution)/shard_map/ppermute | solution.py:359
  14.1 10.4 %collective-permute-start = (bf16[128,512]{1,0:T(8,128)(2,1)S(1)}, bf16[128,512]{1,0:T(8,128)(2,1)S(1)}, u32[]{:S(2)}, u32[]{:S(2)}) collective-permute-start(bf16[128,512]{1,0:T(8,128)(2,1)S(1)} %get-tuple-element.17), channel_id=1, source_target_pairs={{0,1},{1,0},{2,3},{3,2},{4,5},{5,4},{6,7},{7,6},{8,9},{9,8},{10,11... | collective-permute-start | bytes 393224 | tf_op jit(solution)/shard_map/ppermute | solution.py:363
  17.2 8.6 %collective-permute-start.10 = (bf16[256,256]{1,0:T(8,128)(2,1)S(1)}, bf16[256,256]{1,0:T(8,128)(2,1)S(1)}, u32[]{:S(2)}, u32[]{:S(2)}) collective-permute-start(bf16[256,256]{1,0:T(8,128)(2,1)S(1)} %collective-permute-done.9.kv_0), channel_id=1, source_target_pairs={{0,2},{1,3},{2,4},{3,5},{4,6},{5,7},{8,10},{9,11},{10,12},{11,13},... | collective-permute-start | bytes 393224 | tf_op jit(solution)/shard_map/ppermute | solution.py:359
  19.1 8.0 %collective-permute-start.3 = (bf16[256,256]{1,0:T(8,128)(2,1)S(1)}, bf16[256,256]{1,0:T(8,128)(2,1)S(1)}, u32[]{:S(2)}, u32[]{:S(2)}) collective-permute-start(bf16[256,256]{1,0:T(8,128)(2,1)S(1)} %collective-permute-done.2.kv_1), channel_id=1, source_target_pairs={{2,4},{3,5},{4,6},{5,7},{10,12},{11,13},{12,14},{13,15},{18,20},{1... | collective-permute-start | bytes 393224 | tf_op jit(solution)/shard_map/ppermute | solution.py:359
  20.4 16.4 %collective-permute-start.7 = (bf16[128,512]{1,0:T(8,128)(2,1)S(1)}, bf16[128,512]{1,0:T(8,128)(2,1)S(1)}, u32[]{:S(2)}, u32[]{:S(2)}) collective-permute-start(bf16[128,512]{1,0:T(8,128)(2,1)S(1)} %get-tuple-element.22), channel_id=1, source_target_pairs={{0,8},{1,9},{2,10},{3,11},{4,12},{5,13},{6,14},{7,15},{8,16},{9,17... | collective-permute-start | bytes 393224 | tf_op jit(solution)/shard_map/ppermute | solution.py:373
  21.7 16.9 %collective-permute-start.8 = (bf16[128,512]{1,0:T(8,128)(2,1)S(1)}, bf16[128,512]{1,0:T(8,128)(2,1)S(1)}, u32[]{:S(2)}, u32[]{:S(2)}) collective-permute-start(bf16[128,512]{1,0:T(8,128)(2,1)S(1)} %get-tuple-element.23), channel_id=1, source_target_pairs={{0,9},{1,8},{2,11},{3,10},{4,13},{5,12},{6,15},{7,14},{8,17},{9,16... | collective-permute-start | bytes 393224 | tf_op jit(solution)/shard_map/ppermute | solution.py:373
  24.6 8.4 %collective-permute-start.4 = (bf16[256,256]{1,0:T(8,128)(2,1)S(1)}, bf16[256,256]{1,0:T(8,128)(2,1)S(1)}, u32[]{:S(2)}, u32[]{:S(2)}) collective-permute-start(bf16[256,256]{1,0:T(8,128)(2,1)S(1)} %collective-permute-done.2.kv_1), channel_id=1, source_target_pairs={{2,6},{3,7},{10,14},{11,15},{18,22},{19,23},{26,30},{27,31}} | collective-permute-start | bytes 393224 | tf_op jit(solution)/shard_map/ppermute | solution.py:359
  25.9 12.7 %collective-permute-start.11 = (bf16[256,256]{1,0:T(8,128)(2,1)S(1)}, bf16[256,256]{1,0:T(8,128)(2,1)S(1)}, u32[]{:S(2)}, u32[]{:S(2)}) collective-permute-start(bf16[256,256]{1,0:T(8,128)(2,1)S(1)} %collective-permute-done.10.kv_1), channel_id=1, source_target_pairs={{2,4},{3,5},{4,6},{5,7},{10,12},{11,13},{12,14},{13,15},{18,20},{1... | collective-permute-start | bytes 393224 | tf_op jit(solution)/shard_map/ppermute | solution.py:359
  27.2 11.4 %collective-permute-start.12 = (bf16[256,256]{1,0:T(8,128)(2,1)S(1)}, bf16[256,256]{1,0:T(8,128)(2,1)S(1)}, u32[]{:S(2)}, u32[]{:S(2)}) collective-permute-start(bf16[256,256]{1,0:T(8,128)(2,1)S(1)} %collective-permute-done.10.kv_1), channel_id=1, source_target_pairs={{2,6},{3,7},{10,14},{11,15},{18,22},{19,23},{26,30},{27,31}} | collective-permute-start | bytes 393224 | tf_op jit(solution)/shard_map/ppermute | solution.py:359
  32.9 3.7 %collective-permute-start.13 = (s32[1,1152]{1,0:T(1,128)S(1)}, s32[1,1152]{1,0:T(1,128)S(1)}, u32[]{:S(2)}, u32[]{:S(2)}) collective-permute-start(s32[1,1152]{1,0:T(1,128)S(1)} %pad_add_fusion), channel_id=1, source_target_pairs={{0,8},{1,9},{2,10},{3,11},{4,12},{5,13},{6,14},{7,15},{8,16},{9,17... | collective-permute-start | bytes 13832 | tf_op jit(solution)/shard_map/ppermute | solution.py:373
  36.6 8.9 %copy-start.5 = (s32[1,1152]{1,0:T(1,128)}, s32[1,1152]{1,0:T(1,128)S(1)}, u32[]{:S(2)}) copy-start(s32[1,1152]{1,0:T(1,128)S(1)} %collective-permute-done.13.docs.notes) | copy-start | bytes 13828
  36.6 5.8 %collective-permute-start.5 = (bf16[128,512]{1,0:T(8,128)(2,1)S(1)}, bf16[128,512]{1,0:T(8,128)(2,1)S(1)}, u32[]{:S(2)}, u32[]{:S(2)}) collective-permute-start(bf16[128,512]{1,0:T(8,128)(2,1)S(1)} %get-tuple-element.20), channel_id=1, source_target_pairs={{0,8},{1,9},{2,10},{3,11},{4,12},{5,13},{6,14},{7,15},{8,16},{9,17... | collective-permute-start | bytes 393224 | tf_op jit(solution)/shard_map/ppermute | solution.py:373
  36.8 8.7 %collective-permute-start.6 = (bf16[128,512]{1,0:T(8,128)(2,1)S(1)}, bf16[128,512]{1,0:T(8,128)(2,1)S(1)}, u32[]{:S(2)}, u32[]{:S(2)}) collective-permute-start(bf16[128,512]{1,0:T(8,128)(2,1)S(1)} %get-tuple-element.21), channel_id=1, source_target_pairs={{0,9},{1,8},{2,11},{3,10},{4,13},{5,12},{6,15},{7,14},{8,17},{9,16... | collective-permute-start | bytes 393224 | tf_op jit(solution)/shard_map/ppermute | solution.py:373
  40.8 0.6 %copy-start.4 = (bf16[128,512]{1,0:T(8,128)(2,1)}, bf16[128,512]{1,0:T(8,128)(2,1)S(1)}, u32[]{:S(2)}) copy-start(bf16[128,512]{1,0:T(8,128)(2,1)S(1)} %get-tuple-element.25.b_own) | copy-start | bytes 393220
  41.5 4.0 %collective-permute-start.14 = (bf16[128,512]{1,0:T(8,128)(2,1)S(1)}, bf16[128,512]{1,0:T(8,128)(2,1)S(1)}, u32[]{:S(2)}, u32[]{:S(2)}) collective-permute-start(bf16[128,512]{1,0:T(8,128)(2,1)S(1)} %get-tuple-element.26), channel_id=1, source_target_pairs={{0,1},{1,0},{2,3},{3,2},{4,5},{5,4},{6,7},{7,6},{8,9},{9,8},{10,11... | collective-permute-start | bytes 393224 | tf_op jit(solution)/shard_map/ppermute | solution.py:363
  42.4 3.1 %copy-start.7 = (bf16[128,512]{1,0:T(8,128)(2,1)}, bf16[128,512]{1,0:T(8,128)(2,1)S(1)}, u32[]{:S(2)}) copy-start(bf16[128,512]{1,0:T(8,128)(2,1)S(1)} %collective-permute-done.5.a_own) | copy-start | bytes 393220
  45.5 0.6 %copy-start.8 = (bf16[128,512]{1,0:T(8,128)(2,1)}, bf16[128,512]{1,0:T(8,128)(2,1)S(1)}, u32[]{:S(2)}) copy-start(bf16[128,512]{1,0:T(8,128)(2,1)S(1)} %collective-permute-done.6.a_other) | copy-start | bytes 393220
  45.5 0.7 %copy-start.9 = (bf16[128,512]{1,0:T(8,128)(2,1)}, bf16[128,512]{1,0:T(8,128)(2,1)S(1)}, u32[]{:S(2)}) copy-start(bf16[128,512]{1,0:T(8,128)(2,1)S(1)} %collective-permute-done.14.b_other) | copy-start | bytes 393220

commit v2 on v0

--- a/solution.py
+++ b/solution.py
@@ -1,14 +1,22 @@
+import functools
 import math
 
 import jax
 import jax.numpy as jnp
+import numpy as np
 from jax import lax
+from jax.experimental import pallas as pl
+from jax.experimental.pallas import tpu as pltpu
 from jax.sharding import PartitionSpec as P
 
 QUERY_HEADS = 16
 KEY_VALUE_HEADS = 4
 HEAD_SIZE = 128
-
+GROUP = QUERY_HEADS // KEY_VALUE_HEADS
+GROUP_WIDTH = GROUP * HEAD_SIZE
+PAIR_WIDTH = 2 * HEAD_SIZE
+MASKED = -1e30
+NOTE_ROWS = 16
 
 rope_base = 500000.0
 
@@ -36,7 +44,7 @@
     )
 
 
-def per_device(hidden, queries, key_value_weight, doc_ids, scored):
+def gathered_everywhere(hidden, queries, key_value_weight, doc_ids, scored):
     count_of_rows = hidden.shape[1]
     first_row = lax.axis_index("ctx") * count_of_rows
     token_positions = first_row + jnp.arange(count_of_rows, dtype=jnp.int32)
@@ -55,10 +63,7 @@
         .reshape(count_of_rows, key_value_width)
     )
     value_matrix = projected_rows[:, key_value_width:].astype(jnp.bfloat16)
-    query_group_width = QUERY_HEADS // KEY_VALUE_HEADS
-    query_head_count = queries[0].reshape(
-        count_of_rows, KEY_VALUE_HEADS, query_group_width, HEAD_SIZE
-    )
+    query_head_count = queries[0].reshape(count_of_rows, KEY_VALUE_HEADS, GROUP, HEAD_SIZE)
     sequence_docs = doc_ids[0]
     own_docs = lax.dynamic_slice_in_dim(sequence_docs, first_row, count_of_rows, 0)
     score_scale = 1.0 / math.sqrt(HEAD_SIZE)
@@ -88,7 +93,7 @@
         allowed = (key_pos[None, :] <= token_positions[:, None]) & (
             sequence_docs[None, :] == own_docs[:, None]
         )
-        scores = jnp.where(allowed[None, None], scores, jnp.float32(-1e30))
+        scores = jnp.where(allowed[None, None], scores, jnp.float32(MASKED))
         row_max = jnp.max(scores, axis=-1, keepdims=True)
         expo = jnp.exp(scores - row_max)
         total = jnp.sum(expo, axis=-1)
@@ -109,6 +114,434 @@
     return from_behind(outgoing, "phase", 1)
 
 
+def rotary_tables(rows, devices):
+    half = HEAD_SIZE // 2
+    frequency = (rope_base ** (-np.arange(half) * 2.0 / HEAD_SIZE)).astype(np.float32).astype(np.float64)
+    frequency = np.concatenate([frequency, frequency])[None, :]
+    within = np.arange(rows)[:, None] * frequency
+    starts = np.arange(devices)[:, None] * (rows * frequency)
+    return [
+        jnp.asarray(np.concatenate([np.cos(x), np.sin(x)], axis=1), jnp.float32)
+        for x in (within, starts)
+    ]
+
+
+def parity():
+    return lax.rem(lax.axis_index("ctx") // 2, 2)
+
+
+def project_kernel(
+    cuts,
+    hidden,
+    weight,
+    queries,
+    within,
+    starts,
+    docs,
+    scored,
+    mine,
+    other,
+    swap,
+    away,
+    packed,
+    wide,
+    store,
+    normed,
+    hidden_sem,
+    query_sems,
+    weight_sems,
+):
+    rows, width = wide.shape[0], packed.shape[1]
+    odd = parity()
+    load_hidden = pltpu.make_async_copy(hidden.at[0], wide, hidden_sem)
+    load_hidden.start()
+    copies = []
+    for i, (start, stop) in enumerate(cuts):
+        span = pl.ds(start, stop - start)
+        copy = pltpu.make_async_copy(weight.at[0, span, :], store.at[span, :], weight_sems.at[i])
+        copy.start()
+        copies.append(copy)
+    asked = pl.ds(pl.multiple_of((1 - odd) * GROUP_WIDTH, GROUP_WIDTH), GROUP_WIDTH)
+    cut_queries = [
+        pltpu.make_async_copy(
+            queries.at[0, :, asked], swap.at[pl.ds(0, rows), pl.ds(PAIR_WIDTH, GROUP_WIDTH)], query_sems.at[0]
+        ),
+        pltpu.make_async_copy(
+            queries.at[0, :, pl.ds(width, width)], packed.at[pl.ds(0, rows), :], query_sems.at[1]
+        ),
+    ]
+    for copy in cut_queries:
+        copy.start()
+    marks = jnp.concatenate([scored[...]] * (width // rows), axis=1)
+    notes = [docs[...], marks, jnp.zeros((NOTE_ROWS - 2, width), jnp.int32)]
+    notes = jnp.concatenate(notes, axis=0).astype(jnp.float32).astype(jnp.bfloat16)
+    packed[rows:, :] = notes
+    swap[rows:, :] = notes[:, : swap.shape[1]]
+    base = starts[pl.ds(lax.axis_index("ctx"), 1), :]
+    base_cosine, base_sine = base[:, :HEAD_SIZE], base[:, HEAD_SIZE:]
+    cosine, sine = within[:, :HEAD_SIZE], within[:, HEAD_SIZE:]
+    cosine, sine = (
+        cosine * base_cosine - sine * base_sine,
+        sine * base_cosine + cosine * base_sine,
+    )
+    sine = jnp.where(lax.broadcasted_iota(jnp.int32, sine.shape, 1) < HEAD_SIZE // 2, -sine, sine)
+    load_hidden.wait()
+    values = wide[...].astype(jnp.float32)
+    scale = lax.rsqrt(jnp.mean(values * values, axis=-1, keepdims=True) + 1e-05)
+    normed[...] = (values * scale).astype(jnp.bfloat16)
+    total = None
+    for copy, (start, stop) in zip(copies, cuts):
+        copy.wait()
+        part = jnp.dot(
+            normed[:, start:stop], store[start:stop, :], preferred_element_type=jnp.float32
+        )
+        total = part if total is None else total + part
+    pairs = []
+    for head in range(KEY_VALUE_HEADS):
+        key = total[:, head * HEAD_SIZE : (head + 1) * HEAD_SIZE]
+        key = key * cosine + pltpu.roll(key, HEAD_SIZE // 2, 1) * sine
+        at = (KEY_VALUE_HEADS + head) * HEAD_SIZE
+        value = total[:, at : at + HEAD_SIZE]
+        pairs.append(jnp.concatenate([key, value], axis=1).astype(jnp.bfloat16))
+    away[:, :PAIR_WIDTH] = pairs[2]
+    away[:, PAIR_WIDTH:] = pairs[3]
+    for u in range(2):
+
+        @pl.when(odd == u)
+        def _():
+            mine[...] = pairs[u]
+            other[...] = pairs[1 - u]
+            swap[:rows, :PAIR_WIDTH] = pairs[1 - u]
+
+    for copy in cut_queries:
+        copy.wait()
+
+
+def project(hidden, weight, queries, docs, scored):
+    rows, width = hidden.shape[1], hidden.shape[2]
+    columns = weight.shape[2]
+    cuts = ((0, width // 2), (width // 2, width))
+    within, starts = rotary_tables(rows, docs.shape[1] // rows)
+    hbm = pl.BlockSpec(memory_space=pltpu.HBM)
+    vmem = pl.BlockSpec(memory_space=pltpu.VMEM)
+    pair = jax.ShapeDtypeStruct((rows, PAIR_WIDTH), jnp.bfloat16)
+    return pl.pallas_call(
+        functools.partial(project_kernel, cuts),
+        out_shape=(
+            pair,
+            pair,
+            jax.ShapeDtypeStruct((rows + NOTE_ROWS, PAIR_WIDTH + GROUP_WIDTH), jnp.bfloat16),
+            jax.ShapeDtypeStruct((rows, 2 * PAIR_WIDTH), jnp.bfloat16),
+            jax.ShapeDtypeStruct((rows + NOTE_ROWS, 2 * GROUP_WIDTH), jnp.bfloat16),
+        ),
+        in_specs=[hbm, hbm, hbm, vmem, vmem, vmem, vmem],
+        out_specs=(vmem,) * 5,
+        scratch_shapes=[
+            pltpu.VMEM((rows, width), jnp.bfloat16),
+            pltpu.VMEM((width, columns), jnp.bfloat16),
+            pltpu.VMEM((rows, width), jnp.bfloat16),
+            pltpu.SemaphoreType.DMA,
+            pltpu.SemaphoreType.DMA((2,)),
+            pltpu.SemaphoreType.DMA((len(cuts),)),
+        ],
+        compiler_params=pltpu.CompilerParams(vmem_limit_bytes=63 * 2**20),
+        cost_estimate=pl.CostEstimate(flops=0, bytes_accessed=0, transcendentals=0),
+        name="project",
+    )(hidden, weight, queries, within, starts, docs, scored)
+
+
+def attend_body(q, kvs, doc_row, kept, bias, put):
+    rows = q.shape[0]
+    place = lax.axis_index("ctx")
+    chip, core = place // 2, lax.rem(place, 2)
+    cores = (core, 1 - core)
+
+    def docs_of(device):
+        row = doc_row(pl.ds(pl.multiple_of(device * rows, rows), rows))
+        return jnp.broadcast_to(row.astype(jnp.float32), (rows, rows))
+
+    query_docs = docs_of(place).T
+    for back in range(4):
+        for b in range(2):
+            block = chip - back
+            key_docs = docs_of(2 * jnp.maximum(block, 0) + cores[b])
+            allowed = query_docs == jnp.where(block >= 0, key_docs, -1.0)
+            if back == 0:
+                row_at = lax.broadcasted_iota(jnp.int32, (rows, rows), 0)
+                key_at = lax.broadcasted_iota(jnp.int32, (rows, rows), 1)
+                allowed &= core * rows + row_at >= cores[b] * rows + key_at
+            at = (2 * back + b) * rows
+            bias[:, at : at + rows] = jnp.where(allowed, 0.0, MASKED)
+
+    kept_rows = jnp.broadcast_to(kept, (rows, rows)).T[:, :1]
+    factor = math.log2(math.e) / math.sqrt(HEAD_SIZE)
+    for head in range(2):
+        at = head * PAIR_WIDTH
+        for half in range(GROUP // 2):
+            first = (head * GROUP + 2 * half) * HEAD_SIZE
+            pair = jnp.concatenate(
+                [q[:, first : first + HEAD_SIZE], q[:, first + HEAD_SIZE : first + 2 * HEAD_SIZE]],
+                axis=0,
+            )
+            scores = []
+            for back in range(4):
+                keys = jnp.concatenate(
+                    [kvs[2 * back + b][:, at : at + HEAD_SIZE] for b in range(2)], axis=0
+                )
+                part = lax.dot_general(
+                    pair, keys, (((1,), (1,)), ((), ())), preferred_element_type=jnp.float32
+                )
+                block_bias = bias[:, 2 * back * rows : 2 * (back + 1) * rows]
+                scores.append(part + jnp.concatenate([block_bias, block_bias], axis=0))
+            scores = jnp.concatenate(scores, axis=1)
+            row_max = jnp.max(scores, axis=-1, keepdims=True)
+            expo = jnp.exp2((scores - row_max) * factor)
+            total = jnp.sum(expo, axis=-1, keepdims=True)
+            weights = expo.astype(jnp.bfloat16)
+            summed = None
+            for back in range(4):
+                values = jnp.concatenate(
+                    [
+                        kvs[2 * back + b][:, at + HEAD_SIZE : at + 2 * HEAD_SIZE]
+                        for b in range(2)
+                    ],
+                    axis=0,
+                )
+                part = jnp.dot(
+                    weights[:, 2 * back * rows : 2 * (back + 1) * rows],
+                    values,
+                    preferred_element_type=jnp.float32,
+                )
+                summed = part if summed is None else summed + part
+            result = summed / total
+            for i in range(2):
+                put(
+                    first + i * HEAD_SIZE,
+                    (result[i * rows : (i + 1) * rows] * kept_rows).astype(jnp.bfloat16),
+                )
+
+
+def attend_home_kernel(
+    queries, swap, mine, mine_x, near_x, far, far_x, beyond, beyond_x, docs, scored, out_own, out_other, bias
+):
+    rows = queries.shape[1]
+    place = lax.axis_index("ctx")
+    chip, core = place // 2, lax.rem(place, 2)
+    partner = place + 2 - 4 * lax.rem(chip, 2)
+    behind = place - 4
+    crossed = 2 * (3 - chip) + core
+    far_off = chip >= 2
+
+    def other_core(device):
+        return device + 1 - 2 * lax.rem(device, 2)
+
+    def docs_of(device):
+        start = pl.multiple_of(device * rows, rows)
+        return jnp.broadcast_to(docs[:, pl.ds(start, rows)].astype(jnp.float32), (rows, rows))
+
+    row_at = lax.broadcasted_iota(jnp.int32, (rows, rows), 0)
+    key_at = lax.broadcasted_iota(jnp.int32, (rows, rows), 1)
+    sources = []
+    for device in (place, partner, behind, crossed):
+        device = jnp.where(far_off, device, lax.rem(device + 8, 8))
+        sources += [device, other_core(device)]
+    query_docs = [docs_of(place).T, docs_of(partner).T]
+    for k, device in enumerate(sources):
+        key_docs = docs_of(device)
+        if k >= 4:
+            key_docs = jnp.where(far_off, key_docs, -1.0)
+        for a, asker in enumerate((place, partner)):
+            allowed = query_docs[a] == key_docs
+            if k < 4:
+                allowed &= asker * rows + row_at >= device * rows + key_at
+            bias[a * rows : (a + 1) * rows, k * rows : (k + 1) * rows] = jnp.where(
+                allowed, 0.0, MASKED
+            )
+
+    def blocks(at):
+        cut = slice(at, at + HEAD_SIZE)
+        return [
+            jnp.concatenate([one[:rows, cut], twin[:, cut]], axis=0)
+            for one, twin in ((mine, mine_x), (swap, near_x), (far, far_x), (beyond, beyond_x))
+        ]
+
+    kept = jnp.concatenate(
+        [
+            jnp.broadcast_to(row, (rows, rows)).T[:, :1]
+            for row in (
+                scored[...].astype(jnp.float32),
+                swap[rows:, :rows].astype(jnp.float32)[1:2],
+            )
+        ],
+        axis=0,
+    )
+    keys, values = blocks(0), blocks(HEAD_SIZE)
+    factor = math.log2(math.e) / math.sqrt(HEAD_SIZE)
+    for head in range(GROUP):
+        at = head * HEAD_SIZE
+        q = jnp.concatenate(
+            [queries[0, :, at : at + HEAD_SIZE], swap[:rows, PAIR_WIDTH + at : PAIR_WIDTH + at + HEAD_SIZE]], axis=0
+        )
+        scores = jnp.concatenate(
+            [
+                lax.dot_general(q, k, (((1,), (1,)), ((), ())), preferred_element_type=jnp.float32)
+                for k in keys
+            ],
+            axis=1,
+        )
+        scores = scores + bias[...]
+        row_max = jnp.max(scores, axis=-1, keepdims=True)
+        expo = jnp.exp2((scores - row_max) * factor)
+        total = jnp.sum(expo, axis=-1, keepdims=True)
+        weights = expo.astype(jnp.bfloat16)
+        summed = None
+        for i, value in enumerate(values):
+            part = jnp.dot(
+                weights[:, 2 * i * rows : 2 * (i + 1) * rows],
+                value,
+                preferred_element_type=jnp.float32,
+            )
+            summed = part if summed is None else summed + part
+        result = (summed / total * kept).astype(jnp.bfloat16)
+        out_own[:, at : at + HEAD_SIZE] = result[:rows]
+        out_other[:, at : at + HEAD_SIZE] = result[rows:]
+
+
+class Halves:
+    def __init__(self, first, second):
+        self.refs = (first, second)
+        self.width = first.shape[1]
+
+    def __getitem__(self, index):
+        rows, columns = index
+        start = columns.start % self.width
+        ref = self.refs[columns.start // self.width]
+        return ref[rows, start : start + columns.stop - columns.start]
+
+
+def attend_relayed_kernel(packed, *refs):
+    kvs, (out, bias) = refs[:10], refs[10:]
+    kvs = kvs[:5] + (Halves(*kvs[5:7]), kvs[7], Halves(*kvs[8:]))
+    rows = out.shape[0]
+    kept = packed[rows : rows + NOTE_ROWS, :rows].astype(jnp.float32)[1:2]
+
+    def doc_row(at):
+        return packed[rows : rows + NOTE_ROWS, at].astype(jnp.float32)[:1]
+
+    def put(at, value):
+        out[:, at : at + HEAD_SIZE] = value
+
+    attend_body(packed.at[pl.ds(0, rows), :], kvs, doc_row, kept, bias, put)
+
+
+def attend_cost(rows, flops):
+    return dict(
+        scratch_shapes=[pltpu.VMEM((rows, 8 * rows), jnp.float32)],
+        compiler_params=pltpu.CompilerParams(vmem_limit_bytes=32 * 2**20),
+        cost_estimate=pl.CostEstimate(flops=flops, bytes_accessed=0, transcendentals=0),
+    )
+
+
+def attend_home(queries, *rest):
+    rows = queries.shape[1]
+    out = jax.ShapeDtypeStruct((rows, GROUP_WIDTH), jnp.bfloat16)
+
+    def whole(array):
+        return pl.BlockSpec(array.shape, lambda i: (0,) * array.ndim)
+
+    cost = attend_cost(rows, HOME_FLOPS)
+    cost["scratch_shapes"] = [pltpu.VMEM((2 * rows, 8 * rows), jnp.float32)]
+    return pl.pallas_call(
+        attend_home_kernel,
+        grid=(1,),
+        out_shape=(out, out),
+        in_specs=[pl.BlockSpec((1, rows, GROUP_WIDTH), lambda i: (0, 0, parity()))]
+        + [whole(x) for x in rest],
+        out_specs=(pl.BlockSpec((rows, GROUP_WIDTH), lambda i: (0, 0)),) * 2,
+        name="attend_home",
+        **cost,
+    )(queries, *rest)
+
+
+def attend_relayed(packed, kvs):
+    rows, width = kvs[0].shape[0], packed.shape[1]
+    vmem = pl.BlockSpec(memory_space=pltpu.VMEM)
+    return pl.pallas_call(
+        attend_relayed_kernel,
+        out_shape=jax.ShapeDtypeStruct((rows, width), jnp.bfloat16),
+        in_specs=[vmem] * 11,
+        out_specs=vmem,
+        name="attend_relayed",
+        **attend_cost(rows, RELAYED_FLOPS),
+    )(packed, *kvs)
+
+
+def send(block, route):
+    pairs = [(2 * a + core, 2 * b + core) for a, b in route for core in range(2)]
+    return lax.ppermute(block, "ctx", pairs)
+
+
+def across(block):
+    return lax.ppermute(block, "ctx", [(i, i ^ 1) for i in range(lax.axis_size("ctx"))])
+
+
+def onward(block, change=0):
+    sections, count = lax.axis_size("phase"), lax.axis_size("ctx")
+    route = [
+        (p * count + c, (p + 1) % sections * count + (c ^ change))
+        for p in range(sections)
+        for c in range(count)
+    ]
+    return lax.ppermute(block, ("phase", "ctx"), route)
+
+
+HOME_FLOPS = 2 * 10**9
+RELAYED_FLOPS = 0
+
+
+def after(block, *others):
+    return lax.optimization_barrier((block,) + others)[0]
+
+
+def across_halves(block):
+    half = block.shape[1] // 2
+    return across(block[:, :half]), across(block[:, half:])
+
+
+def paired(hidden, queries, key_value_weight, doc_ids, scored):
+    mine, other, swap, away, packed = project(hidden, key_value_weight, queries, doc_ids, scored)
+    away = onward(away)
+    swap = send(swap, ((0, 1), (1, 0), (2, 3), (3, 2)))
+    far = send(mine, ((0, 2), (1, 3)))
+    beyond = send(other, ((0, 3), (1, 2)))
+    packed = onward(after(packed, swap))
+    away_1 = send(away, ((0, 1), (1, 2), (2, 3)))
+    away_2 = send(away_1, ((1, 2), (2, 3)))
+    away_3 = send(away_1, ((1, 3),))
+    swap, far, beyond = lax.optimization_barrier((swap, far, beyond))
+    own, partners = attend_home(
+        queries,
+        swap,
+        mine,
+        across(mine),
+        across(swap[: mine.shape[0], :PAIR_WIDTH]),
+        far,
+        across(far),
+        beyond,
+        across(beyond),
+        doc_ids,
+        scored,
+    )
+    own, partners = onward(own), onward(partners, 2)
+    away = [away, across(away), away_1, across(after(away_1, packed))] + [
+        x for block in (away_2, away_3) for x in (block, *across_halves(block))
+    ]
+    last = attend_relayed(packed, away)
+    straight = jnp.concatenate([own, partners, last], axis=1)
+    crossed = jnp.concatenate([partners, own, last], axis=1)
+    return jnp.where(parity() == 1, crossed, straight)[None]
+
+
 def solution(mesh):
     placed = (
         P("phase", "ctx", None),
@@ -117,6 +550,7 @@
         P("phase", None),
         P("phase", "ctx"),
     )
+    plan = paired if mesh.shape["ctx"] == 8 else gathered_everywhere
     return jax.shard_map(
-        per_device, mesh=mesh, in_specs=placed, out_specs=P("phase", "ctx", None), check_vma=False
-    )
+        plan, mesh=mesh, in_specs=placed, out_specs=P("phase", "ctx", None), check_vma=False
+    )

time: 79.3 us -> 43.2 us (0.54)
  waiting for transfers between devices: 44.2 us -> 3.02 us
  starting transfers between devices: 1.52 us -> 26.6 us
  between operations: 13.6 us -> 0.21 us
  Pallas kernels: 0 us -> 11.4 us
  matrix products: 8.73 us -> 0 us
  local copies, waits for them, and re-layouts: 6.35 us -> 0.87 us
  other arithmetic: 4.67 us -> 0.89 us
    all_gather x1 -> x0, waiting for transfers between devices: 30.7 us -> none  [per_device(): collected_rows = lax.all_gather(stacked, 'ctx', axis=0, tiled=True)]
    ppermute x1 -> x20, starting transfers between devices: 1.52 us -> 26.6 us  [the longest x6 12.7 us: send(): return lax.ppermute(block, 'ctx', pairs)]
    pallas_call x0 -> x3, Pallas kernels: none -> 11.4 us  [the longest x1 6.95 us: project(): pl.pallas_call(functools.partial(project_kernel, cuts), out_shape=(pair,...]
    ppermute x1 -> x20, waiting for transfers between devices: 13.5 us -> 3.02 us  [the longest x10 1.91 us: across(): lax.ppermute(block, 'ctx', [(i, i ^ 1) for i in range(lax.axis_size('ctx'...]
    dot_general x9 -> x0, matrix products: 8.73 us -> none  [the longest x1 5.02 us: per_device(): jnp.dot(normed, key_value_weight[0], preferred_element_type=jnp.float32)]
    slice x4 -> x3, local copies, waits for them, and re-layouts: 3.27 us -> 0.03 us  [the longest x2 0.02 us: across_halves(): return (across(block[:, :half]), across(block[:, half:]))]
    reduce_sum x5 -> x0, other arithmetic: 2.71 us -> none  [the longest x1 1.52 us: per_device(): jnp.mean(wide * wide, axis=-1, keepdims=True) + 1e-05]
    reshape x4 -> x0, local copies, waits for them, and re-layouts: 1.25 us -> none  [the longest x1 0.54 us: per_device(): collected_rows[:, key_value_width:]]
  transfers between devices with their start and end apart: 2 -> 20, of which waited for: 2 -> 6; matrix products, arithmetic and copies ran while one was open for 2% -> 0% of each run, Pallas kernels for 0% -> 10%
where the time goes in v2:
time: 43.2 us; the launch traced here: 43 us
  starting transfers between devices  26.6 us (62%)
  Pallas kernels  11.4 us (26%)
  waiting for transfers between devices  3.02 us (7%)
  other arithmetic  0.89 us (2%)
  local copies, waits for them, and re-layouts  0.87 us (2%)
    ppermute x6, starting transfers between devices, send(): return lax.ppermute(block, 'ctx', pairs)  12.7 us
    ppermute x4, starting transfers between devices, onward(): return lax.ppermute(block, ('phase', 'ctx'), route)  11.5 us
    pallas_call x1, Pallas kernels, project(): pl.pallas_call(functools.partial(project_kernel, cuts), out_shape=(pair,...  6.95 us
    ppermute x10, starting transfers between devices, across(): lax.ppermute(block, 'ctx', [(i, i ^ 1) for i in range(lax.axis_size('ctx'...  2.44 us
    pallas_call x1, Pallas kernels, attend_home(): pl.pallas_call(attend_home_kernel, grid=(1,), out_shape=(out, out), in_sp...  2.32 us
    pallas_call x1, Pallas kernels, attend_relayed(): pl.pallas_call(attend_relayed_kernel, out_shape=jax.ShapeDtypeStruct((row...  2.09 us
    ppermute x10, waiting for transfers between devices, across(): lax.ppermute(block, 'ctx', [(i, i ^ 1) for i in range(lax.axis_size('ctx'...  1.91 us
    select_n x1, other arithmetic, paired(): return jnp.where(parity() == 1, crossed, straight)[None]  0.89 us
  transfers between devices with their start and end apart: 20, of which 6 were waited for; matrix products, arithmetic and copies ran while one was open for 0% of the time, Pallas kernels for 10%

profile of v2, /device:TPU:0, one launch (start us, length us, event | category | flops | bytes accessed | tf_op | source)
XLA Modules:
  0.0 43.0 jit_solution(16919504936026175765)
XLA Ops:
  0.0 6.9 %project.1 = (bf16[128,256]{1,0:T(8,128)(2,1)}, bf16[128,256]{1,0:T(8,128)(2,1)}, bf16[144,768]{1,0:T(8,128)(2,1)}, bf16[128,512]{1,0:T(8,128)(2,1)}, bf16[144,1024]{1,0:T(8,128)(2,1)}) custom-call(bf16[1,128,4096]{2,1,0:T(8,128)(2,1)} %hidden.1, bf16[1,4096,1024]{2,1,0:T(8,128)(2,1)} %weight.1, bf16[1,128,2048]{2,1,0:T(8,128)(2,1)} %queries.3, ...), custom_call_target="tpu_custom_call" | custom-call | tf_op jit(solution)/shard_map/project/pallas_call | solution.py:228
  7.0 3.1 %collective-permute-start = (bf16[144,768]{1,0:T(8,128)(2,1)}, bf16[144,768]{1,0:T(8,128)(2,1)S(1)}, u32[]{:S(2)}, u32[]{:S(2)}) collective-permute-start(bf16[144,768]{1,0:T(8,128)(2,1)} %get-tuple-element.17), channel_id=1, source_target_pairs={{0,2},{1,3},{2,0},{3,1},{4,6},{5,7},{6,4},{7,5},{8,10},{9,11},{10,... | collective-permute-start | bytes 663560 | tf_op jit(solution)/shard_map/ppermute | solution.py:481
  10.1 1.5 %collective-permute-start.10 = (bf16[128,512]{1,0:T(8,128)(2,1)}, bf16[128,512]{1,0:T(8,128)(2,1)S(1)}, u32[]{:S(2)}, u32[]{:S(2)}) collective-permute-start(bf16[128,512]{1,0:T(8,128)(2,1)} %get-tuple-element.27), channel_id=1, source_target_pairs={{0,8},{1,9},{2,10},{3,11},{4,12},{5,13},{6,14},{7,15},{8,16},{9,17... | collective-permute-start | bytes 393224 | tf_op jit(solution)/shard_map/ppermute | solution.py:495
  11.6 4.5 %collective-permute-start.1 = (bf16[128,256]{1,0:T(8,128)(2,1)}, bf16[128,256]{1,0:T(8,128)(2,1)S(1)}, u32[]{:S(2)}, u32[]{:S(2)}) collective-permute-start(bf16[128,256]{1,0:T(8,128)(2,1)} %get-tuple-element.18.mine), channel_id=1, source_target_pairs={{0,4},{1,5},{2,6},{3,7},{8,12},{9,13},{10,14},{11,15},{16,20},{17,... | collective-permute-start | bytes 196616 | tf_op jit(solution)/shard_map/ppermute | solution.py:481
  16.1 1.3 %collective-permute-start.2 = (bf16[128,256]{1,0:T(8,128)(2,1)}, bf16[128,256]{1,0:T(8,128)(2,1)S(1)}, u32[]{:S(2)}, u32[]{:S(2)}) collective-permute-start(bf16[128,256]{1,0:T(8,128)(2,1)} %get-tuple-element.19), channel_id=1, source_target_pairs={{0,6},{1,7},{2,4},{3,5},{8,14},{9,15},{10,12},{11,13},{16,22},{17,... | collective-permute-start | bytes 196616 | tf_op jit(solution)/shard_map/ppermute | solution.py:481
  17.4 0.0 collective-permute-done.10.refs_0_
  17.4 2.5 %collective-permute-start.12 = (bf16[128,512]{1,0:T(8,128)(2,1)S(1)}, bf16[128,512]{1,0:T(8,128)(2,1)S(1)}, u32[]{:S(2)}, u32[]{:S(2)}) collective-permute-start(bf16[128,512]{1,0:T(8,128)(2,1)S(1)} %collective-permute-done.10.refs_0_), channel_id=1, source_target_pairs={{0,2},{1,3},{2,4},{3,5},{4,6},{5,7},{8,10},{9,11},{10,12},{11,13},... | collective-permute-start | bytes 393224 | tf_op jit(solution)/shard_map/ppermute | solution.py:481
  19.8 0.1 collective-permute-start.3
  19.9 0.0 collective-permute-done.1.far
  19.9 0.0 collective-permute-done.2.beyond
  19.9 0.0 collective-permute-done.swap
  20.0 0.5 %collective-permute-start.4 = (bf16[128,256]{1,0:T(8,128)(2,1)S(1)}, bf16[128,256]{1,0:T(8,128)(2,1)S(1)}, u32[]{:S(2)}, u32[]{:S(2)}) collective-permute-start(bf16[128,256]{1,0:T(8,128)(2,1)S(1)} %slice.15), channel_id=1, source_target_pairs={{0,1},{1,0},{2,3},{3,2},{4,5},{5,4},{6,7},{7,6},{8,9},{9,8},{10,11... | collective-permute-start | bytes 196616 | tf_op jit(solution)/shard_map/ppermute | solution.py:485
  20.5 0.1 collective-permute-start.5
  20.6 0.4 %collective-permute-start.6 = (bf16[128,256]{1,0:T(8,128)(2,1)S(1)}, bf16[128,256]{1,0:T(8,128)(2,1)S(1)}, u32[]{:S(2)}, u32[]{:S(2)}) collective-permute-start(bf16[128,256]{1,0:T(8,128)(2,1)S(1)} %collective-permute-done.2.beyond), channel_id=1, source_target_pairs={{0,1},{1,0},{2,3},{3,2},{4,5},{5,4},{6,7},{7,6},{8,9},{9,8},{10,11... | collective-permute-start | bytes 196616 | tf_op jit(solution)/shard_map/ppermute | solution.py:485
  21.0 0.4 collective-permute-done.3.mine_x
  21.4 0.2 collective-permute-start.11
  21.5 0.8 %collective-permute-done.12.refs_2_ = bf16[128,512]{1,0:T(8,128)(2,1)S(1)} collective-permute-done((bf16[128,512]{1,0:T(8,128)(2,1)S(1)}, bf16[128,512]{1,0:T(8,128)(2,1)S(1)}, u32[]{:S(2)}, u32[]{:S(2)}) %collective-permute-start.12) | collective-permute-done | bytes 131104 | tf_op jit(solution)/shard_map/ppermute | solution.py:481
  22.3 1.5 %collective-permute-start.9 = (bf16[144,1024]{1,0:T(8,128)(2,1)}, bf16[144,1024]{1,0:T(8,128)(2,1)S(1)}, u32[]{:S(2)}, u32[]{:S(2)}) collective-permute-start(bf16[144,1024]{1,0:T(8,128)(2,1)} %get-tuple-element.26), channel_id=1, source_target_pairs={{0,8},{1,9},{2,10},{3,11},{4,12},{5,13},{6,14},{7,15},{8,16},{9,17... | collective-permute-start | bytes 884744 | tf_op jit(solution)/shard_map/ppermute | solution.py:495
  23.8 0.0 collective-permute-done.4.near_x
  23.8 0.7 %collective-permute-start.14 = (bf16[128,512]{1,0:T(8,128)(2,1)S(1)}, bf16[128,512]{1,0:T(8,128)(2,1)S(1)}, u32[]{:S(2)}, u32[]{:S(2)}) collective-permute-start(bf16[128,512]{1,0:T(8,128)(2,1)S(1)} %collective-permute-done.12.refs_2_), channel_id=1, source_target_pairs={{2,4},{3,5},{4,6},{5,7},{10,12},{11,13},{12,14},{13,15},{18,20},{1... | collective-permute-start | bytes 393224 | tf_op jit(solution)/shard_map/ppermute | solution.py:481
  24.5 0.0 collective-permute-done.5.far_x
  24.5 0.7 %collective-permute-start.17 = (bf16[128,512]{1,0:T(8,128)(2,1)S(1)}, bf16[128,512]{1,0:T(8,128)(2,1)S(1)}, u32[]{:S(2)}, u32[]{:S(2)}) collective-permute-start(bf16[128,512]{1,0:T(8,128)(2,1)S(1)} %collective-permute-done.12.refs_2_), channel_id=1, source_target_pairs={{2,6},{3,7},{10,14},{11,15},{18,22},{19,23},{26,30},{27,31}} | collective-permute-start | bytes 393224 | tf_op jit(solution)/shard_map/ppermute | solution.py:481
  25.2 0.0 collective-permute-done.6.beyond_x
  25.2 0.0 copy-done.1
  25.2 0.0 copy-done.2
  25.2 0.0 copy-done
  25.2 0.8 %copy-done.3 = bf16[128,256]{1,0:T(8,128)(2,1)S(1)} copy-done((bf16[128,256]{1,0:T(8,128)(2,1)S(1)}, bf16[128,256]{1,0:T(8,128)(2,1)}, u32[]{:S(2)}) %copy-start.3) | copy-done | bytes 65560
  26.1 2.3 %attend_home.1 = (bf16[128,512]{1,0:T(8,128)(2,1)S(1)}, bf16[128,512]{1,0:T(8,128)(2,1)S(1)}) custom-call(bf16[1,128,2048]{2,1,0:T(8,128)(2,1)S(1)} %copy-done, bf16[144,768]{1,0:T(8,128)(2,1)S(1)} %collective-permute-done.swap, bf16[128,256]{1,0:T(8,128)(2,1)S(1)} %copy-done.3, bf16[128,256]{1,0:T(8,128)(2,1)S(1)} %collective-permute-done.3.mine_x, ...), custom_call_target="tpu_custom_call" | custom-call | flops 2000000000 | tf_op jit(solution)/shard_map/attend_home/pallas_call | solution.py:454
  28.4 7.8 %collective-permute-start.7 = (bf16[128,512]{1,0:T(8,128)(2,1)S(1)}, bf16[128,512]{1,0:T(8,128)(2,1)S(1)}, u32[]{:S(2)}, u32[]{:S(2)}) collective-permute-start(bf16[128,512]{1,0:T(8,128)(2,1)S(1)} %get-tuple-element.23), channel_id=1, source_target_pairs={{0,10},{1,11},{2,8},{3,9},{4,14},{5,15},{6,12},{7,13},{8,18},{9,19... | collective-permute-start | bytes 393224 | tf_op jit(solution)/shard_map/ppermute | solution.py:495
  36.2 0.0 collective-permute-done.14.refs_4_
  36.2 0.7 %collective-permute-start.8 = (bf16[128,512]{1,0:T(8,128)(2,1)S(1)}, bf16[128,512]{1,0:T(8,128)(2,1)S(1)}, u32[]{:S(2)}, u32[]{:S(2)}) collective-permute-start(bf16[128,512]{1,0:T(8,128)(2,1)S(1)} %get-tuple-element.24), channel_id=1, source_target_pairs={{0,8},{1,9},{2,10},{3,11},{4,12},{5,13},{6,14},{7,15},{8,16},{9,17... | collective-permute-start | bytes 393224 | tf_op jit(solution)/shard_map/ppermute | solution.py:495
  36.9 0.0 collective-permute-done.9.packed
  36.9 0.1 collective-permute-start.15
  37.0 0.0 collective-permute-done.11.refs_1_
  37.0 0.5 %collective-permute-start.16 = (bf16[128,256]{1,0:T(8,128)(2,1)S(1)}, bf16[128,256]{1,0:T(8,128)(2,1)S(1)}, u32[]{:S(2)}, u32[]{:S(2)}) collective-permute-start(bf16[128,256]{1,0:T(8,128)(2,1)S(1)} %get-tuple-element.31), channel_id=1, source_target_pairs={{0,1},{1,0},{2,3},{3,2},{4,5},{5,4},{6,7},{7,6},{8,9},{9,8},{10,11... | collective-permute-start | bytes 196616 | tf_op jit(solution)/shard_map/ppermute | solution.py:485
  37.5 0.0 collective-permute-done.17.refs_7_
  37.5 0.1 collective-permute-start.13
  37.6 0.6 %collective-permute-done.15.refs_5_ = bf16[128,256]{1,0:T(8,128)(2,1)S(1)} collective-permute-done((bf16[128,256]{1,0:T(8,128)(2,1)S(1)}, bf16[128,256]{1,0:T(8,128)(2,1)S(1)}, u32[]{:S(2)}, u32[]{:S(2)}) %collective-permute-start.15) | collective-permute-done | bytes 65568 | tf_op jit(solution)/shard_map/ppermute | solution.py:485
  38.3 0.2 collective-permute-start.18
  38.4 0.0 collective-permute-done.16.refs_6_
  38.4 0.4 collective-permute-start.19
  38.8 0.7 %collective-permute-done.18.refs_8_ = bf16[128,256]{1,0:T(8,128)(2,1)S(1)} collective-permute-done((bf16[128,256]{1,0:T(8,128)(2,1)S(1)}, bf16[128,256]{1,0:T(8,128)(2,1)S(1)}, u32[]{:S(2)}, u32[]{:S(2)}) %collective-permute-start.18) | collective-permute-done | bytes 65568 | tf_op jit(solution)/shard_map/ppermute | solution.py:485
  39.5 0.2 collective-permute-done.19.refs_9_
  39.7 0.0 collective-permute-done.13.refs_3_
  39.7 2.1 %attend_relayed.1 = bf16[128,1024]{1,0:T(8,128)(2,1)S(1)} custom-call(bf16[144,1024]{1,0:T(8,128)(2,1)S(1)} %collective-permute-done.9.packed, bf16[128,512]{1,0:T(8,128)(2,1)S(1)} %collective-permute-done.10.refs_0_, bf16[128,512]{1,0:T(8,128)(2,1)S(1)} %collective-permute-done.11.refs_1_, bf16[128,512]{1,0:T(8,128)(2,1)S(1)} %collective-permute-done.12.refs_2_, ...), custom_call_target="tpu_custom_call" | custom-call | tf_op jit(solution)/shard_map/attend_relayed/pallas_call | solution.py:469
  41.8 0.0 collective-permute-done.7
  41.8 0.3 collective-permute-done.8
  42.1 0.9 %fusion = bf16[1,128,2048]{2,1,0:T(8,128)(2,1)} fusion(bf16[1,128,1024]{2,1,0:T(8,128)(2,1)S(1)} %bitcast.3, bf16[1,128,512]{2,1,0:T(8,128)(2,1)S(1)} %bitcast.5, bf16[1,128,512]{2,1,0:T(8,128)(2,1)S(1)} %bitcast.4, pred[]{:T(512)S(6)} %eq.3), kind=kLoop, calls=%fused_computation.2 | loop fusion | flops 3145728 | bytes 1048577 | tf_op jit(solution)/shard_map/jit(_where)/select_n | solution.py:542
  (7 shorter events, 0.0 us)
Async XLA Ops:
  0.0 25.2 %copy-start.1 = (s32[1,1024]{1,0:T(1,128)S(1)}, s32[1,1024]{1,0:T(1,128)}, u32[]{:S(2)}) copy-start(s32[1,1024]{1,0:T(1,128)} %docs.3) | copy-start | bytes 12292
  0.0 25.2 %copy-start.2 = (s32[1,128]{1,0:T(1,128)S(1)}, s32[1,128]{1,0:T(1,128)}, u32[]{:S(2)}) copy-start(s32[1,128]{1,0:T(1,128)} %scored.3) | copy-start | bytes 1540
  0.0 25.2 %copy-start = (bf16[1,128,2048]{2,1,0:T(8,128)(2,1)S(1)}, bf16[1,128,2048]{2,1,0:T(8,128)(2,1)}, u32[]{:S(2)}) copy-start(bf16[1,128,2048]{2,1,0:T(8,128)(2,1)} %queries.3) | copy-start | bytes 1572868
  7.0 13.0 %collective-permute-start = (bf16[144,768]{1,0:T(8,128)(2,1)}, bf16[144,768]{1,0:T(8,128)(2,1)S(1)}, u32[]{:S(2)}, u32[]{:S(2)}) collective-permute-start(bf16[144,768]{1,0:T(8,128)(2,1)} %get-tuple-element.17), channel_id=1, source_target_pairs={{0,2},{1,3},{2,0},{3,1},{4,6},{5,7},{6,4},{7,5},{8,10},{9,11},{10,... | collective-permute-start | bytes 663560 | tf_op jit(solution)/shard_map/ppermute | solution.py:481
  10.1 7.3 %collective-permute-start.10 = (bf16[128,512]{1,0:T(8,128)(2,1)}, bf16[128,512]{1,0:T(8,128)(2,1)S(1)}, u32[]{:S(2)}, u32[]{:S(2)}) collective-permute-start(bf16[128,512]{1,0:T(8,128)(2,1)} %get-tuple-element.27), channel_id=1, source_target_pairs={{0,8},{1,9},{2,10},{3,11},{4,12},{5,13},{6,14},{7,15},{8,16},{9,17... | collective-permute-start | bytes 393224 | tf_op jit(solution)/shard_map/ppermute | solution.py:495
  11.6 8.4 %collective-permute-start.1 = (bf16[128,256]{1,0:T(8,128)(2,1)}, bf16[128,256]{1,0:T(8,128)(2,1)S(1)}, u32[]{:S(2)}, u32[]{:S(2)}) collective-permute-start(bf16[128,256]{1,0:T(8,128)(2,1)} %get-tuple-element.18.mine), channel_id=1, source_target_pairs={{0,4},{1,5},{2,6},{3,7},{8,12},{9,13},{10,14},{11,15},{16,20},{17,... | collective-permute-start | bytes 196616 | tf_op jit(solution)/shard_map/ppermute | solution.py:481
  16.1 3.9 %collective-permute-start.2 = (bf16[128,256]{1,0:T(8,128)(2,1)}, bf16[128,256]{1,0:T(8,128)(2,1)S(1)}, u32[]{:S(2)}, u32[]{:S(2)}) collective-permute-start(bf16[128,256]{1,0:T(8,128)(2,1)} %get-tuple-element.19), channel_id=1, source_target_pairs={{0,6},{1,7},{2,4},{3,5},{8,14},{9,15},{10,12},{11,13},{16,22},{17,... | collective-permute-start | bytes 196616 | tf_op jit(solution)/shard_map/ppermute | solution.py:481
  17.4 5.0 %collective-permute-start.12 = (bf16[128,512]{1,0:T(8,128)(2,1)S(1)}, bf16[128,512]{1,0:T(8,128)(2,1)S(1)}, u32[]{:S(2)}, u32[]{:S(2)}) collective-permute-start(bf16[128,512]{1,0:T(8,128)(2,1)S(1)} %collective-permute-done.10.refs_0_), channel_id=1, source_target_pairs={{0,2},{1,3},{2,4},{3,5},{4,6},{5,7},{8,10},{9,11},{10,12},{11,13},... | collective-permute-start | bytes 393224 | tf_op jit(solution)/shard_map/ppermute | solution.py:481
  19.8 1.5 %collective-permute-start.3 = (bf16[128,256]{1,0:T(8,128)(2,1)}, bf16[128,256]{1,0:T(8,128)(2,1)S(1)}, u32[]{:S(2)}, u32[]{:S(2)}) collective-permute-start(bf16[128,256]{1,0:T(8,128)(2,1)} %get-tuple-element.18.mine), channel_id=1, source_target_pairs={{0,1},{1,0},{2,3},{3,2},{4,5},{5,4},{6,7},{7,6},{8,9},{9,8},{10,11... | collective-permute-start | bytes 196616 | tf_op jit(solution)/shard_map/ppermute | solution.py:485
  20.0 3.9 %collective-permute-start.4 = (bf16[128,256]{1,0:T(8,128)(2,1)S(1)}, bf16[128,256]{1,0:T(8,128)(2,1)S(1)}, u32[]{:S(2)}, u32[]{:S(2)}) collective-permute-start(bf16[128,256]{1,0:T(8,128)(2,1)S(1)} %slice.15), channel_id=1, source_target_pairs={{0,1},{1,0},{2,3},{3,2},{4,5},{5,4},{6,7},{7,6},{8,9},{9,8},{10,11... | collective-permute-start | bytes 196616 | tf_op jit(solution)/shard_map/ppermute | solution.py:485
  20.5 4.0 %collective-permute-start.5 = (bf16[128,256]{1,0:T(8,128)(2,1)S(1)}, bf16[128,256]{1,0:T(8,128)(2,1)S(1)}, u32[]{:S(2)}, u32[]{:S(2)}) collective-permute-start(bf16[128,256]{1,0:T(8,128)(2,1)S(1)} %collective-permute-done.1.far), channel_id=1, source_target_pairs={{0,1},{1,0},{2,3},{3,2},{4,5},{5,4},{6,7},{7,6},{8,9},{9,8},{10,11... | collective-permute-start | bytes 196616 | tf_op jit(solution)/shard_map/ppermute | solution.py:485
  20.6 4.6 %collective-permute-start.6 = (bf16[128,256]{1,0:T(8,128)(2,1)S(1)}, bf16[128,256]{1,0:T(8,128)(2,1)S(1)}, u32[]{:S(2)}, u32[]{:S(2)}) collective-permute-start(bf16[128,256]{1,0:T(8,128)(2,1)S(1)} %collective-permute-done.2.beyond), channel_id=1, source_target_pairs={{0,1},{1,0},{2,3},{3,2},{4,5},{5,4},{6,7},{7,6},{8,9},{9,8},{10,11... | collective-permute-start | bytes 196616 | tf_op jit(solution)/shard_map/ppermute | solution.py:485
  21.4 15.6 %collective-permute-start.11 = (bf16[128,512]{1,0:T(8,128)(2,1)S(1)}, bf16[128,512]{1,0:T(8,128)(2,1)S(1)}, u32[]{:S(2)}, u32[]{:S(2)}) collective-permute-start(bf16[128,512]{1,0:T(8,128)(2,1)S(1)} %collective-permute-done.10.refs_0_), channel_id=1, source_target_pairs={{0,1},{1,0},{2,3},{3,2},{4,5},{5,4},{6,7},{7,6},{8,9},{9,8},{10,11... | collective-permute-start | bytes 393224 | tf_op jit(solution)/shard_map/ppermute | solution.py:485
  22.3 14.6 %collective-permute-start.9 = (bf16[144,1024]{1,0:T(8,128)(2,1)}, bf16[144,1024]{1,0:T(8,128)(2,1)S(1)}, u32[]{:S(2)}, u32[]{:S(2)}) collective-permute-start(bf16[144,1024]{1,0:T(8,128)(2,1)} %get-tuple-element.26), channel_id=1, source_target_pairs={{0,8},{1,9},{2,10},{3,11},{4,12},{5,13},{6,14},{7,15},{8,16},{9,17... | collective-permute-start | bytes 884744 | tf_op jit(solution)/shard_map/ppermute | solution.py:495
  23.8 12.4 %collective-permute-start.14 = (bf16[128,512]{1,0:T(8,128)(2,1)S(1)}, bf16[128,512]{1,0:T(8,128)(2,1)S(1)}, u32[]{:S(2)}, u32[]{:S(2)}) collective-permute-start(bf16[128,512]{1,0:T(8,128)(2,1)S(1)} %collective-permute-done.12.refs_2_), channel_id=1, source_target_pairs={{2,4},{3,5},{4,6},{5,7},{10,12},{11,13},{12,14},{13,15},{18,20},{1... | collective-permute-start | bytes 393224 | tf_op jit(solution)/shard_map/ppermute | solution.py:481
  24.5 13.0 %collective-permute-start.17 = (bf16[128,512]{1,0:T(8,128)(2,1)S(1)}, bf16[128,512]{1,0:T(8,128)(2,1)S(1)}, u32[]{:S(2)}, u32[]{:S(2)}) collective-permute-start(bf16[128,512]{1,0:T(8,128)(2,1)S(1)} %collective-permute-done.12.refs_2_), channel_id=1, source_target_pairs={{2,6},{3,7},{10,14},{11,15},{18,22},{19,23},{26,30},{27,31}} | collective-permute-start | bytes 393224 | tf_op jit(solution)/shard_map/ppermute | solution.py:481
  25.2 0.8 %copy-start.3 = (bf16[128,256]{1,0:T(8,128)(2,1)S(1)}, bf16[128,256]{1,0:T(8,128)(2,1)}, u32[]{:S(2)}) copy-start(bf16[128,256]{1,0:T(8,128)(2,1)} %get-tuple-element.18.mine) | copy-start | bytes 196612
  28.4 13.4 %collective-permute-start.7 = (bf16[128,512]{1,0:T(8,128)(2,1)S(1)}, bf16[128,512]{1,0:T(8,128)(2,1)S(1)}, u32[]{:S(2)}, u32[]{:S(2)}) collective-permute-start(bf16[128,512]{1,0:T(8,128)(2,1)S(1)} %get-tuple-element.23), channel_id=1, source_target_pairs={{0,10},{1,11},{2,8},{3,9},{4,14},{5,15},{6,12},{7,13},{8,18},{9,19... | collective-permute-start | bytes 393224 | tf_op jit(solution)/shard_map/ppermute | solution.py:495
  36.2 5.9 %collective-permute-start.8 = (bf16[128,512]{1,0:T(8,128)(2,1)S(1)}, bf16[128,512]{1,0:T(8,128)(2,1)S(1)}, u32[]{:S(2)}, u32[]{:S(2)}) collective-permute-start(bf16[128,512]{1,0:T(8,128)(2,1)S(1)} %get-tuple-element.24), channel_id=1, source_target_pairs={{0,8},{1,9},{2,10},{3,11},{4,12},{5,13},{6,14},{7,15},{8,16},{9,17... | collective-permute-start | bytes 393224 | tf_op jit(solution)/shard_map/ppermute | solution.py:495
  36.9 1.3 %collective-permute-start.15 = (bf16[128,256]{1,0:T(8,128)(2,1)S(1)}, bf16[128,256]{1,0:T(8,128)(2,1)S(1)}, u32[]{:S(2)}, u32[]{:S(2)}) collective-permute-start(bf16[128,256]{1,0:T(8,128)(2,1)S(1)} %get-tuple-element.32), channel_id=1, source_target_pairs={{0,1},{1,0},{2,3},{3,2},{4,5},{5,4},{6,7},{7,6},{8,9},{9,8},{10,11... | collective-permute-start | bytes 196616 | tf_op jit(solution)/shard_map/ppermute | solution.py:485
  37.0 1.4 %collective-permute-start.16 = (bf16[128,256]{1,0:T(8,128)(2,1)S(1)}, bf16[128,256]{1,0:T(8,128)(2,1)S(1)}, u32[]{:S(2)}, u32[]{:S(2)}) collective-permute-start(bf16[128,256]{1,0:T(8,128)(2,1)S(1)} %get-tuple-element.31), channel_id=1, source_target_pairs={{0,1},{1,0},{2,3},{3,2},{4,5},{5,4},{6,7},{7,6},{8,9},{9,8},{10,11... | collective-permute-start | bytes 196616 | tf_op jit(solution)/shard_map/ppermute | solution.py:485
  37.5 2.2 %collective-permute-start.13 = (bf16[128,512]{1,0:T(8,128)(2,1)S(1)}, bf16[128,512]{1,0:T(8,128)(2,1)S(1)}, u32[]{:S(2)}, u32[]{:S(2)}) collective-permute-start(bf16[128,512]{1,0:T(8,128)(2,1)S(1)} %collective-permute-done.12.refs_2_), channel_id=1, source_target_pairs={{0,1},{1,0},{2,3},{3,2},{4,5},{5,4},{6,7},{7,6},{8,9},{9,8},{10,11... | collective-permute-start | bytes 393224 | tf_op jit(solution)/shard_map/ppermute | solution.py:485
  38.3 1.3 %collective-permute-start.18 = (bf16[128,256]{1,0:T(8,128)(2,1)S(1)}, bf16[128,256]{1,0:T(8,128)(2,1)S(1)}, u32[]{:S(2)}, u32[]{:S(2)}) collective-permute-start(bf16[128,256]{1,0:T(8,128)(2,1)S(1)} %get-tuple-element.30), channel_id=1, source_target_pairs={{0,1},{1,0},{2,3},{3,2},{4,5},{5,4},{6,7},{7,6},{8,9},{9,8},{10,11... | collective-permute-start | bytes 196616 | tf_op jit(solution)/shard_map/ppermute | solution.py:485
  38.4 1.3 %collective-permute-start.19 = (bf16[128,256]{1,0:T(8,128)(2,1)S(1)}, bf16[128,256]{1,0:T(8,128)(2,1)S(1)}, u32[]{:S(2)}, u32[]{:S(2)}) collective-permute-start(bf16[128,256]{1,0:T(8,128)(2,1)S(1)} %get-tuple-element.29), channel_id=1, source_target_pairs={{0,1},{1,0},{2,3},{3,2},{4,5},{5,4},{6,7},{7,6},{8,9},{9,8},{10,11... | collective-permute-start | bytes 196616 | tf_op jit(solution)/shard_map/ppermute | solution.py:485

commit v3 on v2

--- a/solution.py
+++ b/solution.py
@@ -114,16 +114,12 @@
     return from_behind(outgoing, "phase", 1)
 
 
-def rotary_tables(rows, devices):
+def rotary_table(rows, devices):
     half = HEAD_SIZE // 2
     frequency = (rope_base ** (-np.arange(half) * 2.0 / HEAD_SIZE)).astype(np.float32).astype(np.float64)
     frequency = np.concatenate([frequency, frequency])[None, :]
-    within = np.arange(rows)[:, None] * frequency
-    starts = np.arange(devices)[:, None] * (rows * frequency)
-    return [
-        jnp.asarray(np.concatenate([np.cos(x), np.sin(x)], axis=1), jnp.float32)
-        for x in (within, starts)
-    ]
+    angles = np.concatenate([np.arange(rows), rows * np.arange(devices)])[:, None] * frequency
+    return jnp.asarray(np.concatenate([np.cos(angles), np.sin(angles)], axis=1), jnp.float32)
 
 
 def parity():
@@ -135,8 +131,7 @@
     hidden,
     weight,
     queries,
-    within,
-    starts,
+    table,
     docs,
     scored,
     mine,
@@ -147,48 +142,77 @@
     wide,
     store,
     normed,
-    hidden_sem,
-    query_sems,
+    angles,
+    doc_row,
+    scored_row,
+    mine_out,
+    other_out,
+    swap_out,
+    away_out,
+    packed_out,
+    in_sems,
     weight_sems,
+    out_sems,
 ):
     rows, width = wide.shape[0], packed.shape[1]
     odd = parity()
-    load_hidden = pltpu.make_async_copy(hidden.at[0], wide, hidden_sem)
-    load_hidden.start()
+    own = slice(0, rows)
+    sources = [
+        (hidden.at[0], wide),
+        (table, angles),
+        (docs, doc_row),
+        (scored, scored_row),
+        (
+            queries.at[0, :, pl.ds(pl.multiple_of((1 - odd) * GROUP_WIDTH, GROUP_WIDTH), GROUP_WIDTH)],
+            swap_out.at[pl.ds(0, rows), pl.ds(PAIR_WIDTH, GROUP_WIDTH)],
+        ),
+        (queries.at[0, :, pl.ds(width, width)], packed_out.at[pl.ds(0, rows), :]),
+    ]
+    loads = [
+        pltpu.make_async_copy(source, target, in_sems.at[i])
+        for i, (source, target) in enumerate(sources)
+    ]
+    loads[0].start()
     copies = []
     for i, (start, stop) in enumerate(cuts):
         span = pl.ds(start, stop - start)
         copy = pltpu.make_async_copy(weight.at[0, span, :], store.at[span, :], weight_sems.at[i])
         copy.start()
         copies.append(copy)
-    asked = pl.ds(pl.multiple_of((1 - odd) * GROUP_WIDTH, GROUP_WIDTH), GROUP_WIDTH)
-    cut_queries = [
-        pltpu.make_async_copy(
-            queries.at[0, :, asked], swap.at[pl.ds(0, rows), pl.ds(PAIR_WIDTH, GROUP_WIDTH)], query_sems.at[0]
-        ),
-        pltpu.make_async_copy(
-            queries.at[0, :, pl.ds(width, width)], packed.at[pl.ds(0, rows), :], query_sems.at[1]
-        ),
+    for load in loads[1:]:
+        load.start()
+    results = [
+        pltpu.make_async_copy(source, target, out_sems.at[i])
+        for i, (source, target) in enumerate(
+            (
+                (swap_out, swap),
+                (away_out, away),
+                (mine_out, mine),
+                (other_out, other),
+                (packed_out, packed),
+            )
+        )
     ]
-    for copy in cut_queries:
-        copy.start()
-    marks = jnp.concatenate([scored[...]] * (width // rows), axis=1)
-    notes = [docs[...], marks, jnp.zeros((NOTE_ROWS - 2, width), jnp.int32)]
+    loads[0].wait()
+    values = wide[...].astype(jnp.float32)
+    scale = lax.rsqrt(jnp.mean(values * values, axis=-1, keepdims=True) + 1e-05)
+    normed[...] = (values * scale).astype(jnp.bfloat16)
+    for load in loads[1:]:
+        load.wait()
+    marks = jnp.concatenate([scored_row[...]] * (width // rows), axis=1)
+    notes = [doc_row[...], marks, jnp.zeros((NOTE_ROWS - 2, width), jnp.int32)]
     notes = jnp.concatenate(notes, axis=0).astype(jnp.float32).astype(jnp.bfloat16)
-    packed[rows:, :] = notes
-    swap[rows:, :] = notes[:, : swap.shape[1]]
-    base = starts[pl.ds(lax.axis_index("ctx"), 1), :]
+    packed_out[rows:, :] = notes
+    swap_out[rows:, :] = notes[:, : swap.shape[1]]
+    results[4].start()
+    base = angles[pl.ds(rows + lax.axis_index("ctx"), 1), :]
     base_cosine, base_sine = base[:, :HEAD_SIZE], base[:, HEAD_SIZE:]
-    cosine, sine = within[:, :HEAD_SIZE], within[:, HEAD_SIZE:]
+    cosine, sine = angles[own, :HEAD_SIZE], angles[own, HEAD_SIZE:]
     cosine, sine = (
         cosine * base_cosine - sine * base_sine,
         sine * base_cosine + cosine * base_sine,
     )
     sine = jnp.where(lax.broadcasted_iota(jnp.int32, sine.shape, 1) < HEAD_SIZE // 2, -sine, sine)
-    load_hidden.wait()
-    values = wide[...].astype(jnp.float32)
-    scale = lax.rsqrt(jnp.mean(values * values, axis=-1, keepdims=True) + 1e-05)
-    normed[...] = (values * scale).astype(jnp.bfloat16)
     total = None
     for copy, (start, stop) in zip(copies, cuts):
         copy.wait()
@@ -203,51 +227,81 @@
         at = (KEY_VALUE_HEADS + head) * HEAD_SIZE
         value = total[:, at : at + HEAD_SIZE]
         pairs.append(jnp.concatenate([key, value], axis=1).astype(jnp.bfloat16))
-    away[:, :PAIR_WIDTH] = pairs[2]
-    away[:, PAIR_WIDTH:] = pairs[3]
     for u in range(2):
 
         @pl.when(odd == u)
         def _():
-            mine[...] = pairs[u]
-            other[...] = pairs[1 - u]
-            swap[:rows, :PAIR_WIDTH] = pairs[1 - u]
-
-    for copy in cut_queries:
-        copy.wait()
+            mine_out[...] = pairs[u]
+            other_out[...] = pairs[1 - u]
+            swap_out[own, :PAIR_WIDTH] = pairs[1 - u]
+
+    away_out[:, :PAIR_WIDTH] = pairs[2]
+    away_out[:, PAIR_WIDTH:] = pairs[3]
+    for result in results[:4]:
+        result.start()
+    for result in results:
+        result.wait()
 
 
 def project(hidden, weight, queries, docs, scored):
     rows, width = hidden.shape[1], hidden.shape[2]
     columns = weight.shape[2]
     cuts = ((0, width // 2), (width // 2, width))
-    within, starts = rotary_tables(rows, docs.shape[1] // rows)
+    table = rotary_table(rows, docs.shape[1] // rows)
     hbm = pl.BlockSpec(memory_space=pltpu.HBM)
-    vmem = pl.BlockSpec(memory_space=pltpu.VMEM)
-    pair = jax.ShapeDtypeStruct((rows, PAIR_WIDTH), jnp.bfloat16)
+    shapes = [
+        (rows, PAIR_WIDTH),
+        (rows, PAIR_WIDTH),
+        (rows + NOTE_ROWS, PAIR_WIDTH + GROUP_WIDTH),
+        (rows, 2 * PAIR_WIDTH),
+        (rows + NOTE_ROWS, 2 * GROUP_WIDTH),
+    ]
     return pl.pallas_call(
         functools.partial(project_kernel, cuts),
-        out_shape=(
-            pair,
-            pair,
-            jax.ShapeDtypeStruct((rows + NOTE_ROWS, PAIR_WIDTH + GROUP_WIDTH), jnp.bfloat16),
-            jax.ShapeDtypeStruct((rows, 2 * PAIR_WIDTH), jnp.bfloat16),
-            jax.ShapeDtypeStruct((rows + NOTE_ROWS, 2 * GROUP_WIDTH), jnp.bfloat16),
-        ),
-        in_specs=[hbm, hbm, hbm, vmem, vmem, vmem, vmem],
-        out_specs=(vmem,) * 5,
+        out_shape=[jax.ShapeDtypeStruct(shape, jnp.bfloat16) for shape in shapes],
+        in_specs=[hbm] * 6,
+        out_specs=[hbm] * 5,
         scratch_shapes=[
             pltpu.VMEM((rows, width), jnp.bfloat16),
             pltpu.VMEM((width, columns), jnp.bfloat16),
             pltpu.VMEM((rows, width), jnp.bfloat16),
-            pltpu.SemaphoreType.DMA,
-            pltpu.SemaphoreType.DMA((2,)),
+            pltpu.VMEM(table.shape, jnp.float32),
+            pltpu.VMEM(docs.shape, jnp.int32),
+            pltpu.VMEM(scored.shape, jnp.int32),
+        ]
+        + [pltpu.VMEM(shape, jnp.bfloat16) for shape in shapes]
+        + [
+            pltpu.SemaphoreType.DMA((6,)),
             pltpu.SemaphoreType.DMA((len(cuts),)),
+            pltpu.SemaphoreType.DMA((5,)),
         ],
         compiler_params=pltpu.CompilerParams(vmem_limit_bytes=63 * 2**20),
         cost_estimate=pl.CostEstimate(flops=0, bytes_accessed=0, transcendentals=0),
         name="project",
-    )(hidden, weight, queries, within, starts, docs, scored)
+    )(hidden, weight, queries, table, docs, scored)
+
+
+def attended(q, keys, values, bias, factor):
+    scores = jnp.concatenate(
+        [
+            lax.dot_general(q, k, (((1,), (1,)), ((), ())), preferred_element_type=jnp.float32)
+            for k in keys
+        ],
+        axis=1,
+    )
+    scores = scores + bias
+    row_max = jnp.max(scores, axis=-1, keepdims=True)
+    expo = jnp.exp2((scores - row_max) * factor)
+    total = jnp.sum(expo, axis=-1, keepdims=True)
+    weights = expo.astype(jnp.bfloat16)
+    summed, at = None, 0
+    for value in values:
+        part = jnp.dot(
+            weights[:, at : at + value.shape[0]], value, preferred_element_type=jnp.float32
+        )
+        summed = part if summed is None else summed + part
+        at += value.shape[0]
+    return summed / total
 
 
 def attend_body(q, kvs, doc_row, kept, bias, put):
@@ -275,50 +329,30 @@
 
     kept_rows = jnp.broadcast_to(kept, (rows, rows)).T[:, :1]
     factor = math.log2(math.e) / math.sqrt(HEAD_SIZE)
-    for head in range(2):
-        at = head * PAIR_WIDTH
-        for half in range(GROUP // 2):
-            first = (head * GROUP + 2 * half) * HEAD_SIZE
-            pair = jnp.concatenate(
-                [q[:, first : first + HEAD_SIZE], q[:, first + HEAD_SIZE : first + 2 * HEAD_SIZE]],
-                axis=0,
-            )
-            scores = []
-            for back in range(4):
-                keys = jnp.concatenate(
-                    [kvs[2 * back + b][:, at : at + HEAD_SIZE] for b in range(2)], axis=0
-                )
-                part = lax.dot_general(
-                    pair, keys, (((1,), (1,)), ((), ())), preferred_element_type=jnp.float32
-                )
-                block_bias = bias[:, 2 * back * rows : 2 * (back + 1) * rows]
-                scores.append(part + jnp.concatenate([block_bias, block_bias], axis=0))
-            scores = jnp.concatenate(scores, axis=1)
-            row_max = jnp.max(scores, axis=-1, keepdims=True)
-            expo = jnp.exp2((scores - row_max) * factor)
-            total = jnp.sum(expo, axis=-1, keepdims=True)
-            weights = expo.astype(jnp.bfloat16)
-            summed = None
-            for back in range(4):
-                values = jnp.concatenate(
-                    [
-                        kvs[2 * back + b][:, at + HEAD_SIZE : at + 2 * HEAD_SIZE]
-                        for b in range(2)
-                    ],
-                    axis=0,
-                )
-                part = jnp.dot(
-                    weights[:, 2 * back * rows : 2 * (back + 1) * rows],
-                    values,
-                    preferred_element_type=jnp.float32,
-                )
-                summed = part if summed is None else summed + part
-            result = summed / total
-            for i in range(2):
-                put(
-                    first + i * HEAD_SIZE,
-                    (result[i * rows : (i + 1) * rows] * kept_rows).astype(jnp.bfloat16),
-                )
+
+    def heads(count):
+        for head in range(2):
+            keys, values = [
+                [
+                    jnp.concatenate(
+                        [kvs[2 * back + b][:, at : at + HEAD_SIZE] for b in range(2)], axis=0
+                    )
+                    for back in range(count)
+                ]
+                for at in (head * PAIR_WIDTH, head * PAIR_WIDTH + HEAD_SIZE)
+            ]
+            for half in range(GROUP // 2):
+                at = [(head * GROUP + 2 * half + i) * HEAD_SIZE for i in range(2)]
+                pair = jnp.concatenate([q[:, x : x + HEAD_SIZE] for x in at], axis=0)
+                mask = bias[:, : 2 * count * rows]
+                mask = jnp.concatenate([mask, mask], axis=0)
+                result = attended(pair, keys, values, mask, factor)
+                for i in range(2):
+                    part = result[i * rows : (i + 1) * rows] * kept_rows
+                    put(at[i], part.astype(jnp.bfloat16))
+
+    pl.when(chip >= 2)(lambda: heads(4))
+    pl.when(chip < 2)(lambda: heads(2))
 
 
 def attend_home_kernel(
@@ -375,36 +409,21 @@
         ],
         axis=0,
     )
-    keys, values = blocks(0), blocks(HEAD_SIZE)
     factor = math.log2(math.e) / math.sqrt(HEAD_SIZE)
-    for head in range(GROUP):
-        at = head * HEAD_SIZE
-        q = jnp.concatenate(
-            [queries[0, :, at : at + HEAD_SIZE], swap[:rows, PAIR_WIDTH + at : PAIR_WIDTH + at + HEAD_SIZE]], axis=0
-        )
-        scores = jnp.concatenate(
-            [
-                lax.dot_general(q, k, (((1,), (1,)), ((), ())), preferred_element_type=jnp.float32)
-                for k in keys
-            ],
-            axis=1,
-        )
-        scores = scores + bias[...]
-        row_max = jnp.max(scores, axis=-1, keepdims=True)
-        expo = jnp.exp2((scores - row_max) * factor)
-        total = jnp.sum(expo, axis=-1, keepdims=True)
-        weights = expo.astype(jnp.bfloat16)
-        summed = None
-        for i, value in enumerate(values):
-            part = jnp.dot(
-                weights[:, 2 * i * rows : 2 * (i + 1) * rows],
-                value,
-                preferred_element_type=jnp.float32,
-            )
-            summed = part if summed is None else summed + part
-        result = (summed / total * kept).astype(jnp.bfloat16)
-        out_own[:, at : at + HEAD_SIZE] = result[:rows]
-        out_other[:, at : at + HEAD_SIZE] = result[rows:]
+
+    def heads(count):
+        keys, values = blocks(0)[:count], blocks(HEAD_SIZE)[:count]
+        for head in range(GROUP):
+            at = head * HEAD_SIZE
+            asked = swap[:rows, PAIR_WIDTH + at : PAIR_WIDTH + at + HEAD_SIZE]
+            q = jnp.concatenate([queries[0, :, at : at + HEAD_SIZE], asked], axis=0)
+            result = attended(q, keys, values, bias[:, : 2 * count * rows], factor)
+            result = (result * kept).astype(jnp.bfloat16)
+            out_own[:, at : at + HEAD_SIZE] = result[:rows]
+            out_other[:, at : at + HEAD_SIZE] = result[rows:]
+
+    pl.when(far_off)(lambda: heads(4))
+    pl.when(jnp.logical_not(far_off))(lambda: heads(2))
 
 
 class Halves:
@@ -495,7 +514,7 @@
     return lax.ppermute(block, ("phase", "ctx"), route)
 
 
-HOME_FLOPS = 2 * 10**9
+HOME_FLOPS = int(1.9 * 10**9)
 RELAYED_FLOPS = 0
 
 
@@ -514,16 +533,17 @@
     swap = send(swap, ((0, 1), (1, 0), (2, 3), (3, 2)))
     far = send(mine, ((0, 2), (1, 3)))
     beyond = send(other, ((0, 3), (1, 2)))
-    packed = onward(after(packed, swap))
+    packed = onward(packed)
     away_1 = send(away, ((0, 1), (1, 2), (2, 3)))
     away_2 = send(away_1, ((1, 2), (2, 3)))
     away_3 = send(away_1, ((1, 3),))
     swap, far, beyond = lax.optimization_barrier((swap, far, beyond))
+    mine_x = across(mine)
     own, partners = attend_home(
         queries,
         swap,
-        mine,
-        across(mine),
+        across(mine_x),
+        mine_x,
         across(swap[: mine.shape[0], :PAIR_WIDTH]),
         far,
         across(far),

time: 43.2 us -> 41.3 us (0.956)
  Pallas kernels: 11.4 us -> 9.48 us
  local copies, waits for them, and re-layouts: 0.87 us -> 0.04 us
  starting transfers between devices: 26.6 us -> 27.3 us
    ppermute x4, starting transfers between devices: 11.5 us -> 12.6 us  [onward(): return lax.ppermute(block, ('phase', 'ctx'), route)]
    unnamed x8 -> x6, local copies, waits for them, and re-layouts: 0.84 us -> 0.01 us
    pallas_call x1, Pallas kernels: 2.32 us -> 1.6 us  [attend_home(): pl.pallas_call(attend_home_kernel, grid=(1,), out_shape=(out, out), in_sp...]
    pallas_call x1, Pallas kernels: 6.95 us -> 6.36 us  [project(): pl.pallas_call(functools.partial(project_kernel, cuts), out_shape=[jax.Sh...]
    ppermute x4, waiting for transfers between devices: 0.3 us -> 0.89 us  [onward(): return lax.ppermute(block, ('phase', 'ctx'), route)]
    pallas_call x1, Pallas kernels: 2.09 us -> 1.52 us  [attend_relayed(): pl.pallas_call(attend_relayed_kernel, out_shape=jax.ShapeDtypeStruct((row...]
    ppermute x10 -> x11, starting transfers between devices: 2.44 us -> 1.98 us  [across(): lax.ppermute(block, 'ctx', [(i, i ^ 1) for i in range(lax.axis_size('ctx'...]
    ppermute x10 -> x11, waiting for transfers between devices: 1.91 us -> 1.56 us  [across(): lax.ppermute(block, 'ctx', [(i, i ^ 1) for i in range(lax.axis_size('ctx'...]
  transfers between devices with their start and end apart: 20 -> 21, of which waited for: 6 -> 6; matrix products, arithmetic and copies ran while one was open for 0% -> 0% of each run, Pallas kernels for 10% -> 8%
where the time goes in v3:
time: 41.3 us; the launch traced here: 41.1 us
  starting transfers between devices  27.3 us (66%)
  Pallas kernels  9.48 us (23%)
  waiting for transfers between devices  3.18 us (8%)
  other arithmetic  0.89 us (2%)
    ppermute x6, starting transfers between devices, send(): return lax.ppermute(block, 'ctx', pairs)  12.7 us
    ppermute x4, starting transfers between devices, onward(): return lax.ppermute(block, ('phase', 'ctx'), route)  12.6 us
    pallas_call x1, Pallas kernels, project(): pl.pallas_call(functools.partial(project_kernel, cuts), out_shape=[jax.Sh...  6.36 us
    ppermute x11, starting transfers between devices, across(): lax.ppermute(block, 'ctx', [(i, i ^ 1) for i in range(lax.axis_size('ctx'...  1.98 us
    pallas_call x1, Pallas kernels, attend_home(): pl.pallas_call(attend_home_kernel, grid=(1,), out_shape=(out, out), in_sp...  1.6 us
    ppermute x11, waiting for transfers between devices, across(): lax.ppermute(block, 'ctx', [(i, i ^ 1) for i in range(lax.axis_size('ctx'...  1.56 us
    pallas_call x1, Pallas kernels, attend_relayed(): pl.pallas_call(attend_relayed_kernel, out_shape=jax.ShapeDtypeStruct((row...  1.52 us
    select_n x1, other arithmetic, paired(): return jnp.where(parity() == 1, crossed, straight)[None]  0.89 us
  transfers between devices with their start and end apart: 21, of which 6 were waited for; matrix products, arithmetic and copies ran while one was open for 0% of the time, Pallas kernels for 8%

profile of v3, /device:TPU:0, one launch (start us, length us, event | category | flops | bytes accessed | tf_op | source)
XLA Modules:
  0.0 41.1 jit_solution(3215081664365316603)
XLA Ops:
  0.0 6.4 %project.1 = (bf16[128,256]{1,0:T(8,128)(2,1)}, bf16[128,256]{1,0:T(8,128)(2,1)}, bf16[144,768]{1,0:T(8,128)(2,1)}, bf16[128,512]{1,0:T(8,128)(2,1)}, bf16[144,1024]{1,0:T(8,128)(2,1)}) custom-call(bf16[1,128,4096]{2,1,0:T(8,128)(2,1)} %hidden.1, bf16[1,4096,1024]{2,1,0:T(8,128)(2,1)} %weight.1, bf16[1,128,2048]{2,1,0:T(8,128)(2,1)} %queries.3, ...), custom_call_target="tpu_custom_call" | custom-call | tf_op jit(solution)/shard_map/project/pallas_call | solution.py:259
  6.4 3.1 %collective-permute-start = (bf16[144,768]{1,0:T(8,128)(2,1)}, bf16[144,768]{1,0:T(8,128)(2,1)S(1)}, u32[]{:S(2)}, u32[]{:S(2)}) collective-permute-start(bf16[144,768]{1,0:T(8,128)(2,1)} %get-tuple-element.16), channel_id=1, source_target_pairs={{0,2},{1,3},{2,0},{3,1},{4,6},{5,7},{6,4},{7,5},{8,10},{9,11},{10,... | collective-permute-start | bytes 663560 | tf_op jit(solution)/shard_map/ppermute | solution.py:500
  9.5 1.5 %collective-permute-start.11 = (bf16[128,512]{1,0:T(8,128)(2,1)}, bf16[128,512]{1,0:T(8,128)(2,1)S(1)}, u32[]{:S(2)}, u32[]{:S(2)}) collective-permute-start(bf16[128,512]{1,0:T(8,128)(2,1)} %get-tuple-element.25), channel_id=1, source_target_pairs={{0,8},{1,9},{2,10},{3,11},{4,12},{5,13},{6,14},{7,15},{8,16},{9,17... | collective-permute-start | bytes 393224 | tf_op jit(solution)/shard_map/ppermute | solution.py:514
  11.0 0.0 collective-permute-start.3
  11.0 4.5 %collective-permute-start.1 = (bf16[128,256]{1,0:T(8,128)(2,1)}, bf16[128,256]{1,0:T(8,128)(2,1)S(1)}, u32[]{:S(2)}, u32[]{:S(2)}) collective-permute-start(bf16[128,256]{1,0:T(8,128)(2,1)} %get-tuple-element.17), channel_id=1, source_target_pairs={{0,4},{1,5},{2,6},{3,7},{8,12},{9,13},{10,14},{11,15},{16,20},{17,... | collective-permute-start | bytes 196616 | tf_op jit(solution)/shard_map/ppermute | solution.py:500
  15.5 1.3 %collective-permute-start.2 = (bf16[128,256]{1,0:T(8,128)(2,1)}, bf16[128,256]{1,0:T(8,128)(2,1)S(1)}, u32[]{:S(2)}, u32[]{:S(2)}) collective-permute-start(bf16[128,256]{1,0:T(8,128)(2,1)} %get-tuple-element.18), channel_id=1, source_target_pairs={{0,6},{1,7},{2,4},{3,5},{8,14},{9,15},{10,12},{11,13},{16,22},{17,... | collective-permute-start | bytes 196616 | tf_op jit(solution)/shard_map/ppermute | solution.py:500
  16.8 0.0 collective-permute-done.11.refs_0_
  16.8 2.5 %collective-permute-start.13 = (bf16[128,512]{1,0:T(8,128)(2,1)S(1)}, bf16[128,512]{1,0:T(8,128)(2,1)S(1)}, u32[]{:S(2)}, u32[]{:S(2)}) collective-permute-start(bf16[128,512]{1,0:T(8,128)(2,1)S(1)} %collective-permute-done.11.refs_0_), channel_id=1, source_target_pairs={{0,2},{1,3},{2,4},{3,5},{4,6},{5,7},{8,10},{9,11},{10,12},{11,13},... | collective-permute-start | bytes 393224 | tf_op jit(solution)/shard_map/ppermute | solution.py:500
  19.2 0.0 collective-permute-done.3.mine_x
  19.3 0.1 collective-permute-start.4
  19.3 0.0 collective-permute-done.1.far
  19.3 1.5 %collective-permute-start.10 = (bf16[144,1024]{1,0:T(8,128)(2,1)}, bf16[144,1024]{1,0:T(8,128)(2,1)S(1)}, u32[]{:S(2)}, u32[]{:S(2)}) collective-permute-start(bf16[144,1024]{1,0:T(8,128)(2,1)} %get-tuple-element.24), channel_id=1, source_target_pairs={{0,8},{1,9},{2,10},{3,11},{4,12},{5,13},{6,14},{7,15},{8,16},{9,17... | collective-permute-start | bytes 884744 | tf_op jit(solution)/shard_map/ppermute | solution.py:514
  20.9 0.0 collective-permute-done.2.beyond
  20.9 0.0 collective-permute-done.swap
  20.9 0.2 collective-permute-start.5
  21.1 0.4 collective-permute-start.6
  21.5 0.0 collective-permute-done.4.mine
  21.5 0.2 collective-permute-start.7
  21.6 0.7 %collective-permute-done.13.refs_2_ = bf16[128,512]{1,0:T(8,128)(2,1)S(1)} collective-permute-done((bf16[128,512]{1,0:T(8,128)(2,1)S(1)}, bf16[128,512]{1,0:T(8,128)(2,1)S(1)}, u32[]{:S(2)}, u32[]{:S(2)}) %collective-permute-start.13) | collective-permute-done | bytes 131104 | tf_op jit(solution)/shard_map/ppermute | solution.py:500
  22.4 0.0 collective-permute-start.12
  22.4 0.0 collective-permute-done.5.near_x
  22.4 0.7 %collective-permute-start.15 = (bf16[128,512]{1,0:T(8,128)(2,1)S(1)}, bf16[128,512]{1,0:T(8,128)(2,1)S(1)}, u32[]{:S(2)}, u32[]{:S(2)}) collective-permute-start(bf16[128,512]{1,0:T(8,128)(2,1)S(1)} %collective-permute-done.13.refs_2_), channel_id=1, source_target_pairs={{2,4},{3,5},{4,6},{5,7},{10,12},{11,13},{12,14},{13,15},{18,20},{1... | collective-permute-start | bytes 393224 | tf_op jit(solution)/shard_map/ppermute | solution.py:500
  23.0 0.0 collective-permute-done.6.far_x
  23.1 0.7 %collective-permute-start.18 = (bf16[128,512]{1,0:T(8,128)(2,1)S(1)}, bf16[128,512]{1,0:T(8,128)(2,1)S(1)}, u32[]{:S(2)}, u32[]{:S(2)}) collective-permute-start(bf16[128,512]{1,0:T(8,128)(2,1)S(1)} %collective-permute-done.13.refs_2_), channel_id=1, source_target_pairs={{2,6},{3,7},{10,14},{11,15},{18,22},{19,23},{26,30},{27,31}} | collective-permute-start | bytes 393224 | tf_op jit(solution)/shard_map/ppermute | solution.py:500
  23.7 0.0 collective-permute-done.7.beyond_x
  23.7 0.0 copy-done.2
  23.8 0.0 copy-done
  23.8 1.6 %attend_home.1 = (bf16[128,512]{1,0:T(8,128)(2,1)S(1)}, bf16[128,512]{1,0:T(8,128)(2,1)S(1)}) custom-call(bf16[1,128,2048]{2,1,0:T(8,128)(2,1)S(1)} %copy-done, bf16[144,768]{1,0:T(8,128)(2,1)S(1)} %collective-permute-done.swap, bf16[128,256]{1,0:T(8,128)(2,1)S(1)} %collective-permute-done.4.mine, bf16[128,256]{1,0:T(8,128)(2,1)S(1)} %collective-permute-done.3.mine_x, ...), custom_call_target="tpu_custom_call" | custom-call | flops 1900000000 | tf_op jit(solution)/shard_map/attend_home/pallas_call | solution.py:473
  25.4 8.1 %collective-permute-start.8 = (bf16[128,512]{1,0:T(8,128)(2,1)S(1)}, bf16[128,512]{1,0:T(8,128)(2,1)S(1)}, u32[]{:S(2)}, u32[]{:S(2)}) collective-permute-start(bf16[128,512]{1,0:T(8,128)(2,1)S(1)} %get-tuple-element.22), channel_id=1, source_target_pairs={{0,10},{1,11},{2,8},{3,9},{4,14},{5,15},{6,12},{7,13},{8,18},{9,19... | collective-permute-start | bytes 393224 | tf_op jit(solution)/shard_map/ppermute | solution.py:514
  33.5 0.0 collective-permute-done.10.packed
  33.5 1.5 %collective-permute-start.9 = (bf16[128,512]{1,0:T(8,128)(2,1)S(1)}, bf16[128,512]{1,0:T(8,128)(2,1)S(1)}, u32[]{:S(2)}, u32[]{:S(2)}) collective-permute-start(bf16[128,512]{1,0:T(8,128)(2,1)S(1)} %get-tuple-element.23), channel_id=1, source_target_pairs={{0,8},{1,9},{2,10},{3,11},{4,12},{5,13},{6,14},{7,15},{8,16},{9,17... | collective-permute-start | bytes 393224 | tf_op jit(solution)/shard_map/ppermute | solution.py:514
  35.0 0.0 collective-permute-done.15.refs_4_
  35.0 0.0 collective-permute-start.14
  35.0 0.0 collective-permute-done.18.refs_7_
  35.0 0.6 %collective-permute-start.16 = (bf16[128,256]{1,0:T(8,128)(2,1)S(1)}, bf16[128,256]{1,0:T(8,128)(2,1)S(1)}, u32[]{:S(2)}, u32[]{:S(2)}) collective-permute-start(bf16[128,256]{1,0:T(8,128)(2,1)S(1)} %get-tuple-element.30), channel_id=1, source_target_pairs={{0,1},{1,0},{2,3},{3,2},{4,5},{5,4},{6,7},{7,6},{8,9},{9,8},{10,11... | collective-permute-start | bytes 196616 | tf_op jit(solution)/shard_map/ppermute | solution.py:504
  35.6 0.0 collective-permute-done.12.refs_1_
  35.6 0.1 collective-permute-start.17
  35.7 0.6 %collective-permute-done.14.refs_3_ = bf16[128,512]{1,0:T(8,128)(2,1)S(1)} collective-permute-done((bf16[128,512]{1,0:T(8,128)(2,1)S(1)}, bf16[128,512]{1,0:T(8,128)(2,1)S(1)}, u32[]{:S(2)}, u32[]{:S(2)}) %collective-permute-start.14) | collective-permute-done | bytes 131104 | tf_op jit(solution)/shard_map/ppermute | solution.py:504
  36.3 0.1 collective-permute-start.19
  36.5 0.0 collective-permute-done.16.refs_5_
  36.5 0.4 collective-permute-start.20
  36.8 0.1 collective-permute-done.17.refs_6_
  36.9 0.7 %collective-permute-done.19.refs_8_ = bf16[128,256]{1,0:T(8,128)(2,1)S(1)} collective-permute-done((bf16[128,256]{1,0:T(8,128)(2,1)S(1)}, bf16[128,256]{1,0:T(8,128)(2,1)S(1)}, u32[]{:S(2)}, u32[]{:S(2)}) %collective-permute-start.19) | collective-permute-done | bytes 65568 | tf_op jit(solution)/shard_map/ppermute | solution.py:504
  37.6 0.2 collective-permute-done.20.refs_9_
  37.7 1.5 %attend_relayed.1 = bf16[128,1024]{1,0:T(8,128)(2,1)S(1)} custom-call(bf16[144,1024]{1,0:T(8,128)(2,1)S(1)} %collective-permute-done.10.packed, bf16[128,512]{1,0:T(8,128)(2,1)S(1)} %collective-permute-done.11.refs_0_, bf16[128,512]{1,0:T(8,128)(2,1)S(1)} %collective-permute-done.12.refs_1_, bf16[128,512]{1,0:T(8,128)(2,1)S(1)} %collective-permute-done.13.refs_2_, ...), custom_call_target="tpu_custom_call" | custom-call | tf_op jit(solution)/shard_map/attend_relayed/pallas_call | solution.py:488
  39.3 0.0 collective-permute-done.8
  39.3 0.9 %collective-permute-done.9 = bf16[128,512]{1,0:T(8,128)(2,1)S(1)} collective-permute-done((bf16[128,512]{1,0:T(8,128)(2,1)S(1)}, bf16[128,512]{1,0:T(8,128)(2,1)S(1)}, u32[]{:S(2)}, u32[]{:S(2)}) %collective-permute-start.9) | collective-permute-done | bytes 131104 | tf_op jit(solution)/shard_map/ppermute | solution.py:514
  40.2 0.9 %fusion = bf16[1,128,2048]{2,1,0:T(8,128)(2,1)} fusion(bf16[1,128,1024]{2,1,0:T(8,128)(2,1)S(1)} %bitcast.3, bf16[1,128,512]{2,1,0:T(8,128)(2,1)S(1)} %bitcast.5, bf16[1,128,512]{2,1,0:T(8,128)(2,1)S(1)} %bitcast.4, pred[]{:T(512)S(6)} %eq.3), kind=kLoop, calls=%fused_computation.2 | loop fusion | flops 3145728 | bytes 1048577 | tf_op jit(solution)/shard_map/jit(_where)/select_n | solution.py:562
  (7 shorter events, 0.0 us)
Async XLA Ops:
  0.0 23.7 %copy-start.2 = (s32[1,128]{1,0:T(1,128)S(1)}, s32[1,128]{1,0:T(1,128)}, u32[]{:S(2)}) copy-start(s32[1,128]{1,0:T(1,128)} %scored.3) | copy-start | bytes 1540
  0.0 23.8 %copy-start = (bf16[1,128,2048]{2,1,0:T(8,128)(2,1)S(1)}, bf16[1,128,2048]{2,1,0:T(8,128)(2,1)}, u32[]{:S(2)}) copy-start(bf16[1,128,2048]{2,1,0:T(8,128)(2,1)} %queries.3) | copy-start | bytes 1572868
  0.0 23.8 %copy-start.1 = (s32[1,1024]{1,0:T(1,128)S(1)}, s32[1,1024]{1,0:T(1,128)}, u32[]{:S(2)}) copy-start(s32[1,1024]{1,0:T(1,128)} %docs.3) | copy-start | bytes 12292
  6.4 14.5 %collective-permute-start = (bf16[144,768]{1,0:T(8,128)(2,1)}, bf16[144,768]{1,0:T(8,128)(2,1)S(1)}, u32[]{:S(2)}, u32[]{:S(2)}) collective-permute-start(bf16[144,768]{1,0:T(8,128)(2,1)} %get-tuple-element.16), channel_id=1, source_target_pairs={{0,2},{1,3},{2,0},{3,1},{4,6},{5,7},{6,4},{7,5},{8,10},{9,11},{10,... | collective-permute-start | bytes 663560 | tf_op jit(solution)/shard_map/ppermute | solution.py:500
  9.5 7.3 %collective-permute-start.11 = (bf16[128,512]{1,0:T(8,128)(2,1)}, bf16[128,512]{1,0:T(8,128)(2,1)S(1)}, u32[]{:S(2)}, u32[]{:S(2)}) collective-permute-start(bf16[128,512]{1,0:T(8,128)(2,1)} %get-tuple-element.25), channel_id=1, source_target_pairs={{0,8},{1,9},{2,10},{3,11},{4,12},{5,13},{6,14},{7,15},{8,16},{9,17... | collective-permute-start | bytes 393224 | tf_op jit(solution)/shard_map/ppermute | solution.py:514
  11.0 8.3 %collective-permute-start.3 = (bf16[128,256]{1,0:T(8,128)(2,1)}, bf16[128,256]{1,0:T(8,128)(2,1)S(1)}, u32[]{:S(2)}, u32[]{:S(2)}) collective-permute-start(bf16[128,256]{1,0:T(8,128)(2,1)} %get-tuple-element.17), channel_id=1, source_target_pairs={{0,1},{1,0},{2,3},{3,2},{4,5},{5,4},{6,7},{7,6},{8,9},{9,8},{10,11... | collective-permute-start | bytes 196616 | tf_op jit(solution)/shard_map/ppermute | solution.py:504
  11.0 8.4 %collective-permute-start.1 = (bf16[128,256]{1,0:T(8,128)(2,1)}, bf16[128,256]{1,0:T(8,128)(2,1)S(1)}, u32[]{:S(2)}, u32[]{:S(2)}) collective-permute-start(bf16[128,256]{1,0:T(8,128)(2,1)} %get-tuple-element.17), channel_id=1, source_target_pairs={{0,4},{1,5},{2,6},{3,7},{8,12},{9,13},{10,14},{11,15},{16,20},{17,... | collective-permute-start | bytes 196616 | tf_op jit(solution)/shard_map/ppermute | solution.py:500
  15.5 5.4 %collective-permute-start.2 = (bf16[128,256]{1,0:T(8,128)(2,1)}, bf16[128,256]{1,0:T(8,128)(2,1)S(1)}, u32[]{:S(2)}, u32[]{:S(2)}) collective-permute-start(bf16[128,256]{1,0:T(8,128)(2,1)} %get-tuple-element.18), channel_id=1, source_target_pairs={{0,6},{1,7},{2,4},{3,5},{8,14},{9,15},{10,12},{11,13},{16,22},{17,... | collective-permute-start | bytes 196616 | tf_op jit(solution)/shard_map/ppermute | solution.py:500
  16.8 5.6 %collective-permute-start.13 = (bf16[128,512]{1,0:T(8,128)(2,1)S(1)}, bf16[128,512]{1,0:T(8,128)(2,1)S(1)}, u32[]{:S(2)}, u32[]{:S(2)}) collective-permute-start(bf16[128,512]{1,0:T(8,128)(2,1)S(1)} %collective-permute-done.11.refs_0_), channel_id=1, source_target_pairs={{0,2},{1,3},{2,4},{3,5},{4,6},{5,7},{8,10},{9,11},{10,12},{11,13},... | collective-permute-start | bytes 393224 | tf_op jit(solution)/shard_map/ppermute | solution.py:500
  19.3 2.2 %collective-permute-start.4 = (bf16[128,256]{1,0:T(8,128)(2,1)S(1)}, bf16[128,256]{1,0:T(8,128)(2,1)S(1)}, u32[]{:S(2)}, u32[]{:S(2)}) collective-permute-start(bf16[128,256]{1,0:T(8,128)(2,1)S(1)} %collective-permute-done.3.mine_x), channel_id=1, source_target_pairs={{0,1},{1,0},{2,3},{3,2},{4,5},{5,4},{6,7},{7,6},{8,9},{9,8},{10,11... | collective-permute-start | bytes 196616 | tf_op jit(solution)/shard_map/ppermute | solution.py:504
  19.3 14.1 %collective-permute-start.10 = (bf16[144,1024]{1,0:T(8,128)(2,1)}, bf16[144,1024]{1,0:T(8,128)(2,1)S(1)}, u32[]{:S(2)}, u32[]{:S(2)}) collective-permute-start(bf16[144,1024]{1,0:T(8,128)(2,1)} %get-tuple-element.24), channel_id=1, source_target_pairs={{0,8},{1,9},{2,10},{3,11},{4,12},{5,13},{6,14},{7,15},{8,16},{9,17... | collective-permute-start | bytes 884744 | tf_op jit(solution)/shard_map/ppermute | solution.py:514
  20.9 1.5 %collective-permute-start.5 = (bf16[128,256]{1,0:T(8,128)(2,1)S(1)}, bf16[128,256]{1,0:T(8,128)(2,1)S(1)}, u32[]{:S(2)}, u32[]{:S(2)}) collective-permute-start(bf16[128,256]{1,0:T(8,128)(2,1)S(1)} %slice.15), channel_id=1, source_target_pairs={{0,1},{1,0},{2,3},{3,2},{4,5},{5,4},{6,7},{7,6},{8,9},{9,8},{10,11... | collective-permute-start | bytes 196616 | tf_op jit(solution)/shard_map/ppermute | solution.py:504
  21.1 1.9 %collective-permute-start.6 = (bf16[128,256]{1,0:T(8,128)(2,1)S(1)}, bf16[128,256]{1,0:T(8,128)(2,1)S(1)}, u32[]{:S(2)}, u32[]{:S(2)}) collective-permute-start(bf16[128,256]{1,0:T(8,128)(2,1)S(1)} %collective-permute-done.1.far), channel_id=1, source_target_pairs={{0,1},{1,0},{2,3},{3,2},{4,5},{5,4},{6,7},{7,6},{8,9},{9,8},{10,11... | collective-permute-start | bytes 196616 | tf_op jit(solution)/shard_map/ppermute | solution.py:504
  21.5 2.2 %collective-permute-start.7 = (bf16[128,256]{1,0:T(8,128)(2,1)S(1)}, bf16[128,256]{1,0:T(8,128)(2,1)S(1)}, u32[]{:S(2)}, u32[]{:S(2)}) collective-permute-start(bf16[128,256]{1,0:T(8,128)(2,1)S(1)} %collective-permute-done.2.beyond), channel_id=1, source_target_pairs={{0,1},{1,0},{2,3},{3,2},{4,5},{5,4},{6,7},{7,6},{8,9},{9,8},{10,11... | collective-permute-start | bytes 196616 | tf_op jit(solution)/shard_map/ppermute | solution.py:504
  22.4 13.2 %collective-permute-start.12 = (bf16[128,512]{1,0:T(8,128)(2,1)S(1)}, bf16[128,512]{1,0:T(8,128)(2,1)S(1)}, u32[]{:S(2)}, u32[]{:S(2)}) collective-permute-start(bf16[128,512]{1,0:T(8,128)(2,1)S(1)} %collective-permute-done.11.refs_0_), channel_id=1, source_target_pairs={{0,1},{1,0},{2,3},{3,2},{4,5},{5,4},{6,7},{7,6},{8,9},{9,8},{10,11... | collective-permute-start | bytes 393224 | tf_op jit(solution)/shard_map/ppermute | solution.py:504
  22.4 12.6 %collective-permute-start.15 = (bf16[128,512]{1,0:T(8,128)(2,1)S(1)}, bf16[128,512]{1,0:T(8,128)(2,1)S(1)}, u32[]{:S(2)}, u32[]{:S(2)}) collective-permute-start(bf16[128,512]{1,0:T(8,128)(2,1)S(1)} %collective-permute-done.13.refs_2_), channel_id=1, source_target_pairs={{2,4},{3,5},{4,6},{5,7},{10,12},{11,13},{12,14},{13,15},{18,20},{1... | collective-permute-start | bytes 393224 | tf_op jit(solution)/shard_map/ppermute | solution.py:500
  23.1 11.9 %collective-permute-start.18 = (bf16[128,512]{1,0:T(8,128)(2,1)S(1)}, bf16[128,512]{1,0:T(8,128)(2,1)S(1)}, u32[]{:S(2)}, u32[]{:S(2)}) collective-permute-start(bf16[128,512]{1,0:T(8,128)(2,1)S(1)} %collective-permute-done.13.refs_2_), channel_id=1, source_target_pairs={{2,6},{3,7},{10,14},{11,15},{18,22},{19,23},{26,30},{27,31}} | collective-permute-start | bytes 393224 | tf_op jit(solution)/shard_map/ppermute | solution.py:500
  25.4 13.9 %collective-permute-start.8 = (bf16[128,512]{1,0:T(8,128)(2,1)S(1)}, bf16[128,512]{1,0:T(8,128)(2,1)S(1)}, u32[]{:S(2)}, u32[]{:S(2)}) collective-permute-start(bf16[128,512]{1,0:T(8,128)(2,1)S(1)} %get-tuple-element.22), channel_id=1, source_target_pairs={{0,10},{1,11},{2,8},{3,9},{4,14},{5,15},{6,12},{7,13},{8,18},{9,19... | collective-permute-start | bytes 393224 | tf_op jit(solution)/shard_map/ppermute | solution.py:514
  33.5 6.7 %collective-permute-start.9 = (bf16[128,512]{1,0:T(8,128)(2,1)S(1)}, bf16[128,512]{1,0:T(8,128)(2,1)S(1)}, u32[]{:S(2)}, u32[]{:S(2)}) collective-permute-start(bf16[128,512]{1,0:T(8,128)(2,1)S(1)} %get-tuple-element.23), channel_id=1, source_target_pairs={{0,8},{1,9},{2,10},{3,11},{4,12},{5,13},{6,14},{7,15},{8,16},{9,17... | collective-permute-start | bytes 393224 | tf_op jit(solution)/shard_map/ppermute | solution.py:514
  35.0 1.3 %collective-permute-start.14 = (bf16[128,512]{1,0:T(8,128)(2,1)S(1)}, bf16[128,512]{1,0:T(8,128)(2,1)S(1)}, u32[]{:S(2)}, u32[]{:S(2)}) collective-permute-start(bf16[128,512]{1,0:T(8,128)(2,1)S(1)} %collective-permute-done.13.refs_2_), channel_id=1, source_target_pairs={{0,1},{1,0},{2,3},{3,2},{4,5},{5,4},{6,7},{7,6},{8,9},{9,8},{10,11... | collective-permute-start | bytes 393224 | tf_op jit(solution)/shard_map/ppermute | solution.py:504
  35.0 1.5 %collective-permute-start.16 = (bf16[128,256]{1,0:T(8,128)(2,1)S(1)}, bf16[128,256]{1,0:T(8,128)(2,1)S(1)}, u32[]{:S(2)}, u32[]{:S(2)}) collective-permute-start(bf16[128,256]{1,0:T(8,128)(2,1)S(1)} %get-tuple-element.30), channel_id=1, source_target_pairs={{0,1},{1,0},{2,3},{3,2},{4,5},{5,4},{6,7},{7,6},{8,9},{9,8},{10,11... | collective-permute-start | bytes 196616 | tf_op jit(solution)/shard_map/ppermute | solution.py:504
  35.6 1.3 %collective-permute-start.17 = (bf16[128,256]{1,0:T(8,128)(2,1)S(1)}, bf16[128,256]{1,0:T(8,128)(2,1)S(1)}, u32[]{:S(2)}, u32[]{:S(2)}) collective-permute-start(bf16[128,256]{1,0:T(8,128)(2,1)S(1)} %get-tuple-element.29), channel_id=1, source_target_pairs={{0,1},{1,0},{2,3},{3,2},{4,5},{5,4},{6,7},{7,6},{8,9},{9,8},{10,11... | collective-permute-start | bytes 196616 | tf_op jit(solution)/shard_map/ppermute | solution.py:504
  36.3 1.3 %collective-permute-start.19 = (bf16[128,256]{1,0:T(8,128)(2,1)S(1)}, bf16[128,256]{1,0:T(8,128)(2,1)S(1)}, u32[]{:S(2)}, u32[]{:S(2)}) collective-permute-start(bf16[128,256]{1,0:T(8,128)(2,1)S(1)} %get-tuple-element.28), channel_id=1, source_target_pairs={{0,1},{1,0},{2,3},{3,2},{4,5},{5,4},{6,7},{7,6},{8,9},{9,8},{10,11... | collective-permute-start | bytes 196616 | tf_op jit(solution)/shard_map/ppermute | solution.py:504
  36.5 1.3 %collective-permute-start.20 = (bf16[128,256]{1,0:T(8,128)(2,1)S(1)}, bf16[128,256]{1,0:T(8,128)(2,1)S(1)}, u32[]{:S(2)}, u32[]{:S(2)}) collective-permute-start(bf16[128,256]{1,0:T(8,128)(2,1)S(1)} %get-tuple-element.27), channel_id=1, source_target_pairs={{0,1},{1,0},{2,3},{3,2},{4,5},{5,4},{6,7},{7,6},{8,9},{9,8},{10,11... | collective-permute-start | bytes 196616 | tf_op jit(solution)/shard_map/ppermute | solution.py:504

commit v4 on v3

--- a/solution.py
+++ b/solution.py
@@ -176,9 +176,11 @@
     copies = []
     for i, (start, stop) in enumerate(cuts):
         span = pl.ds(start, stop - start)
-        copy = pltpu.make_async_copy(weight.at[0, span, :], store.at[span, :], weight_sems.at[i])
+        copies.append(
+            pltpu.make_async_copy(weight.at[0, span, :], store.at[span, :], weight_sems.at[i])
+        )
+    for copy in copies[:2]:
         copy.start()
-        copies.append(copy)
     for load in loads[1:]:
         load.start()
     results = [
@@ -194,6 +196,8 @@
         )
     ]
     loads[0].wait()
+    for copy in copies[2:3]:
+        copy.start()
     values = wide[...].astype(jnp.float32)
     scale = lax.rsqrt(jnp.mean(values * values, axis=-1, keepdims=True) + 1e-05)
     normed[...] = (values * scale).astype(jnp.bfloat16)
@@ -214,8 +218,10 @@
     )
     sine = jnp.where(lax.broadcasted_iota(jnp.int32, sine.shape, 1) < HEAD_SIZE // 2, -sine, sine)
     total = None
-    for copy, (start, stop) in zip(copies, cuts):
-        copy.wait()
+    for i, (start, stop) in enumerate(cuts):
+        copies[i].wait()
+        if i + 3 < len(copies):
+            copies[i + 3].start()
         part = jnp.dot(
             normed[:, start:stop], store[start:stop, :], preferred_element_type=jnp.float32
         )
@@ -246,7 +252,8 @@
 def project(hidden, weight, queries, docs, scored):
     rows, width = hidden.shape[1], hidden.shape[2]
     columns = weight.shape[2]
-    cuts = ((0, width // 2), (width // 2, width))
+    edges = [width * x // 16 for x in [0, 5, 10, 14, 16]]
+    cuts = tuple(zip(edges[:-1], edges[1:]))
     table = rotary_table(rows, docs.shape[1] // rows)
     hbm = pl.BlockSpec(memory_space=pltpu.HBM)
     shapes = [

time: 41.3 us -> 40.7 us (0.985)
  Pallas kernels: 9.48 us -> 8.91 us
    pallas_call x1, Pallas kernels: 6.36 us -> 5.77 us  [project(): pl.pallas_call(functools.partial(project_kernel, cuts), out_shape=[jax.Sh...]
where the time goes in v4:
time: 40.7 us; the launch traced here: 40.5 us
  starting transfers between devices  27.3 us (67%)
  Pallas kernels  8.91 us (22%)
  waiting for transfers between devices  3.18 us (8%)
  other arithmetic  0.89 us (2%)
    ppermute x6, starting transfers between devices, send(): return lax.ppermute(block, 'ctx', pairs)  12.7 us
    ppermute x4, starting transfers between devices, onward(): return lax.ppermute(block, ('phase', 'ctx'), route)  12.6 us
    pallas_call x1, Pallas kernels, project(): pl.pallas_call(functools.partial(project_kernel, cuts), out_shape=[jax.Sh...  5.77 us
    ppermute x11, starting transfers between devices, across(): lax.ppermute(block, 'ctx', [(i, i ^ 1) for i in range(lax.axis_size('ctx'...  1.98 us
    pallas_call x1, Pallas kernels, attend_home(): pl.pallas_call(attend_home_kernel, grid=(1,), out_shape=(out, out), in_sp...  1.6 us
    ppermute x11, waiting for transfers between devices, across(): lax.ppermute(block, 'ctx', [(i, i ^ 1) for i in range(lax.axis_size('ctx'...  1.56 us
    pallas_call x1, Pallas kernels, attend_relayed(): pl.pallas_call(attend_relayed_kernel, out_shape=jax.ShapeDtypeStruct((row...  1.53 us
    select_n x1, other arithmetic, paired(): return jnp.where(parity() == 1, crossed, straight)[None]  0.89 us
  transfers between devices with their start and end apart: 21, of which 6 were waited for; matrix products, arithmetic and copies ran while one was open for 0% of the time, Pallas kernels for 8%

profile of v4, /device:TPU:0, one launch (start us, length us, event | category | flops | bytes accessed | tf_op | source)
XLA Modules:
  0.0 40.5 jit_solution(9747304307252265215)
XLA Ops:
  0.0 5.8 %project.1 = (bf16[128,256]{1,0:T(8,128)(2,1)}, bf16[128,256]{1,0:T(8,128)(2,1)}, bf16[144,768]{1,0:T(8,128)(2,1)}, bf16[128,512]{1,0:T(8,128)(2,1)}, bf16[144,1024]{1,0:T(8,128)(2,1)}) custom-call(bf16[1,128,4096]{2,1,0:T(8,128)(2,1)} %hidden.1, bf16[1,4096,1024]{2,1,0:T(8,128)(2,1)} %weight.1, bf16[1,128,2048]{2,1,0:T(8,128)(2,1)} %queries.3, ...), custom_call_target="tpu_custom_call" | custom-call | tf_op jit(solution)/shard_map/project/pallas_call | solution.py:266
  5.8 3.1 %collective-permute-start = (bf16[144,768]{1,0:T(8,128)(2,1)}, bf16[144,768]{1,0:T(8,128)(2,1)S(1)}, u32[]{:S(2)}, u32[]{:S(2)}) collective-permute-start(bf16[144,768]{1,0:T(8,128)(2,1)} %get-tuple-element.16), channel_id=1, source_target_pairs={{0,2},{1,3},{2,0},{3,1},{4,6},{5,7},{6,4},{7,5},{8,10},{9,11},{10,... | collective-permute-start | bytes 663560 | tf_op jit(solution)/shard_map/ppermute | solution.py:507
  8.9 1.5 %collective-permute-start.11 = (bf16[128,512]{1,0:T(8,128)(2,1)}, bf16[128,512]{1,0:T(8,128)(2,1)S(1)}, u32[]{:S(2)}, u32[]{:S(2)}) collective-permute-start(bf16[128,512]{1,0:T(8,128)(2,1)} %get-tuple-element.25), channel_id=1, source_target_pairs={{0,8},{1,9},{2,10},{3,11},{4,12},{5,13},{6,14},{7,15},{8,16},{9,17... | collective-permute-start | bytes 393224 | tf_op jit(solution)/shard_map/ppermute | solution.py:521
  10.4 0.0 collective-permute-start.3
  10.4 4.5 %collective-permute-start.1 = (bf16[128,256]{1,0:T(8,128)(2,1)}, bf16[128,256]{1,0:T(8,128)(2,1)S(1)}, u32[]{:S(2)}, u32[]{:S(2)}) collective-permute-start(bf16[128,256]{1,0:T(8,128)(2,1)} %get-tuple-element.17), channel_id=1, source_target_pairs={{0,4},{1,5},{2,6},{3,7},{8,12},{9,13},{10,14},{11,15},{16,20},{17,... | collective-permute-start | bytes 196616 | tf_op jit(solution)/shard_map/ppermute | solution.py:507
  14.9 1.3 %collective-permute-start.2 = (bf16[128,256]{1,0:T(8,128)(2,1)}, bf16[128,256]{1,0:T(8,128)(2,1)S(1)}, u32[]{:S(2)}, u32[]{:S(2)}) collective-permute-start(bf16[128,256]{1,0:T(8,128)(2,1)} %get-tuple-element.18), channel_id=1, source_target_pairs={{0,6},{1,7},{2,4},{3,5},{8,14},{9,15},{10,12},{11,13},{16,22},{17,... | collective-permute-start | bytes 196616 | tf_op jit(solution)/shard_map/ppermute | solution.py:507
  16.2 0.0 collective-permute-done.11.refs_0_
  16.2 2.5 %collective-permute-start.13 = (bf16[128,512]{1,0:T(8,128)(2,1)S(1)}, bf16[128,512]{1,0:T(8,128)(2,1)S(1)}, u32[]{:S(2)}, u32[]{:S(2)}) collective-permute-start(bf16[128,512]{1,0:T(8,128)(2,1)S(1)} %collective-permute-done.11.refs_0_), channel_id=1, source_target_pairs={{0,2},{1,3},{2,4},{3,5},{4,6},{5,7},{8,10},{9,11},{10,12},{11,13},... | collective-permute-start | bytes 393224 | tf_op jit(solution)/shard_map/ppermute | solution.py:507
  18.7 0.0 collective-permute-done.3.mine_x
  18.7 0.1 collective-permute-start.4
  18.8 0.0 collective-permute-done.1.far
  18.8 1.5 %collective-permute-start.10 = (bf16[144,1024]{1,0:T(8,128)(2,1)}, bf16[144,1024]{1,0:T(8,128)(2,1)S(1)}, u32[]{:S(2)}, u32[]{:S(2)}) collective-permute-start(bf16[144,1024]{1,0:T(8,128)(2,1)} %get-tuple-element.24), channel_id=1, source_target_pairs={{0,8},{1,9},{2,10},{3,11},{4,12},{5,13},{6,14},{7,15},{8,16},{9,17... | collective-permute-start | bytes 884744 | tf_op jit(solution)/shard_map/ppermute | solution.py:521
  20.3 0.0 collective-permute-done.2.beyond
  20.3 0.0 collective-permute-done.swap
  20.3 0.2 collective-permute-start.5
  20.6 0.4 collective-permute-start.6
  20.9 0.0 collective-permute-done.4.mine
  20.9 0.2 collective-permute-start.7
  21.1 0.7 %collective-permute-done.13.refs_2_ = bf16[128,512]{1,0:T(8,128)(2,1)S(1)} collective-permute-done((bf16[128,512]{1,0:T(8,128)(2,1)S(1)}, bf16[128,512]{1,0:T(8,128)(2,1)S(1)}, u32[]{:S(2)}, u32[]{:S(2)}) %collective-permute-start.13) | collective-permute-done | bytes 131104 | tf_op jit(solution)/shard_map/ppermute | solution.py:507
  21.8 0.0 collective-permute-start.12
  21.8 0.0 collective-permute-done.5.near_x
  21.8 0.7 %collective-permute-start.15 = (bf16[128,512]{1,0:T(8,128)(2,1)S(1)}, bf16[128,512]{1,0:T(8,128)(2,1)S(1)}, u32[]{:S(2)}, u32[]{:S(2)}) collective-permute-start(bf16[128,512]{1,0:T(8,128)(2,1)S(1)} %collective-permute-done.13.refs_2_), channel_id=1, source_target_pairs={{2,4},{3,5},{4,6},{5,7},{10,12},{11,13},{12,14},{13,15},{18,20},{1... | collective-permute-start | bytes 393224 | tf_op jit(solution)/shard_map/ppermute | solution.py:507
  22.5 0.0 collective-permute-done.6.far_x
  22.5 0.7 %collective-permute-start.18 = (bf16[128,512]{1,0:T(8,128)(2,1)S(1)}, bf16[128,512]{1,0:T(8,128)(2,1)S(1)}, u32[]{:S(2)}, u32[]{:S(2)}) collective-permute-start(bf16[128,512]{1,0:T(8,128)(2,1)S(1)} %collective-permute-done.13.refs_2_), channel_id=1, source_target_pairs={{2,6},{3,7},{10,14},{11,15},{18,22},{19,23},{26,30},{27,31}} | collective-permute-start | bytes 393224 | tf_op jit(solution)/shard_map/ppermute | solution.py:507
  23.2 0.0 collective-permute-done.7.beyond_x
  23.2 0.0 copy-done.2
  23.2 0.0 copy-done
  23.2 1.6 %attend_home.1 = (bf16[128,512]{1,0:T(8,128)(2,1)S(1)}, bf16[128,512]{1,0:T(8,128)(2,1)S(1)}) custom-call(bf16[1,128,2048]{2,1,0:T(8,128)(2,1)S(1)} %copy-done, bf16[144,768]{1,0:T(8,128)(2,1)S(1)} %collective-permute-done.swap, bf16[128,256]{1,0:T(8,128)(2,1)S(1)} %collective-permute-done.4.mine, bf16[128,256]{1,0:T(8,128)(2,1)S(1)} %collective-permute-done.3.mine_x, ...), custom_call_target="tpu_custom_call" | custom-call | flops 1900000000 | tf_op jit(solution)/shard_map/attend_home/pallas_call | solution.py:480
  24.8 8.1 %collective-permute-start.8 = (bf16[128,512]{1,0:T(8,128)(2,1)S(1)}, bf16[128,512]{1,0:T(8,128)(2,1)S(1)}, u32[]{:S(2)}, u32[]{:S(2)}) collective-permute-start(bf16[128,512]{1,0:T(8,128)(2,1)S(1)} %get-tuple-element.22), channel_id=1, source_target_pairs={{0,10},{1,11},{2,8},{3,9},{4,14},{5,15},{6,12},{7,13},{8,18},{9,19... | collective-permute-start | bytes 393224 | tf_op jit(solution)/shard_map/ppermute | solution.py:521
  32.9 0.0 collective-permute-done.10.packed
  32.9 1.5 %collective-permute-start.9 = (bf16[128,512]{1,0:T(8,128)(2,1)S(1)}, bf16[128,512]{1,0:T(8,128)(2,1)S(1)}, u32[]{:S(2)}, u32[]{:S(2)}) collective-permute-start(bf16[128,512]{1,0:T(8,128)(2,1)S(1)} %get-tuple-element.23), channel_id=1, source_target_pairs={{0,8},{1,9},{2,10},{3,11},{4,12},{5,13},{6,14},{7,15},{8,16},{9,17... | collective-permute-start | bytes 393224 | tf_op jit(solution)/shard_map/ppermute | solution.py:521
  34.4 0.0 collective-permute-done.15.refs_4_
  34.4 0.0 collective-permute-start.14
  34.4 0.0 collective-permute-done.18.refs_7_
  34.4 0.6 %collective-permute-start.16 = (bf16[128,256]{1,0:T(8,128)(2,1)S(1)}, bf16[128,256]{1,0:T(8,128)(2,1)S(1)}, u32[]{:S(2)}, u32[]{:S(2)}) collective-permute-start(bf16[128,256]{1,0:T(8,128)(2,1)S(1)} %get-tuple-element.30), channel_id=1, source_target_pairs={{0,1},{1,0},{2,3},{3,2},{4,5},{5,4},{6,7},{7,6},{8,9},{9,8},{10,11... | collective-permute-start | bytes 196616 | tf_op jit(solution)/shard_map/ppermute | solution.py:511
  35.0 0.0 collective-permute-done.12.refs_1_
  35.0 0.1 collective-permute-start.17
  35.1 0.6 %collective-permute-done.14.refs_3_ = bf16[128,512]{1,0:T(8,128)(2,1)S(1)} collective-permute-done((bf16[128,512]{1,0:T(8,128)(2,1)S(1)}, bf16[128,512]{1,0:T(8,128)(2,1)S(1)}, u32[]{:S(2)}, u32[]{:S(2)}) %collective-permute-start.14) | collective-permute-done | bytes 131104 | tf_op jit(solution)/shard_map/ppermute | solution.py:511
  35.7 0.1 collective-permute-start.19
  35.9 0.0 collective-permute-done.16.refs_5_
  35.9 0.4 collective-permute-start.20
  36.3 0.1 collective-permute-done.17.refs_6_
  36.3 0.7 %collective-permute-done.19.refs_8_ = bf16[128,256]{1,0:T(8,128)(2,1)S(1)} collective-permute-done((bf16[128,256]{1,0:T(8,128)(2,1)S(1)}, bf16[128,256]{1,0:T(8,128)(2,1)S(1)}, u32[]{:S(2)}, u32[]{:S(2)}) %collective-permute-start.19) | collective-permute-done | bytes 65568 | tf_op jit(solution)/shard_map/ppermute | solution.py:511
  37.0 0.2 collective-permute-done.20.refs_9_
  37.2 1.5 %attend_relayed.1 = bf16[128,1024]{1,0:T(8,128)(2,1)S(1)} custom-call(bf16[144,1024]{1,0:T(8,128)(2,1)S(1)} %collective-permute-done.10.packed, bf16[128,512]{1,0:T(8,128)(2,1)S(1)} %collective-permute-done.11.refs_0_, bf16[128,512]{1,0:T(8,128)(2,1)S(1)} %collective-permute-done.12.refs_1_, bf16[128,512]{1,0:T(8,128)(2,1)S(1)} %collective-permute-done.13.refs_2_, ...), custom_call_target="tpu_custom_call" | custom-call | tf_op jit(solution)/shard_map/attend_relayed/pallas_call | solution.py:495
  38.7 0.0 collective-permute-done.8
  38.7 0.9 %collective-permute-done.9 = bf16[128,512]{1,0:T(8,128)(2,1)S(1)} collective-permute-done((bf16[128,512]{1,0:T(8,128)(2,1)S(1)}, bf16[128,512]{1,0:T(8,128)(2,1)S(1)}, u32[]{:S(2)}, u32[]{:S(2)}) %collective-permute-start.9) | collective-permute-done | bytes 131104 | tf_op jit(solution)/shard_map/ppermute | solution.py:521
  39.6 0.9 %fusion = bf16[1,128,2048]{2,1,0:T(8,128)(2,1)} fusion(bf16[1,128,1024]{2,1,0:T(8,128)(2,1)S(1)} %bitcast.3, bf16[1,128,512]{2,1,0:T(8,128)(2,1)S(1)} %bitcast.5, bf16[1,128,512]{2,1,0:T(8,128)(2,1)S(1)} %bitcast.4, pred[]{:T(512)S(6)} %eq.3), kind=kLoop, calls=%fused_computation.2 | loop fusion | flops 3145728 | bytes 1048577 | tf_op jit(solution)/shard_map/jit(_where)/select_n | solution.py:569
  (7 shorter events, 0.0 us)
Async XLA Ops:
  0.0 23.2 %copy-start.2 = (s32[1,128]{1,0:T(1,128)S(1)}, s32[1,128]{1,0:T(1,128)}, u32[]{:S(2)}) copy-start(s32[1,128]{1,0:T(1,128)} %scored.3) | copy-start | bytes 1540
  0.0 23.2 %copy-start = (bf16[1,128,2048]{2,1,0:T(8,128)(2,1)S(1)}, bf16[1,128,2048]{2,1,0:T(8,128)(2,1)}, u32[]{:S(2)}) copy-start(bf16[1,128,2048]{2,1,0:T(8,128)(2,1)} %queries.3) | copy-start | bytes 1572868
  0.0 23.2 %copy-start.1 = (s32[1,1024]{1,0:T(1,128)S(1)}, s32[1,1024]{1,0:T(1,128)}, u32[]{:S(2)}) copy-start(s32[1,1024]{1,0:T(1,128)} %docs.3) | copy-start | bytes 12292
  5.8 14.5 %collective-permute-start = (bf16[144,768]{1,0:T(8,128)(2,1)}, bf16[144,768]{1,0:T(8,128)(2,1)S(1)}, u32[]{:S(2)}, u32[]{:S(2)}) collective-permute-start(bf16[144,768]{1,0:T(8,128)(2,1)} %get-tuple-element.16), channel_id=1, source_target_pairs={{0,2},{1,3},{2,0},{3,1},{4,6},{5,7},{6,4},{7,5},{8,10},{9,11},{10,... | collective-permute-start | bytes 663560 | tf_op jit(solution)/shard_map/ppermute | solution.py:507
  8.9 7.3 %collective-permute-start.11 = (bf16[128,512]{1,0:T(8,128)(2,1)}, bf16[128,512]{1,0:T(8,128)(2,1)S(1)}, u32[]{:S(2)}, u32[]{:S(2)}) collective-permute-start(bf16[128,512]{1,0:T(8,128)(2,1)} %get-tuple-element.25), channel_id=1, source_target_pairs={{0,8},{1,9},{2,10},{3,11},{4,12},{5,13},{6,14},{7,15},{8,16},{9,17... | collective-permute-start | bytes 393224 | tf_op jit(solution)/shard_map/ppermute | solution.py:521
  10.4 8.3 %collective-permute-start.3 = (bf16[128,256]{1,0:T(8,128)(2,1)}, bf16[128,256]{1,0:T(8,128)(2,1)S(1)}, u32[]{:S(2)}, u32[]{:S(2)}) collective-permute-start(bf16[128,256]{1,0:T(8,128)(2,1)} %get-tuple-element.17), channel_id=1, source_target_pairs={{0,1},{1,0},{2,3},{3,2},{4,5},{5,4},{6,7},{7,6},{8,9},{9,8},{10,11... | collective-permute-start | bytes 196616 | tf_op jit(solution)/shard_map/ppermute | solution.py:511
  10.4 8.4 %collective-permute-start.1 = (bf16[128,256]{1,0:T(8,128)(2,1)}, bf16[128,256]{1,0:T(8,128)(2,1)S(1)}, u32[]{:S(2)}, u32[]{:S(2)}) collective-permute-start(bf16[128,256]{1,0:T(8,128)(2,1)} %get-tuple-element.17), channel_id=1, source_target_pairs={{0,4},{1,5},{2,6},{3,7},{8,12},{9,13},{10,14},{11,15},{16,20},{17,... | collective-permute-start | bytes 196616 | tf_op jit(solution)/shard_map/ppermute | solution.py:507
  14.9 5.4 %collective-permute-start.2 = (bf16[128,256]{1,0:T(8,128)(2,1)}, bf16[128,256]{1,0:T(8,128)(2,1)S(1)}, u32[]{:S(2)}, u32[]{:S(2)}) collective-permute-start(bf16[128,256]{1,0:T(8,128)(2,1)} %get-tuple-element.18), channel_id=1, source_target_pairs={{0,6},{1,7},{2,4},{3,5},{8,14},{9,15},{10,12},{11,13},{16,22},{17,... | collective-permute-start | bytes 196616 | tf_op jit(solution)/shard_map/ppermute | solution.py:507
  16.2 5.6 %collective-permute-start.13 = (bf16[128,512]{1,0:T(8,128)(2,1)S(1)}, bf16[128,512]{1,0:T(8,128)(2,1)S(1)}, u32[]{:S(2)}, u32[]{:S(2)}) collective-permute-start(bf16[128,512]{1,0:T(8,128)(2,1)S(1)} %collective-permute-done.11.refs_0_), channel_id=1, source_target_pairs={{0,2},{1,3},{2,4},{3,5},{4,6},{5,7},{8,10},{9,11},{10,12},{11,13},... | collective-permute-start | bytes 393224 | tf_op jit(solution)/shard_map/ppermute | solution.py:507
  18.7 2.2 %collective-permute-start.4 = (bf16[128,256]{1,0:T(8,128)(2,1)S(1)}, bf16[128,256]{1,0:T(8,128)(2,1)S(1)}, u32[]{:S(2)}, u32[]{:S(2)}) collective-permute-start(bf16[128,256]{1,0:T(8,128)(2,1)S(1)} %collective-permute-done.3.mine_x), channel_id=1, source_target_pairs={{0,1},{1,0},{2,3},{3,2},{4,5},{5,4},{6,7},{7,6},{8,9},{9,8},{10,11... | collective-permute-start | bytes 196616 | tf_op jit(solution)/shard_map/ppermute | solution.py:511
  18.8 14.1 %collective-permute-start.10 = (bf16[144,1024]{1,0:T(8,128)(2,1)}, bf16[144,1024]{1,0:T(8,128)(2,1)S(1)}, u32[]{:S(2)}, u32[]{:S(2)}) collective-permute-start(bf16[144,1024]{1,0:T(8,128)(2,1)} %get-tuple-element.24), channel_id=1, source_target_pairs={{0,8},{1,9},{2,10},{3,11},{4,12},{5,13},{6,14},{7,15},{8,16},{9,17... | collective-permute-start | bytes 884744 | tf_op jit(solution)/shard_map/ppermute | solution.py:521
  20.3 1.5 %collective-permute-start.5 = (bf16[128,256]{1,0:T(8,128)(2,1)S(1)}, bf16[128,256]{1,0:T(8,128)(2,1)S(1)}, u32[]{:S(2)}, u32[]{:S(2)}) collective-permute-start(bf16[128,256]{1,0:T(8,128)(2,1)S(1)} %slice.15), channel_id=1, source_target_pairs={{0,1},{1,0},{2,3},{3,2},{4,5},{5,4},{6,7},{7,6},{8,9},{9,8},{10,11... | collective-permute-start | bytes 196616 | tf_op jit(solution)/shard_map/ppermute | solution.py:511
  20.6 1.9 %collective-permute-start.6 = (bf16[128,256]{1,0:T(8,128)(2,1)S(1)}, bf16[128,256]{1,0:T(8,128)(2,1)S(1)}, u32[]{:S(2)}, u32[]{:S(2)}) collective-permute-start(bf16[128,256]{1,0:T(8,128)(2,1)S(1)} %collective-permute-done.1.far), channel_id=1, source_target_pairs={{0,1},{1,0},{2,3},{3,2},{4,5},{5,4},{6,7},{7,6},{8,9},{9,8},{10,11... | collective-permute-start | bytes 196616 | tf_op jit(solution)/shard_map/ppermute | solution.py:511
  20.9 2.2 %collective-permute-start.7 = (bf16[128,256]{1,0:T(8,128)(2,1)S(1)}, bf16[128,256]{1,0:T(8,128)(2,1)S(1)}, u32[]{:S(2)}, u32[]{:S(2)}) collective-permute-start(bf16[128,256]{1,0:T(8,128)(2,1)S(1)} %collective-permute-done.2.beyond), channel_id=1, source_target_pairs={{0,1},{1,0},{2,3},{3,2},{4,5},{5,4},{6,7},{7,6},{8,9},{9,8},{10,11... | collective-permute-start | bytes 196616 | tf_op jit(solution)/shard_map/ppermute | solution.py:511
  21.8 13.2 %collective-permute-start.12 = (bf16[128,512]{1,0:T(8,128)(2,1)S(1)}, bf16[128,512]{1,0:T(8,128)(2,1)S(1)}, u32[]{:S(2)}, u32[]{:S(2)}) collective-permute-start(bf16[128,512]{1,0:T(8,128)(2,1)S(1)} %collective-permute-done.11.refs_0_), channel_id=1, source_target_pairs={{0,1},{1,0},{2,3},{3,2},{4,5},{5,4},{6,7},{7,6},{8,9},{9,8},{10,11... | collective-permute-start | bytes 393224 | tf_op jit(solution)/shard_map/ppermute | solution.py:511
  21.8 12.6 %collective-permute-start.15 = (bf16[128,512]{1,0:T(8,128)(2,1)S(1)}, bf16[128,512]{1,0:T(8,128)(2,1)S(1)}, u32[]{:S(2)}, u32[]{:S(2)}) collective-permute-start(bf16[128,512]{1,0:T(8,128)(2,1)S(1)} %collective-permute-done.13.refs_2_), channel_id=1, source_target_pairs={{2,4},{3,5},{4,6},{5,7},{10,12},{11,13},{12,14},{13,15},{18,20},{1... | collective-permute-start | bytes 393224 | tf_op jit(solution)/shard_map/ppermute | solution.py:507
  22.5 11.9 %collective-permute-start.18 = (bf16[128,512]{1,0:T(8,128)(2,1)S(1)}, bf16[128,512]{1,0:T(8,128)(2,1)S(1)}, u32[]{:S(2)}, u32[]{:S(2)}) collective-permute-start(bf16[128,512]{1,0:T(8,128)(2,1)S(1)} %collective-permute-done.13.refs_2_), channel_id=1, source_target_pairs={{2,6},{3,7},{10,14},{11,15},{18,22},{19,23},{26,30},{27,31}} | collective-permute-start | bytes 393224 | tf_op jit(solution)/shard_map/ppermute | solution.py:507
  24.8 13.9 %collective-permute-start.8 = (bf16[128,512]{1,0:T(8,128)(2,1)S(1)}, bf16[128,512]{1,0:T(8,128)(2,1)S(1)}, u32[]{:S(2)}, u32[]{:S(2)}) collective-permute-start(bf16[128,512]{1,0:T(8,128)(2,1)S(1)} %get-tuple-element.22), channel_id=1, source_target_pairs={{0,10},{1,11},{2,8},{3,9},{4,14},{5,15},{6,12},{7,13},{8,18},{9,19... | collective-permute-start | bytes 393224 | tf_op jit(solution)/shard_map/ppermute | solution.py:521
  32.9 6.7 %collective-permute-start.9 = (bf16[128,512]{1,0:T(8,128)(2,1)S(1)}, bf16[128,512]{1,0:T(8,128)(2,1)S(1)}, u32[]{:S(2)}, u32[]{:S(2)}) collective-permute-start(bf16[128,512]{1,0:T(8,128)(2,1)S(1)} %get-tuple-element.23), channel_id=1, source_target_pairs={{0,8},{1,9},{2,10},{3,11},{4,12},{5,13},{6,14},{7,15},{8,16},{9,17... | collective-permute-start | bytes 393224 | tf_op jit(solution)/shard_map/ppermute | solution.py:521
  34.4 1.3 %collective-permute-start.14 = (bf16[128,512]{1,0:T(8,128)(2,1)S(1)}, bf16[128,512]{1,0:T(8,128)(2,1)S(1)}, u32[]{:S(2)}, u32[]{:S(2)}) collective-permute-start(bf16[128,512]{1,0:T(8,128)(2,1)S(1)} %collective-permute-done.13.refs_2_), channel_id=1, source_target_pairs={{0,1},{1,0},{2,3},{3,2},{4,5},{5,4},{6,7},{7,6},{8,9},{9,8},{10,11... | collective-permute-start | bytes 393224 | tf_op jit(solution)/shard_map/ppermute | solution.py:511
  34.4 1.5 %collective-permute-start.16 = (bf16[128,256]{1,0:T(8,128)(2,1)S(1)}, bf16[128,256]{1,0:T(8,128)(2,1)S(1)}, u32[]{:S(2)}, u32[]{:S(2)}) collective-permute-start(bf16[128,256]{1,0:T(8,128)(2,1)S(1)} %get-tuple-element.30), channel_id=1, source_target_pairs={{0,1},{1,0},{2,3},{3,2},{4,5},{5,4},{6,7},{7,6},{8,9},{9,8},{10,11... | collective-permute-start | bytes 196616 | tf_op jit(solution)/shard_map/ppermute | solution.py:511
  35.0 1.3 %collective-permute-start.17 = (bf16[128,256]{1,0:T(8,128)(2,1)S(1)}, bf16[128,256]{1,0:T(8,128)(2,1)S(1)}, u32[]{:S(2)}, u32[]{:S(2)}) collective-permute-start(bf16[128,256]{1,0:T(8,128)(2,1)S(1)} %get-tuple-element.29), channel_id=1, source_target_pairs={{0,1},{1,0},{2,3},{3,2},{4,5},{5,4},{6,7},{7,6},{8,9},{9,8},{10,11... | collective-permute-start | bytes 196616 | tf_op jit(solution)/shard_map/ppermute | solution.py:511
  35.7 1.3 %collective-permute-start.19 = (bf16[128,256]{1,0:T(8,128)(2,1)S(1)}, bf16[128,256]{1,0:T(8,128)(2,1)S(1)}, u32[]{:S(2)}, u32[]{:S(2)}) collective-permute-start(bf16[128,256]{1,0:T(8,128)(2,1)S(1)} %get-tuple-element.28), channel_id=1, source_target_pairs={{0,1},{1,0},{2,3},{3,2},{4,5},{5,4},{6,7},{7,6},{8,9},{9,8},{10,11... | collective-permute-start | bytes 196616 | tf_op jit(solution)/shard_map/ppermute | solution.py:511
  35.9 1.3 %collective-permute-start.20 = (bf16[128,256]{1,0:T(8,128)(2,1)S(1)}, bf16[128,256]{1,0:T(8,128)(2,1)S(1)}, u32[]{:S(2)}, u32[]{:S(2)}) collective-permute-start(bf16[128,256]{1,0:T(8,128)(2,1)S(1)} %get-tuple-element.27), channel_id=1, source_target_pairs={{0,1},{1,0},{2,3},{3,2},{4,5},{5,4},{6,7},{7,6},{8,9},{9,8},{10,11... | collective-permute-start | bytes 196616 | tf_op jit(solution)/shard_map/ppermute | solution.py:511

commit v5 on v4

--- a/solution.py
+++ b/solution.py
@@ -358,8 +358,8 @@
                     part = result[i * rows : (i + 1) * rows] * kept_rows
                     put(at[i], part.astype(jnp.bfloat16))
 
-    pl.when(chip >= 2)(lambda: heads(4))
-    pl.when(chip < 2)(lambda: heads(2))
+    for last in range(4):
+        pl.when(chip == last)(functools.partial(heads, last + 1))
 
 
 def attend_home_kernel(
@@ -564,9 +564,9 @@
         x for block in (away_2, away_3) for x in (block, *across_halves(block))
     ]
     last = attend_relayed(packed, away)
+    crossed = jnp.concatenate([partners, own, last], axis=1)
     straight = jnp.concatenate([own, partners, last], axis=1)
-    crossed = jnp.concatenate([partners, own, last], axis=1)
-    return jnp.where(parity() == 1, crossed, straight)[None]
+    return jnp.where(parity() == 0, straight, crossed)[None]
 
 
 def solution(mesh):

time: 40.7 us -> 39.4 us (0.968)
  starting transfers between devices: 27.3 us -> 24 us
  waiting for transfers between devices: 3.18 us -> 5.6 us
  Pallas kernels: 8.91 us -> 8.36 us
    ppermute x4, starting transfers between devices: 12.6 us -> 9.33 us  [onward(): return lax.ppermute(block, ('phase', 'ctx'), route)]
    ppermute x4, waiting for transfers between devices: 0.88 us -> 3.3 us  [onward(): return lax.ppermute(block, ('phase', 'ctx'), route)]
    pallas_call x1, Pallas kernels: 1.53 us -> 0.99 us  [attend_relayed(): pl.pallas_call(attend_relayed_kernel, out_shape=jax.ShapeDtypeStruct((row...]
  transfers between devices with their start and end apart: 21 -> 21, of which waited for: 6 -> 6; matrix products, arithmetic and copies ran while one was open for 0% -> 0% of each run, Pallas kernels for 8% -> 7%
where the time goes in v5:
time: 39.4 us; the launch traced here: 39.1 us
  starting transfers between devices  24 us (61%)
  Pallas kernels  8.36 us (21%)
  waiting for transfers between devices  5.6 us (14%)
  other arithmetic  0.9 us (2%)
    ppermute x6, starting transfers between devices, send(): return lax.ppermute(block, 'ctx', pairs)  12.7 us
    ppermute x4, starting transfers between devices, onward(): return lax.ppermute(block, ('phase', 'ctx'), route)  9.33 us
    pallas_call x1, Pallas kernels, project(): pl.pallas_call(functools.partial(project_kernel, cuts), out_shape=[jax.Sh...  5.77 us
    ppermute x4, waiting for transfers between devices, onward(): return lax.ppermute(block, ('phase', 'ctx'), route)  3.3 us
    ppermute x11, starting transfers between devices, across(): lax.ppermute(block, 'ctx', [(i, i ^ 1) for i in range(lax.axis_size('ctx'...  1.98 us
    pallas_call x1, Pallas kernels, attend_home(): pl.pallas_call(attend_home_kernel, grid=(1,), out_shape=(out, out), in_sp...  1.6 us
    ppermute x11, waiting for transfers between devices, across(): lax.ppermute(block, 'ctx', [(i, i ^ 1) for i in range(lax.axis_size('ctx'...  1.56 us
    pallas_call x1, Pallas kernels, attend_relayed(): pl.pallas_call(attend_relayed_kernel, out_shape=jax.ShapeDtypeStruct((row...  0.99 us
  transfers between devices with their start and end apart: 21, of which 6 were waited for; matrix products, arithmetic and copies ran while one was open for 0% of the time, Pallas kernels for 7%

profile of v5, /device:TPU:0, one launch (start us, length us, event | category | flops | bytes accessed | tf_op | source)
XLA Modules:
  0.0 39.1 jit_solution(9934146953567762352)
XLA Ops:
  0.0 5.8 %project.1 = (bf16[128,256]{1,0:T(8,128)(2,1)}, bf16[128,256]{1,0:T(8,128)(2,1)}, bf16[144,768]{1,0:T(8,128)(2,1)}, bf16[128,512]{1,0:T(8,128)(2,1)}, bf16[144,1024]{1,0:T(8,128)(2,1)}) custom-call(bf16[1,128,4096]{2,1,0:T(8,128)(2,1)} %hidden.1, bf16[1,4096,1024]{2,1,0:T(8,128)(2,1)} %weight.1, bf16[1,128,2048]{2,1,0:T(8,128)(2,1)} %queries.3, ...), custom_call_target="tpu_custom_call" | custom-call | tf_op jit(solution)/shard_map/project/pallas_call | solution.py:266
  5.8 3.1 %collective-permute-start = (bf16[144,768]{1,0:T(8,128)(2,1)}, bf16[144,768]{1,0:T(8,128)(2,1)S(1)}, u32[]{:S(2)}, u32[]{:S(2)}) collective-permute-start(bf16[144,768]{1,0:T(8,128)(2,1)} %get-tuple-element.16), channel_id=1, source_target_pairs={{0,2},{1,3},{2,0},{3,1},{4,6},{5,7},{6,4},{7,5},{8,10},{9,11},{10,... | collective-permute-start | bytes 663560 | tf_op jit(solution)/shard_map/ppermute | solution.py:507
  8.9 1.5 %collective-permute-start.11 = (bf16[128,512]{1,0:T(8,128)(2,1)}, bf16[128,512]{1,0:T(8,128)(2,1)S(1)}, u32[]{:S(2)}, u32[]{:S(2)}) collective-permute-start(bf16[128,512]{1,0:T(8,128)(2,1)} %get-tuple-element.25), channel_id=1, source_target_pairs={{0,8},{1,9},{2,10},{3,11},{4,12},{5,13},{6,14},{7,15},{8,16},{9,17... | collective-permute-start | bytes 393224 | tf_op jit(solution)/shard_map/ppermute | solution.py:521
  10.4 0.0 collective-permute-start.3
  10.4 4.5 %collective-permute-start.1 = (bf16[128,256]{1,0:T(8,128)(2,1)}, bf16[128,256]{1,0:T(8,128)(2,1)S(1)}, u32[]{:S(2)}, u32[]{:S(2)}) collective-permute-start(bf16[128,256]{1,0:T(8,128)(2,1)} %get-tuple-element.17), channel_id=1, source_target_pairs={{0,4},{1,5},{2,6},{3,7},{8,12},{9,13},{10,14},{11,15},{16,20},{17,... | collective-permute-start | bytes 196616 | tf_op jit(solution)/shard_map/ppermute | solution.py:507
  14.9 1.3 %collective-permute-start.2 = (bf16[128,256]{1,0:T(8,128)(2,1)}, bf16[128,256]{1,0:T(8,128)(2,1)S(1)}, u32[]{:S(2)}, u32[]{:S(2)}) collective-permute-start(bf16[128,256]{1,0:T(8,128)(2,1)} %get-tuple-element.18), channel_id=1, source_target_pairs={{0,6},{1,7},{2,4},{3,5},{8,14},{9,15},{10,12},{11,13},{16,22},{17,... | collective-permute-start | bytes 196616 | tf_op jit(solution)/shard_map/ppermute | solution.py:507
  16.2 0.0 collective-permute-done.11.refs_0_
  16.2 2.5 %collective-permute-start.13 = (bf16[128,512]{1,0:T(8,128)(2,1)S(1)}, bf16[128,512]{1,0:T(8,128)(2,1)S(1)}, u32[]{:S(2)}, u32[]{:S(2)}) collective-permute-start(bf16[128,512]{1,0:T(8,128)(2,1)S(1)} %collective-permute-done.11.refs_0_), channel_id=1, source_target_pairs={{0,2},{1,3},{2,4},{3,5},{4,6},{5,7},{8,10},{9,11},{10,12},{11,13},... | collective-permute-start | bytes 393224 | tf_op jit(solution)/shard_map/ppermute | solution.py:507
  18.7 0.0 collective-permute-done.3.mine_x
  18.7 0.1 collective-permute-start.4
  18.8 0.0 collective-permute-done.1.far
  18.8 1.5 %collective-permute-start.10 = (bf16[144,1024]{1,0:T(8,128)(2,1)}, bf16[144,1024]{1,0:T(8,128)(2,1)S(1)}, u32[]{:S(2)}, u32[]{:S(2)}) collective-permute-start(bf16[144,1024]{1,0:T(8,128)(2,1)} %get-tuple-element.24), channel_id=1, source_target_pairs={{0,8},{1,9},{2,10},{3,11},{4,12},{5,13},{6,14},{7,15},{8,16},{9,17... | collective-permute-start | bytes 884744 | tf_op jit(solution)/shard_map/ppermute | solution.py:521
  20.3 0.0 collective-permute-done.2.beyond
  20.3 0.0 collective-permute-done.swap
  20.3 0.2 collective-permute-start.5
  20.6 0.4 collective-permute-start.6
  20.9 0.0 collective-permute-done.4.mine
  20.9 0.2 collective-permute-start.7
  21.1 0.7 %collective-permute-done.13.refs_2_ = bf16[128,512]{1,0:T(8,128)(2,1)S(1)} collective-permute-done((bf16[128,512]{1,0:T(8,128)(2,1)S(1)}, bf16[128,512]{1,0:T(8,128)(2,1)S(1)}, u32[]{:S(2)}, u32[]{:S(2)}) %collective-permute-start.13) | collective-permute-done | bytes 131104 | tf_op jit(solution)/shard_map/ppermute | solution.py:507
  21.8 0.0 collective-permute-start.12
  21.8 0.0 collective-permute-done.5.near_x
  21.8 0.7 %collective-permute-start.15 = (bf16[128,512]{1,0:T(8,128)(2,1)S(1)}, bf16[128,512]{1,0:T(8,128)(2,1)S(1)}, u32[]{:S(2)}, u32[]{:S(2)}) collective-permute-start(bf16[128,512]{1,0:T(8,128)(2,1)S(1)} %collective-permute-done.13.refs_2_), channel_id=1, source_target_pairs={{2,4},{3,5},{4,6},{5,7},{10,12},{11,13},{12,14},{13,15},{18,20},{1... | collective-permute-start | bytes 393224 | tf_op jit(solution)/shard_map/ppermute | solution.py:507
  22.5 0.0 collective-permute-done.6.far_x
  22.5 0.7 %collective-permute-start.18 = (bf16[128,512]{1,0:T(8,128)(2,1)S(1)}, bf16[128,512]{1,0:T(8,128)(2,1)S(1)}, u32[]{:S(2)}, u32[]{:S(2)}) collective-permute-start(bf16[128,512]{1,0:T(8,128)(2,1)S(1)} %collective-permute-done.13.refs_2_), channel_id=1, source_target_pairs={{2,6},{3,7},{10,14},{11,15},{18,22},{19,23},{26,30},{27,31}} | collective-permute-start | bytes 393224 | tf_op jit(solution)/shard_map/ppermute | solution.py:507
  23.2 0.0 collective-permute-done.7.beyond_x
  23.2 0.0 copy-done.2
  23.2 0.0 copy-done
  23.2 1.6 %attend_home.1 = (bf16[128,512]{1,0:T(8,128)(2,1)S(1)}, bf16[128,512]{1,0:T(8,128)(2,1)S(1)}) custom-call(bf16[1,128,2048]{2,1,0:T(8,128)(2,1)S(1)} %copy-done, bf16[144,768]{1,0:T(8,128)(2,1)S(1)} %collective-permute-done.swap, bf16[128,256]{1,0:T(8,128)(2,1)S(1)} %collective-permute-done.4.mine, bf16[128,256]{1,0:T(8,128)(2,1)S(1)} %collective-permute-done.3.mine_x, ...), custom_call_target="tpu_custom_call" | custom-call | flops 1900000000 | tf_op jit(solution)/shard_map/attend_home/pallas_call | solution.py:480
  24.8 1.6 %collective-permute-start.8 = (bf16[128,512]{1,0:T(8,128)(2,1)S(1)}, bf16[128,512]{1,0:T(8,128)(2,1)S(1)}, u32[]{:S(2)}, u32[]{:S(2)}) collective-permute-start(bf16[128,512]{1,0:T(8,128)(2,1)S(1)} %get-tuple-element.22), channel_id=1, source_target_pairs={{0,8},{1,9},{2,10},{3,11},{4,12},{5,13},{6,14},{7,15},{8,16},{9,17... | collective-permute-start | bytes 393224 | tf_op jit(solution)/shard_map/ppermute | solution.py:521
  26.4 3.3 %collective-permute-done.10.packed = bf16[144,1024]{1,0:T(8,128)(2,1)S(1)} collective-permute-done((bf16[144,1024]{1,0:T(8,128)(2,1)}, bf16[144,1024]{1,0:T(8,128)(2,1)S(1)}, u32[]{:S(2)}, u32[]{:S(2)}) %collective-permute-start.10) | collective-permute-done | bytes 294944 | tf_op jit(solution)/shard_map/ppermute | solution.py:521
  29.6 4.7 %collective-permute-start.9 = (bf16[128,512]{1,0:T(8,128)(2,1)S(1)}, bf16[128,512]{1,0:T(8,128)(2,1)S(1)}, u32[]{:S(2)}, u32[]{:S(2)}) collective-permute-start(bf16[128,512]{1,0:T(8,128)(2,1)S(1)} %get-tuple-element.23), channel_id=1, source_target_pairs={{0,10},{1,11},{2,8},{3,9},{4,14},{5,15},{6,12},{7,13},{8,18},{9,19... | collective-permute-start | bytes 393224 | tf_op jit(solution)/shard_map/ppermute | solution.py:521
  34.4 0.0 collective-permute-done.15.refs_4_
  34.4 0.0 collective-permute-start.14
  34.4 0.0 collective-permute-done.18.refs_7_
  34.4 0.6 %collective-permute-start.16 = (bf16[128,256]{1,0:T(8,128)(2,1)S(1)}, bf16[128,256]{1,0:T(8,128)(2,1)S(1)}, u32[]{:S(2)}, u32[]{:S(2)}) collective-permute-start(bf16[128,256]{1,0:T(8,128)(2,1)S(1)} %get-tuple-element.30), channel_id=1, source_target_pairs={{0,1},{1,0},{2,3},{3,2},{4,5},{5,4},{6,7},{7,6},{8,9},{9,8},{10,11... | collective-permute-start | bytes 196616 | tf_op jit(solution)/shard_map/ppermute | solution.py:511
  35.0 0.0 collective-permute-done.12.refs_1_
  35.0 0.1 collective-permute-start.17
  35.1 0.6 %collective-permute-done.14.refs_3_ = bf16[128,512]{1,0:T(8,128)(2,1)S(1)} collective-permute-done((bf16[128,512]{1,0:T(8,128)(2,1)S(1)}, bf16[128,512]{1,0:T(8,128)(2,1)S(1)}, u32[]{:S(2)}, u32[]{:S(2)}) %collective-permute-start.14) | collective-permute-done | bytes 131104 | tf_op jit(solution)/shard_map/ppermute | solution.py:511
  35.7 0.1 collective-permute-start.19
  35.9 0.0 collective-permute-done.16.refs_5_
  35.9 0.4 collective-permute-start.20
  36.3 0.1 collective-permute-done.17.refs_6_
  36.3 0.7 %collective-permute-done.19.refs_8_ = bf16[128,256]{1,0:T(8,128)(2,1)S(1)} collective-permute-done((bf16[128,256]{1,0:T(8,128)(2,1)S(1)}, bf16[128,256]{1,0:T(8,128)(2,1)S(1)}, u32[]{:S(2)}, u32[]{:S(2)}) %collective-permute-start.19) | collective-permute-done | bytes 65568 | tf_op jit(solution)/shard_map/ppermute | solution.py:511
  37.0 0.2 collective-permute-done.20.refs_9_
  37.2 1.0 %attend_relayed.1 = bf16[128,1024]{1,0:T(8,128)(2,1)S(1)} custom-call(bf16[144,1024]{1,0:T(8,128)(2,1)S(1)} %collective-permute-done.10.packed, bf16[128,512]{1,0:T(8,128)(2,1)S(1)} %collective-permute-done.11.refs_0_, bf16[128,512]{1,0:T(8,128)(2,1)S(1)} %collective-permute-done.12.refs_1_, bf16[128,512]{1,0:T(8,128)(2,1)S(1)} %collective-permute-done.13.refs_2_, ...), custom_call_target="tpu_custom_call" | custom-call | tf_op jit(solution)/shard_map/attend_relayed/pallas_call | solution.py:495
  38.2 0.0 collective-permute-done.8
  38.2 0.0 collective-permute-done.9
  38.2 0.9 %fusion = bf16[1,128,2048]{2,1,0:T(8,128)(2,1)} fusion(bf16[1,128,1024]{2,1,0:T(8,128)(2,1)S(1)} %bitcast.3, bf16[1,128,512]{2,1,0:T(8,128)(2,1)S(1)} %bitcast.5, bf16[1,128,512]{2,1,0:T(8,128)(2,1)S(1)} %bitcast.4, pred[]{:T(512)S(6)} %eq.3), kind=kLoop, calls=%fused_computation.2 | loop fusion | flops 3145728 | bytes 1048577 | tf_op jit(solution)/shard_map/jit(_where)/select_n | solution.py:569
  (7 shorter events, 0.0 us)
Async XLA Ops:
  0.0 23.2 %copy-start.2 = (s32[1,128]{1,0:T(1,128)S(1)}, s32[1,128]{1,0:T(1,128)}, u32[]{:S(2)}) copy-start(s32[1,128]{1,0:T(1,128)} %scored.3) | copy-start | bytes 1540
  0.0 23.2 %copy-start = (bf16[1,128,2048]{2,1,0:T(8,128)(2,1)S(1)}, bf16[1,128,2048]{2,1,0:T(8,128)(2,1)}, u32[]{:S(2)}) copy-start(bf16[1,128,2048]{2,1,0:T(8,128)(2,1)} %queries.3) | copy-start | bytes 1572868
  0.0 23.2 %copy-start.1 = (s32[1,1024]{1,0:T(1,128)S(1)}, s32[1,1024]{1,0:T(1,128)}, u32[]{:S(2)}) copy-start(s32[1,1024]{1,0:T(1,128)} %docs.3) | copy-start | bytes 12292
  5.8 14.5 %collective-permute-start = (bf16[144,768]{1,0:T(8,128)(2,1)}, bf16[144,768]{1,0:T(8,128)(2,1)S(1)}, u32[]{:S(2)}, u32[]{:S(2)}) collective-permute-start(bf16[144,768]{1,0:T(8,128)(2,1)} %get-tuple-element.16), channel_id=1, source_target_pairs={{0,2},{1,3},{2,0},{3,1},{4,6},{5,7},{6,4},{7,5},{8,10},{9,11},{10,... | collective-permute-start | bytes 663560 | tf_op jit(solution)/shard_map/ppermute | solution.py:507
  8.9 7.3 %collective-permute-start.11 = (bf16[128,512]{1,0:T(8,128)(2,1)}, bf16[128,512]{1,0:T(8,128)(2,1)S(1)}, u32[]{:S(2)}, u32[]{:S(2)}) collective-permute-start(bf16[128,512]{1,0:T(8,128)(2,1)} %get-tuple-element.25), channel_id=1, source_target_pairs={{0,8},{1,9},{2,10},{3,11},{4,12},{5,13},{6,14},{7,15},{8,16},{9,17... | collective-permute-start | bytes 393224 | tf_op jit(solution)/shard_map/ppermute | solution.py:521
  10.4 8.3 %collective-permute-start.3 = (bf16[128,256]{1,0:T(8,128)(2,1)}, bf16[128,256]{1,0:T(8,128)(2,1)S(1)}, u32[]{:S(2)}, u32[]{:S(2)}) collective-permute-start(bf16[128,256]{1,0:T(8,128)(2,1)} %get-tuple-element.17), channel_id=1, source_target_pairs={{0,1},{1,0},{2,3},{3,2},{4,5},{5,4},{6,7},{7,6},{8,9},{9,8},{10,11... | collective-permute-start | bytes 196616 | tf_op jit(solution)/shard_map/ppermute | solution.py:511
  10.4 8.4 %collective-permute-start.1 = (bf16[128,256]{1,0:T(8,128)(2,1)}, bf16[128,256]{1,0:T(8,128)(2,1)S(1)}, u32[]{:S(2)}, u32[]{:S(2)}) collective-permute-start(bf16[128,256]{1,0:T(8,128)(2,1)} %get-tuple-element.17), channel_id=1, source_target_pairs={{0,4},{1,5},{2,6},{3,7},{8,12},{9,13},{10,14},{11,15},{16,20},{17,... | collective-permute-start | bytes 196616 | tf_op jit(solution)/shard_map/ppermute | solution.py:507
  14.9 5.4 %collective-permute-start.2 = (bf16[128,256]{1,0:T(8,128)(2,1)}, bf16[128,256]{1,0:T(8,128)(2,1)S(1)}, u32[]{:S(2)}, u32[]{:S(2)}) collective-permute-start(bf16[128,256]{1,0:T(8,128)(2,1)} %get-tuple-element.18), channel_id=1, source_target_pairs={{0,6},{1,7},{2,4},{3,5},{8,14},{9,15},{10,12},{11,13},{16,22},{17,... | collective-permute-start | bytes 196616 | tf_op jit(solution)/shard_map/ppermute | solution.py:507
  16.2 5.6 %collective-permute-start.13 = (bf16[128,512]{1,0:T(8,128)(2,1)S(1)}, bf16[128,512]{1,0:T(8,128)(2,1)S(1)}, u32[]{:S(2)}, u32[]{:S(2)}) collective-permute-start(bf16[128,512]{1,0:T(8,128)(2,1)S(1)} %collective-permute-done.11.refs_0_), channel_id=1, source_target_pairs={{0,2},{1,3},{2,4},{3,5},{4,6},{5,7},{8,10},{9,11},{10,12},{11,13},... | collective-permute-start | bytes 393224 | tf_op jit(solution)/shard_map/ppermute | solution.py:507
  18.7 2.2 %collective-permute-start.4 = (bf16[128,256]{1,0:T(8,128)(2,1)S(1)}, bf16[128,256]{1,0:T(8,128)(2,1)S(1)}, u32[]{:S(2)}, u32[]{:S(2)}) collective-permute-start(bf16[128,256]{1,0:T(8,128)(2,1)S(1)} %collective-permute-done.3.mine_x), channel_id=1, source_target_pairs={{0,1},{1,0},{2,3},{3,2},{4,5},{5,4},{6,7},{7,6},{8,9},{9,8},{10,11... | collective-permute-start | bytes 196616 | tf_op jit(solution)/shard_map/ppermute | solution.py:511
  18.8 10.9 %collective-permute-start.10 = (bf16[144,1024]{1,0:T(8,128)(2,1)}, bf16[144,1024]{1,0:T(8,128)(2,1)S(1)}, u32[]{:S(2)}, u32[]{:S(2)}) collective-permute-start(bf16[144,1024]{1,0:T(8,128)(2,1)} %get-tuple-element.24), channel_id=1, source_target_pairs={{0,8},{1,9},{2,10},{3,11},{4,12},{5,13},{6,14},{7,15},{8,16},{9,17... | collective-permute-start | bytes 884744 | tf_op jit(solution)/shard_map/ppermute | solution.py:521
  20.3 1.5 %collective-permute-start.5 = (bf16[128,256]{1,0:T(8,128)(2,1)S(1)}, bf16[128,256]{1,0:T(8,128)(2,1)S(1)}, u32[]{:S(2)}, u32[]{:S(2)}) collective-permute-start(bf16[128,256]{1,0:T(8,128)(2,1)S(1)} %slice.15), channel_id=1, source_target_pairs={{0,1},{1,0},{2,3},{3,2},{4,5},{5,4},{6,7},{7,6},{8,9},{9,8},{10,11... | collective-permute-start | bytes 196616 | tf_op jit(solution)/shard_map/ppermute | solution.py:511
  20.6 1.9 %collective-permute-start.6 = (bf16[128,256]{1,0:T(8,128)(2,1)S(1)}, bf16[128,256]{1,0:T(8,128)(2,1)S(1)}, u32[]{:S(2)}, u32[]{:S(2)}) collective-permute-start(bf16[128,256]{1,0:T(8,128)(2,1)S(1)} %collective-permute-done.1.far), channel_id=1, source_target_pairs={{0,1},{1,0},{2,3},{3,2},{4,5},{5,4},{6,7},{7,6},{8,9},{9,8},{10,11... | collective-permute-start | bytes 196616 | tf_op jit(solution)/shard_map/ppermute | solution.py:511
  20.9 2.2 %collective-permute-start.7 = (bf16[128,256]{1,0:T(8,128)(2,1)S(1)}, bf16[128,256]{1,0:T(8,128)(2,1)S(1)}, u32[]{:S(2)}, u32[]{:S(2)}) collective-permute-start(bf16[128,256]{1,0:T(8,128)(2,1)S(1)} %collective-permute-done.2.beyond), channel_id=1, source_target_pairs={{0,1},{1,0},{2,3},{3,2},{4,5},{5,4},{6,7},{7,6},{8,9},{9,8},{10,11... | collective-permute-start | bytes 196616 | tf_op jit(solution)/shard_map/ppermute | solution.py:511
  21.8 13.2 %collective-permute-start.12 = (bf16[128,512]{1,0:T(8,128)(2,1)S(1)}, bf16[128,512]{1,0:T(8,128)(2,1)S(1)}, u32[]{:S(2)}, u32[]{:S(2)}) collective-permute-start(bf16[128,512]{1,0:T(8,128)(2,1)S(1)} %collective-permute-done.11.refs_0_), channel_id=1, source_target_pairs={{0,1},{1,0},{2,3},{3,2},{4,5},{5,4},{6,7},{7,6},{8,9},{9,8},{10,11... | collective-permute-start | bytes 393224 | tf_op jit(solution)/shard_map/ppermute | solution.py:511
  21.8 12.6 %collective-permute-start.15 = (bf16[128,512]{1,0:T(8,128)(2,1)S(1)}, bf16[128,512]{1,0:T(8,128)(2,1)S(1)}, u32[]{:S(2)}, u32[]{:S(2)}) collective-permute-start(bf16[128,512]{1,0:T(8,128)(2,1)S(1)} %collective-permute-done.13.refs_2_), channel_id=1, source_target_pairs={{2,4},{3,5},{4,6},{5,7},{10,12},{11,13},{12,14},{13,15},{18,20},{1... | collective-permute-start | bytes 393224 | tf_op jit(solution)/shard_map/ppermute | solution.py:507
  22.5 11.9 %collective-permute-start.18 = (bf16[128,512]{1,0:T(8,128)(2,1)S(1)}, bf16[128,512]{1,0:T(8,128)(2,1)S(1)}, u32[]{:S(2)}, u32[]{:S(2)}) collective-permute-start(bf16[128,512]{1,0:T(8,128)(2,1)S(1)} %collective-permute-done.13.refs_2_), channel_id=1, source_target_pairs={{2,6},{3,7},{10,14},{11,15},{18,22},{19,23},{26,30},{27,31}} | collective-permute-start | bytes 393224 | tf_op jit(solution)/shard_map/ppermute | solution.py:507
  24.8 13.4 %collective-permute-start.8 = (bf16[128,512]{1,0:T(8,128)(2,1)S(1)}, bf16[128,512]{1,0:T(8,128)(2,1)S(1)}, u32[]{:S(2)}, u32[]{:S(2)}) collective-permute-start(bf16[128,512]{1,0:T(8,128)(2,1)S(1)} %get-tuple-element.22), channel_id=1, source_target_pairs={{0,8},{1,9},{2,10},{3,11},{4,12},{5,13},{6,14},{7,15},{8,16},{9,17... | collective-permute-start | bytes 393224 | tf_op jit(solution)/shard_map/ppermute | solution.py:521
  29.6 8.5 %collective-permute-start.9 = (bf16[128,512]{1,0:T(8,128)(2,1)S(1)}, bf16[128,512]{1,0:T(8,128)(2,1)S(1)}, u32[]{:S(2)}, u32[]{:S(2)}) collective-permute-start(bf16[128,512]{1,0:T(8,128)(2,1)S(1)} %get-tuple-element.23), channel_id=1, source_target_pairs={{0,10},{1,11},{2,8},{3,9},{4,14},{5,15},{6,12},{7,13},{8,18},{9,19... | collective-permute-start | bytes 393224 | tf_op jit(solution)/shard_map/ppermute | solution.py:521
  34.4 1.3 %collective-permute-start.14 = (bf16[128,512]{1,0:T(8,128)(2,1)S(1)}, bf16[128,512]{1,0:T(8,128)(2,1)S(1)}, u32[]{:S(2)}, u32[]{:S(2)}) collective-permute-start(bf16[128,512]{1,0:T(8,128)(2,1)S(1)} %collective-permute-done.13.refs_2_), channel_id=1, source_target_pairs={{0,1},{1,0},{2,3},{3,2},{4,5},{5,4},{6,7},{7,6},{8,9},{9,8},{10,11... | collective-permute-start | bytes 393224 | tf_op jit(solution)/shard_map/ppermute | solution.py:511
  34.4 1.5 %collective-permute-start.16 = (bf16[128,256]{1,0:T(8,128)(2,1)S(1)}, bf16[128,256]{1,0:T(8,128)(2,1)S(1)}, u32[]{:S(2)}, u32[]{:S(2)}) collective-permute-start(bf16[128,256]{1,0:T(8,128)(2,1)S(1)} %get-tuple-element.30), channel_id=1, source_target_pairs={{0,1},{1,0},{2,3},{3,2},{4,5},{5,4},{6,7},{7,6},{8,9},{9,8},{10,11... | collective-permute-start | bytes 196616 | tf_op jit(solution)/shard_map/ppermute | solution.py:511
  35.0 1.3 %collective-permute-start.17 = (bf16[128,256]{1,0:T(8,128)(2,1)S(1)}, bf16[128,256]{1,0:T(8,128)(2,1)S(1)}, u32[]{:S(2)}, u32[]{:S(2)}) collective-permute-start(bf16[128,256]{1,0:T(8,128)(2,1)S(1)} %get-tuple-element.29), channel_id=1, source_target_pairs={{0,1},{1,0},{2,3},{3,2},{4,5},{5,4},{6,7},{7,6},{8,9},{9,8},{10,11... | collective-permute-start | bytes 196616 | tf_op jit(solution)/shard_map/ppermute | solution.py:511
  35.7 1.3 %collective-permute-start.19 = (bf16[128,256]{1,0:T(8,128)(2,1)S(1)}, bf16[128,256]{1,0:T(8,128)(2,1)S(1)}, u32[]{:S(2)}, u32[]{:S(2)}) collective-permute-start(bf16[128,256]{1,0:T(8,128)(2,1)S(1)} %get-tuple-element.28), channel_id=1, source_target_pairs={{0,1},{1,0},{2,3},{3,2},{4,5},{5,4},{6,7},{7,6},{8,9},{9,8},{10,11... | collective-permute-start | bytes 196616 | tf_op jit(solution)/shard_map/ppermute | solution.py:511
  35.9 1.3 %collective-permute-start.20 = (bf16[128,256]{1,0:T(8,128)(2,1)S(1)}, bf16[128,256]{1,0:T(8,128)(2,1)S(1)}, u32[]{:S(2)}, u32[]{:S(2)}) collective-permute-start(bf16[128,256]{1,0:T(8,128)(2,1)S(1)} %get-tuple-element.27), channel_id=1, source_target_pairs={{0,1},{1,0},{2,3},{3,2},{4,5},{5,4},{6,7},{7,6},{8,9},{9,8},{10,11... | collective-permute-start | bytes 196616 | tf_op jit(solution)/shard_map/ppermute | solution.py:511

commit v6 on v5

--- a/solution.py
+++ b/solution.py
@@ -544,7 +544,6 @@
     away_1 = send(away, ((0, 1), (1, 2), (2, 3)))
     away_2 = send(away_1, ((1, 2), (2, 3)))
     away_3 = send(away_1, ((1, 3),))
-    swap, far, beyond = lax.optimization_barrier((swap, far, beyond))
     mine_x = across(mine)
     own, partners = attend_home(
         queries,

time: 39.4 us -> 39.3 us (level)
    ppermute x6, waiting for transfers between devices: 0.74 us -> 0.07 us  [send(): return lax.ppermute(block, 'ctx', pairs)]
    ppermute x11, waiting for transfers between devices: 1.56 us -> 2.06 us  [across(): lax.ppermute(block, 'ctx', [(i, i ^ 1) for i in range(lax.axis_size('ctx'...]
  transfers between devices with their start and end apart: 21 -> 21, of which waited for: 6 -> 7; matrix products, arithmetic and copies ran while one was open for 0% -> 0% of each run, Pallas kernels for 7% -> 7%
where the time goes in v6:
time: 39.3 us; the launch traced here: 39.1 us
  starting transfers between devices  24 us (61%)
  Pallas kernels  8.36 us (21%)
  waiting for transfers between devices  5.55 us (14%)
  other arithmetic  0.9 us (2%)
    ppermute x6, starting transfers between devices, send(): return lax.ppermute(block, 'ctx', pairs)  12.7 us
    ppermute x4, starting transfers between devices, onward(): return lax.ppermute(block, ('phase', 'ctx'), route)  9.21 us
    pallas_call x1, Pallas kernels, project(): pl.pallas_call(functools.partial(project_kernel, cuts), out_shape=[jax.Sh...  5.77 us
    ppermute x4, waiting for transfers between devices, onward(): return lax.ppermute(block, ('phase', 'ctx'), route)  3.42 us
    ppermute x11, starting transfers between devices, across(): lax.ppermute(block, 'ctx', [(i, i ^ 1) for i in range(lax.axis_size('ctx'...  2.13 us
    ppermute x11, waiting for transfers between devices, across(): lax.ppermute(block, 'ctx', [(i, i ^ 1) for i in range(lax.axis_size('ctx'...  2.06 us
    pallas_call x1, Pallas kernels, attend_home(): pl.pallas_call(attend_home_kernel, grid=(1,), out_shape=(out, out), in_sp...  1.6 us
    pallas_call x1, Pallas kernels, attend_relayed(): pl.pallas_call(attend_relayed_kernel, out_shape=jax.ShapeDtypeStruct((row...  0.99 us
  transfers between devices with their start and end apart: 21, of which 7 were waited for; matrix products, arithmetic and copies ran while one was open for 0% of the time, Pallas kernels for 7%

profile of v6, /device:TPU:0, one launch (start us, length us, event | category | flops | bytes accessed | tf_op | source)
XLA Modules:
  0.0 39.1 jit_solution(5313776852252349909)
XLA Ops:
  0.0 5.8 %project.1 = (bf16[128,256]{1,0:T(8,128)(2,1)}, bf16[128,256]{1,0:T(8,128)(2,1)}, bf16[144,768]{1,0:T(8,128)(2,1)}, bf16[128,512]{1,0:T(8,128)(2,1)}, bf16[144,1024]{1,0:T(8,128)(2,1)}) custom-call(bf16[1,128,4096]{2,1,0:T(8,128)(2,1)} %hidden.1, bf16[1,4096,1024]{2,1,0:T(8,128)(2,1)} %weight.1, bf16[1,128,2048]{2,1,0:T(8,128)(2,1)} %queries.3, ...), custom_call_target="tpu_custom_call" | custom-call | tf_op jit(solution)/shard_map/project/pallas_call | solution.py:266
  5.8 3.1 %collective-permute-start = (bf16[144,768]{1,0:T(8,128)(2,1)}, bf16[144,768]{1,0:T(8,128)(2,1)S(1)}, u32[]{:S(2)}, u32[]{:S(2)}) collective-permute-start(bf16[144,768]{1,0:T(8,128)(2,1)} %get-tuple-element.13), channel_id=1, source_target_pairs={{0,2},{1,3},{2,0},{3,1},{4,6},{5,7},{6,4},{7,5},{8,10},{9,11},{10,... | collective-permute-start | bytes 663560 | tf_op jit(solution)/shard_map/ppermute | solution.py:507
  8.9 1.5 %collective-permute-start.11 = (bf16[128,512]{1,0:T(8,128)(2,1)}, bf16[128,512]{1,0:T(8,128)(2,1)S(1)}, u32[]{:S(2)}, u32[]{:S(2)}) collective-permute-start(bf16[128,512]{1,0:T(8,128)(2,1)} %get-tuple-element.19), channel_id=1, source_target_pairs={{0,8},{1,9},{2,10},{3,11},{4,12},{5,13},{6,14},{7,15},{8,16},{9,17... | collective-permute-start | bytes 393224 | tf_op jit(solution)/shard_map/ppermute | solution.py:521
  10.4 0.0 collective-permute-start.1
  10.4 4.5 %collective-permute-start.4 = (bf16[128,256]{1,0:T(8,128)(2,1)}, bf16[128,256]{1,0:T(8,128)(2,1)S(1)}, u32[]{:S(2)}, u32[]{:S(2)}) collective-permute-start(bf16[128,256]{1,0:T(8,128)(2,1)} %get-tuple-element.14), channel_id=1, source_target_pairs={{0,4},{1,5},{2,6},{3,7},{8,12},{9,13},{10,14},{11,15},{16,20},{17,... | collective-permute-start | bytes 196616 | tf_op jit(solution)/shard_map/ppermute | solution.py:507
  14.9 1.3 %collective-permute-start.6 = (bf16[128,256]{1,0:T(8,128)(2,1)}, bf16[128,256]{1,0:T(8,128)(2,1)S(1)}, u32[]{:S(2)}, u32[]{:S(2)}) collective-permute-start(bf16[128,256]{1,0:T(8,128)(2,1)} %get-tuple-element.15), channel_id=1, source_target_pairs={{0,6},{1,7},{2,4},{3,5},{8,14},{9,15},{10,12},{11,13},{16,22},{17,... | collective-permute-start | bytes 196616 | tf_op jit(solution)/shard_map/ppermute | solution.py:507
  16.2 0.0 collective-permute-done.11.refs_0_
  16.2 2.5 %collective-permute-start.13 = (bf16[128,512]{1,0:T(8,128)(2,1)S(1)}, bf16[128,512]{1,0:T(8,128)(2,1)S(1)}, u32[]{:S(2)}, u32[]{:S(2)}) collective-permute-start(bf16[128,512]{1,0:T(8,128)(2,1)S(1)} %collective-permute-done.11.refs_0_), channel_id=1, source_target_pairs={{0,2},{1,3},{2,4},{3,5},{4,6},{5,7},{8,10},{9,11},{10,12},{11,13},... | collective-permute-start | bytes 393224 | tf_op jit(solution)/shard_map/ppermute | solution.py:507
  18.7 0.0 collective-permute-done.1.mine_x
  18.7 0.1 collective-permute-start.2
  18.8 0.0 collective-permute-done.4.far
  18.8 1.5 %collective-permute-start.10 = (bf16[144,1024]{1,0:T(8,128)(2,1)}, bf16[144,1024]{1,0:T(8,128)(2,1)S(1)}, u32[]{:S(2)}, u32[]{:S(2)}) collective-permute-start(bf16[144,1024]{1,0:T(8,128)(2,1)} %get-tuple-element.18), channel_id=1, source_target_pairs={{0,8},{1,9},{2,10},{3,11},{4,12},{5,13},{6,14},{7,15},{8,16},{9,17... | collective-permute-start | bytes 884744 | tf_op jit(solution)/shard_map/ppermute | solution.py:521
  20.3 0.0 collective-permute-done.6.beyond
  20.3 0.2 collective-permute-start.5
  20.5 0.0 collective-permute-done.swap
  20.5 0.4 collective-permute-start.7
  20.8 0.0 collective-permute-done.2.mine
  20.8 0.2 collective-permute-start.3
  21.1 0.5 %collective-permute-done.5.far_x = bf16[128,256]{1,0:T(8,128)(2,1)S(1)} collective-permute-done((bf16[128,256]{1,0:T(8,128)(2,1)S(1)}, bf16[128,256]{1,0:T(8,128)(2,1)S(1)}, u32[]{:S(2)}, u32[]{:S(2)}) %collective-permute-start.5) | collective-permute-done | bytes 65568 | tf_op jit(solution)/shard_map/ppermute | solution.py:511
  21.6 0.2 collective-permute-start.12
  21.7 0.1 collective-permute-done.13.refs_2_
  21.8 0.7 %collective-permute-start.15 = (bf16[128,512]{1,0:T(8,128)(2,1)S(1)}, bf16[128,512]{1,0:T(8,128)(2,1)S(1)}, u32[]{:S(2)}, u32[]{:S(2)}) collective-permute-start(bf16[128,512]{1,0:T(8,128)(2,1)S(1)} %collective-permute-done.13.refs_2_), channel_id=1, source_target_pairs={{2,4},{3,5},{4,6},{5,7},{10,12},{11,13},{12,14},{13,15},{18,20},{1... | collective-permute-start | bytes 393224 | tf_op jit(solution)/shard_map/ppermute | solution.py:507
  22.5 0.0 collective-permute-done.7.beyond_x
  22.5 0.7 %collective-permute-start.18 = (bf16[128,512]{1,0:T(8,128)(2,1)S(1)}, bf16[128,512]{1,0:T(8,128)(2,1)S(1)}, u32[]{:S(2)}, u32[]{:S(2)}) collective-permute-start(bf16[128,512]{1,0:T(8,128)(2,1)S(1)} %collective-permute-done.13.refs_2_), channel_id=1, source_target_pairs={{2,6},{3,7},{10,14},{11,15},{18,22},{19,23},{26,30},{27,31}} | collective-permute-start | bytes 393224 | tf_op jit(solution)/shard_map/ppermute | solution.py:507
  23.1 0.0 collective-permute-done.3.near_x
  23.2 0.0 copy-done.2
  23.2 0.0 copy-done
  23.2 1.6 %attend_home.1 = (bf16[128,512]{1,0:T(8,128)(2,1)S(1)}, bf16[128,512]{1,0:T(8,128)(2,1)S(1)}) custom-call(bf16[1,128,2048]{2,1,0:T(8,128)(2,1)S(1)} %copy-done, bf16[144,768]{1,0:T(8,128)(2,1)S(1)} %collective-permute-done.swap, bf16[128,256]{1,0:T(8,128)(2,1)S(1)} %collective-permute-done.2.mine, bf16[128,256]{1,0:T(8,128)(2,1)S(1)} %collective-permute-done.1.mine_x, ...), custom_call_target="tpu_custom_call" | custom-call | flops 1900000000 | tf_op jit(solution)/shard_map/attend_home/pallas_call | solution.py:480
  24.8 1.5 %collective-permute-start.8 = (bf16[128,512]{1,0:T(8,128)(2,1)S(1)}, bf16[128,512]{1,0:T(8,128)(2,1)S(1)}, u32[]{:S(2)}, u32[]{:S(2)}) collective-permute-start(bf16[128,512]{1,0:T(8,128)(2,1)S(1)} %get-tuple-element.16), channel_id=1, source_target_pairs={{0,8},{1,9},{2,10},{3,11},{4,12},{5,13},{6,14},{7,15},{8,16},{9,17... | collective-permute-start | bytes 393224 | tf_op jit(solution)/shard_map/ppermute | solution.py:521
  26.3 3.4 %collective-permute-done.10.packed = bf16[144,1024]{1,0:T(8,128)(2,1)S(1)} collective-permute-done((bf16[144,1024]{1,0:T(8,128)(2,1)}, bf16[144,1024]{1,0:T(8,128)(2,1)S(1)}, u32[]{:S(2)}, u32[]{:S(2)}) %collective-permute-start.10) | collective-permute-done | bytes 294944 | tf_op jit(solution)/shard_map/ppermute | solution.py:521
  29.7 4.6 %collective-permute-start.9 = (bf16[128,512]{1,0:T(8,128)(2,1)S(1)}, bf16[128,512]{1,0:T(8,128)(2,1)S(1)}, u32[]{:S(2)}, u32[]{:S(2)}) collective-permute-start(bf16[128,512]{1,0:T(8,128)(2,1)S(1)} %get-tuple-element.17), channel_id=1, source_target_pairs={{0,10},{1,11},{2,8},{3,9},{4,14},{5,15},{6,12},{7,13},{8,18},{9,19... | collective-permute-start | bytes 393224 | tf_op jit(solution)/shard_map/ppermute | solution.py:521
  34.4 0.0 collective-permute-done.15.refs_4_
  34.4 0.0 collective-permute-start.14
  34.4 0.0 collective-permute-done.18.refs_7_
  34.4 0.6 %collective-permute-start.16 = (bf16[128,256]{1,0:T(8,128)(2,1)S(1)}, bf16[128,256]{1,0:T(8,128)(2,1)S(1)}, u32[]{:S(2)}, u32[]{:S(2)}) collective-permute-start(bf16[128,256]{1,0:T(8,128)(2,1)S(1)} %get-tuple-element.24), channel_id=1, source_target_pairs={{0,1},{1,0},{2,3},{3,2},{4,5},{5,4},{6,7},{7,6},{8,9},{9,8},{10,11... | collective-permute-start | bytes 196616 | tf_op jit(solution)/shard_map/ppermute | solution.py:511
  35.0 0.0 collective-permute-done.12.refs_1_
  35.0 0.1 collective-permute-start.17
  35.1 0.6 %collective-permute-done.14.refs_3_ = bf16[128,512]{1,0:T(8,128)(2,1)S(1)} collective-permute-done((bf16[128,512]{1,0:T(8,128)(2,1)S(1)}, bf16[128,512]{1,0:T(8,128)(2,1)S(1)}, u32[]{:S(2)}, u32[]{:S(2)}) %collective-permute-start.14) | collective-permute-done | bytes 131104 | tf_op jit(solution)/shard_map/ppermute | solution.py:511
  35.7 0.1 collective-permute-start.19
  35.9 0.0 collective-permute-done.16.refs_5_
  35.9 0.4 collective-permute-start.20
  36.3 0.1 collective-permute-done.17.refs_6_
  36.3 0.7 %collective-permute-done.19.refs_8_ = bf16[128,256]{1,0:T(8,128)(2,1)S(1)} collective-permute-done((bf16[128,256]{1,0:T(8,128)(2,1)S(1)}, bf16[128,256]{1,0:T(8,128)(2,1)S(1)}, u32[]{:S(2)}, u32[]{:S(2)}) %collective-permute-start.19) | collective-permute-done | bytes 65568 | tf_op jit(solution)/shard_map/ppermute | solution.py:511
  37.0 0.2 collective-permute-done.20.refs_9_
  37.2 1.0 %attend_relayed.1 = bf16[128,1024]{1,0:T(8,128)(2,1)S(1)} custom-call(bf16[144,1024]{1,0:T(8,128)(2,1)S(1)} %collective-permute-done.10.packed, bf16[128,512]{1,0:T(8,128)(2,1)S(1)} %collective-permute-done.11.refs_0_, bf16[128,512]{1,0:T(8,128)(2,1)S(1)} %collective-permute-done.12.refs_1_, bf16[128,512]{1,0:T(8,128)(2,1)S(1)} %collective-permute-done.13.refs_2_, ...), custom_call_target="tpu_custom_call" | custom-call | tf_op jit(solution)/shard_map/attend_relayed/pallas_call | solution.py:495
  38.1 0.0 collective-permute-done.8
  38.2 0.0 collective-permute-done.9
  38.2 0.9 %fusion = bf16[1,128,2048]{2,1,0:T(8,128)(2,1)} fusion(bf16[1,128,1024]{2,1,0:T(8,128)(2,1)S(1)} %bitcast.3, bf16[1,128,512]{2,1,0:T(8,128)(2,1)S(1)} %bitcast.5, bf16[1,128,512]{2,1,0:T(8,128)(2,1)S(1)} %bitcast.4, pred[]{:T(512)S(6)} %eq.3), kind=kLoop, calls=%fused_computation.2 | loop fusion | flops 3145728 | bytes 1048577 | tf_op jit(solution)/shard_map/jit(_where)/select_n | solution.py:568
  (7 shorter events, 0.0 us)
Async XLA Ops:
  0.0 23.2 %copy-start.2 = (s32[1,128]{1,0:T(1,128)S(1)}, s32[1,128]{1,0:T(1,128)}, u32[]{:S(2)}) copy-start(s32[1,128]{1,0:T(1,128)} %scored.3) | copy-start | bytes 1540
  0.0 23.2 %copy-start = (bf16[1,128,2048]{2,1,0:T(8,128)(2,1)S(1)}, bf16[1,128,2048]{2,1,0:T(8,128)(2,1)}, u32[]{:S(2)}) copy-start(bf16[1,128,2048]{2,1,0:T(8,128)(2,1)} %queries.3) | copy-start | bytes 1572868
  0.0 23.2 %copy-start.1 = (s32[1,1024]{1,0:T(1,128)S(1)}, s32[1,1024]{1,0:T(1,128)}, u32[]{:S(2)}) copy-start(s32[1,1024]{1,0:T(1,128)} %docs.3) | copy-start | bytes 12292
  5.8 14.7 %collective-permute-start = (bf16[144,768]{1,0:T(8,128)(2,1)}, bf16[144,768]{1,0:T(8,128)(2,1)S(1)}, u32[]{:S(2)}, u32[]{:S(2)}) collective-permute-start(bf16[144,768]{1,0:T(8,128)(2,1)} %get-tuple-element.13), channel_id=1, source_target_pairs={{0,2},{1,3},{2,0},{3,1},{4,6},{5,7},{6,4},{7,5},{8,10},{9,11},{10,... | collective-permute-start | bytes 663560 | tf_op jit(solution)/shard_map/ppermute | solution.py:507
  8.9 7.3 %collective-permute-start.11 = (bf16[128,512]{1,0:T(8,128)(2,1)}, bf16[128,512]{1,0:T(8,128)(2,1)S(1)}, u32[]{:S(2)}, u32[]{:S(2)}) collective-permute-start(bf16[128,512]{1,0:T(8,128)(2,1)} %get-tuple-element.19), channel_id=1, source_target_pairs={{0,8},{1,9},{2,10},{3,11},{4,12},{5,13},{6,14},{7,15},{8,16},{9,17... | collective-permute-start | bytes 393224 | tf_op jit(solution)/shard_map/ppermute | solution.py:521
  10.4 8.3 %collective-permute-start.1 = (bf16[128,256]{1,0:T(8,128)(2,1)}, bf16[128,256]{1,0:T(8,128)(2,1)S(1)}, u32[]{:S(2)}, u32[]{:S(2)}) collective-permute-start(bf16[128,256]{1,0:T(8,128)(2,1)} %get-tuple-element.14), channel_id=1, source_target_pairs={{0,1},{1,0},{2,3},{3,2},{4,5},{5,4},{6,7},{7,6},{8,9},{9,8},{10,11... | collective-permute-start | bytes 196616 | tf_op jit(solution)/shard_map/ppermute | solution.py:511
  10.4 8.4 %collective-permute-start.4 = (bf16[128,256]{1,0:T(8,128)(2,1)}, bf16[128,256]{1,0:T(8,128)(2,1)S(1)}, u32[]{:S(2)}, u32[]{:S(2)}) collective-permute-start(bf16[128,256]{1,0:T(8,128)(2,1)} %get-tuple-element.14), channel_id=1, source_target_pairs={{0,4},{1,5},{2,6},{3,7},{8,12},{9,13},{10,14},{11,15},{16,20},{17,... | collective-permute-start | bytes 196616 | tf_op jit(solution)/shard_map/ppermute | solution.py:507
  14.9 5.4 %collective-permute-start.6 = (bf16[128,256]{1,0:T(8,128)(2,1)}, bf16[128,256]{1,0:T(8,128)(2,1)S(1)}, u32[]{:S(2)}, u32[]{:S(2)}) collective-permute-start(bf16[128,256]{1,0:T(8,128)(2,1)} %get-tuple-element.15), channel_id=1, source_target_pairs={{0,6},{1,7},{2,4},{3,5},{8,14},{9,15},{10,12},{11,13},{16,22},{17,... | collective-permute-start | bytes 196616 | tf_op jit(solution)/shard_map/ppermute | solution.py:507
  16.2 5.6 %collective-permute-start.13 = (bf16[128,512]{1,0:T(8,128)(2,1)S(1)}, bf16[128,512]{1,0:T(8,128)(2,1)S(1)}, u32[]{:S(2)}, u32[]{:S(2)}) collective-permute-start(bf16[128,512]{1,0:T(8,128)(2,1)S(1)} %collective-permute-done.11.refs_0_), channel_id=1, source_target_pairs={{0,2},{1,3},{2,4},{3,5},{4,6},{5,7},{8,10},{9,11},{10,12},{11,13},... | collective-permute-start | bytes 393224 | tf_op jit(solution)/shard_map/ppermute | solution.py:507
  18.7 2.2 %collective-permute-start.2 = (bf16[128,256]{1,0:T(8,128)(2,1)S(1)}, bf16[128,256]{1,0:T(8,128)(2,1)S(1)}, u32[]{:S(2)}, u32[]{:S(2)}) collective-permute-start(bf16[128,256]{1,0:T(8,128)(2,1)S(1)} %collective-permute-done.1.mine_x), channel_id=1, source_target_pairs={{0,1},{1,0},{2,3},{3,2},{4,5},{5,4},{6,7},{7,6},{8,9},{9,8},{10,11... | collective-permute-start | bytes 196616 | tf_op jit(solution)/shard_map/ppermute | solution.py:511
  18.8 11.0 %collective-permute-start.10 = (bf16[144,1024]{1,0:T(8,128)(2,1)}, bf16[144,1024]{1,0:T(8,128)(2,1)S(1)}, u32[]{:S(2)}, u32[]{:S(2)}) collective-permute-start(bf16[144,1024]{1,0:T(8,128)(2,1)} %get-tuple-element.18), channel_id=1, source_target_pairs={{0,8},{1,9},{2,10},{3,11},{4,12},{5,13},{6,14},{7,15},{8,16},{9,17... | collective-permute-start | bytes 884744 | tf_op jit(solution)/shard_map/ppermute | solution.py:521
  20.3 1.3 %collective-permute-start.5 = (bf16[128,256]{1,0:T(8,128)(2,1)S(1)}, bf16[128,256]{1,0:T(8,128)(2,1)S(1)}, u32[]{:S(2)}, u32[]{:S(2)}) collective-permute-start(bf16[128,256]{1,0:T(8,128)(2,1)S(1)} %collective-permute-done.4.far), channel_id=1, source_target_pairs={{0,1},{1,0},{2,3},{3,2},{4,5},{5,4},{6,7},{7,6},{8,9},{9,8},{10,11... | collective-permute-start | bytes 196616 | tf_op jit(solution)/shard_map/ppermute | solution.py:511
  20.5 2.0 %collective-permute-start.7 = (bf16[128,256]{1,0:T(8,128)(2,1)S(1)}, bf16[128,256]{1,0:T(8,128)(2,1)S(1)}, u32[]{:S(2)}, u32[]{:S(2)}) collective-permute-start(bf16[128,256]{1,0:T(8,128)(2,1)S(1)} %collective-permute-done.6.beyond), channel_id=1, source_target_pairs={{0,1},{1,0},{2,3},{3,2},{4,5},{5,4},{6,7},{7,6},{8,9},{9,8},{10,11... | collective-permute-start | bytes 196616 | tf_op jit(solution)/shard_map/ppermute | solution.py:511
  20.8 2.3 %collective-permute-start.3 = (bf16[128,256]{1,0:T(8,128)(2,1)S(1)}, bf16[128,256]{1,0:T(8,128)(2,1)S(1)}, u32[]{:S(2)}, u32[]{:S(2)}) collective-permute-start(bf16[128,256]{1,0:T(8,128)(2,1)S(1)} %slice.20), channel_id=1, source_target_pairs={{0,1},{1,0},{2,3},{3,2},{4,5},{5,4},{6,7},{7,6},{8,9},{9,8},{10,11... | collective-permute-start | bytes 196616 | tf_op jit(solution)/shard_map/ppermute | solution.py:511
  21.6 13.4 %collective-permute-start.12 = (bf16[128,512]{1,0:T(8,128)(2,1)S(1)}, bf16[128,512]{1,0:T(8,128)(2,1)S(1)}, u32[]{:S(2)}, u32[]{:S(2)}) collective-permute-start(bf16[128,512]{1,0:T(8,128)(2,1)S(1)} %collective-permute-done.11.refs_0_), channel_id=1, source_target_pairs={{0,1},{1,0},{2,3},{3,2},{4,5},{5,4},{6,7},{7,6},{8,9},{9,8},{10,11... | collective-permute-start | bytes 393224 | tf_op jit(solution)/shard_map/ppermute | solution.py:511
  21.8 12.6 %collective-permute-start.15 = (bf16[128,512]{1,0:T(8,128)(2,1)S(1)}, bf16[128,512]{1,0:T(8,128)(2,1)S(1)}, u32[]{:S(2)}, u32[]{:S(2)}) collective-permute-start(bf16[128,512]{1,0:T(8,128)(2,1)S(1)} %collective-permute-done.13.refs_2_), channel_id=1, source_target_pairs={{2,4},{3,5},{4,6},{5,7},{10,12},{11,13},{12,14},{13,15},{18,20},{1... | collective-permute-start | bytes 393224 | tf_op jit(solution)/shard_map/ppermute | solution.py:507
  22.5 11.9 %collective-permute-start.18 = (bf16[128,512]{1,0:T(8,128)(2,1)S(1)}, bf16[128,512]{1,0:T(8,128)(2,1)S(1)}, u32[]{:S(2)}, u32[]{:S(2)}) collective-permute-start(bf16[128,512]{1,0:T(8,128)(2,1)S(1)} %collective-permute-done.13.refs_2_), channel_id=1, source_target_pairs={{2,6},{3,7},{10,14},{11,15},{18,22},{19,23},{26,30},{27,31}} | collective-permute-start | bytes 393224 | tf_op jit(solution)/shard_map/ppermute | solution.py:507
  24.8 13.4 %collective-permute-start.8 = (bf16[128,512]{1,0:T(8,128)(2,1)S(1)}, bf16[128,512]{1,0:T(8,128)(2,1)S(1)}, u32[]{:S(2)}, u32[]{:S(2)}) collective-permute-start(bf16[128,512]{1,0:T(8,128)(2,1)S(1)} %get-tuple-element.16), channel_id=1, source_target_pairs={{0,8},{1,9},{2,10},{3,11},{4,12},{5,13},{6,14},{7,15},{8,16},{9,17... | collective-permute-start | bytes 393224 | tf_op jit(solution)/shard_map/ppermute | solution.py:521
  29.7 8.4 %collective-permute-start.9 = (bf16[128,512]{1,0:T(8,128)(2,1)S(1)}, bf16[128,512]{1,0:T(8,128)(2,1)S(1)}, u32[]{:S(2)}, u32[]{:S(2)}) collective-permute-start(bf16[128,512]{1,0:T(8,128)(2,1)S(1)} %get-tuple-element.17), channel_id=1, source_target_pairs={{0,10},{1,11},{2,8},{3,9},{4,14},{5,15},{6,12},{7,13},{8,18},{9,19... | collective-permute-start | bytes 393224 | tf_op jit(solution)/shard_map/ppermute | solution.py:521
  34.4 1.3 %collective-permute-start.14 = (bf16[128,512]{1,0:T(8,128)(2,1)S(1)}, bf16[128,512]{1,0:T(8,128)(2,1)S(1)}, u32[]{:S(2)}, u32[]{:S(2)}) collective-permute-start(bf16[128,512]{1,0:T(8,128)(2,1)S(1)} %collective-permute-done.13.refs_2_), channel_id=1, source_target_pairs={{0,1},{1,0},{2,3},{3,2},{4,5},{5,4},{6,7},{7,6},{8,9},{9,8},{10,11... | collective-permute-start | bytes 393224 | tf_op jit(solution)/shard_map/ppermute | solution.py:511
  34.4 1.5 %collective-permute-start.16 = (bf16[128,256]{1,0:T(8,128)(2,1)S(1)}, bf16[128,256]{1,0:T(8,128)(2,1)S(1)}, u32[]{:S(2)}, u32[]{:S(2)}) collective-permute-start(bf16[128,256]{1,0:T(8,128)(2,1)S(1)} %get-tuple-element.24), channel_id=1, source_target_pairs={{0,1},{1,0},{2,3},{3,2},{4,5},{5,4},{6,7},{7,6},{8,9},{9,8},{10,11... | collective-permute-start | bytes 196616 | tf_op jit(solution)/shard_map/ppermute | solution.py:511
  35.0 1.3 %collective-permute-start.17 = (bf16[128,256]{1,0:T(8,128)(2,1)S(1)}, bf16[128,256]{1,0:T(8,128)(2,1)S(1)}, u32[]{:S(2)}, u32[]{:S(2)}) collective-permute-start(bf16[128,256]{1,0:T(8,128)(2,1)S(1)} %get-tuple-element.23), channel_id=1, source_target_pairs={{0,1},{1,0},{2,3},{3,2},{4,5},{5,4},{6,7},{7,6},{8,9},{9,8},{10,11... | collective-permute-start | bytes 196616 | tf_op jit(solution)/shard_map/ppermute | solution.py:511
  35.7 1.3 %collective-permute-start.19 = (bf16[128,256]{1,0:T(8,128)(2,1)S(1)}, bf16[128,256]{1,0:T(8,128)(2,1)S(1)}, u32[]{:S(2)}, u32[]{:S(2)}) collective-permute-start(bf16[128,256]{1,0:T(8,128)(2,1)S(1)} %get-tuple-element.22), channel_id=1, source_target_pairs={{0,1},{1,0},{2,3},{3,2},{4,5},{5,4},{6,7},{7,6},{8,9},{9,8},{10,11... | collective-permute-start | bytes 196616 | tf_op jit(solution)/shard_map/ppermute | solution.py:511
  35.9 1.3 %collective-permute-start.20 = (bf16[128,256]{1,0:T(8,128)(2,1)S(1)}, bf16[128,256]{1,0:T(8,128)(2,1)S(1)}, u32[]{:S(2)}, u32[]{:S(2)}) collective-permute-start(bf16[128,256]{1,0:T(8,128)(2,1)S(1)} %get-tuple-element.21), channel_id=1, source_target_pairs={{0,1},{1,0},{2,3},{3,2},{4,5},{5,4},{6,7},{7,6},{8,9},{9,8},{10,11... | collective-permute-start | bytes 196616 | tf_op jit(solution)/shard_map/ppermute | solution.py:511

commit v7 on v6

--- a/solution.py
+++ b/solution.py
@@ -446,8 +446,8 @@
 
 
 def attend_relayed_kernel(packed, *refs):
-    kvs, (out, bias) = refs[:10], refs[10:]
-    kvs = kvs[:5] + (Halves(*kvs[5:7]), kvs[7], Halves(*kvs[8:]))
+    kvs, (out, bias) = refs[:9], refs[9:]
+    kvs = kvs[:5] + (Halves(*kvs[5:7]), *kvs[7:])
     rows = out.shape[0]
     kept = packed[rows : rows + NOTE_ROWS, :rows].astype(jnp.float32)[1:2]
 
@@ -495,7 +495,7 @@
     return pl.pallas_call(
         attend_relayed_kernel,
         out_shape=jax.ShapeDtypeStruct((rows, width), jnp.bfloat16),
-        in_specs=[vmem] * 11,
+        in_specs=[vmem] * 10,
         out_specs=vmem,
         name="attend_relayed",
         **attend_cost(rows, RELAYED_FLOPS),
@@ -559,13 +559,12 @@
         scored,
     )
     own, partners = onward(own), onward(partners, 2)
-    away = [away, across(away), away_1, across(after(away_1, packed))] + [
-        x for block in (away_2, away_3) for x in (block, *across_halves(block))
-    ]
+    away = [away, across(away), away_1, across(after(away_1, packed)), away_2]
+    away += [*across_halves(away_2), away_3, across(away_3)]
     last = attend_relayed(packed, away)
+    straight = jnp.concatenate([own, partners, last], axis=1)
     crossed = jnp.concatenate([partners, own, last], axis=1)
-    straight = jnp.concatenate([own, partners, last], axis=1)
-    return jnp.where(parity() == 0, straight, crossed)[None]
+    return jnp.where(parity() == 1, crossed, straight)[None]
 
 
 def solution(mesh):

time: 39.3 us -> 39.1 us (level)
    ppermute x11 -> x10, starting transfers between devices: 2.13 us -> 1.76 us  [across(): lax.ppermute(block, 'ctx', [(i, i ^ 1) for i in range(lax.axis_size('ctx'...]
    ppermute x11 -> x10, waiting for transfers between devices: 2.06 us -> 2.3 us  [across(): lax.ppermute(block, 'ctx', [(i, i ^ 1) for i in range(lax.axis_size('ctx'...]
  transfers between devices with their start and end apart: 21 -> 20, of which waited for: 7 -> 6; matrix products, arithmetic and copies ran while one was open for 0% -> 0% of each run, Pallas kernels for 7% -> 7%
where the time goes in v7:
time: 39.1 us; the launch traced here: 38.9 us
  starting transfers between devices  23.7 us (61%)
  Pallas kernels  8.36 us (21%)
  waiting for transfers between devices  5.78 us (15%)
  other arithmetic  0.9 us (2%)
    ppermute x6, starting transfers between devices, send(): return lax.ppermute(block, 'ctx', pairs)  12.7 us
    ppermute x4, starting transfers between devices, onward(): return lax.ppermute(block, ('phase', 'ctx'), route)  9.23 us
    pallas_call x1, Pallas kernels, project(): pl.pallas_call(functools.partial(project_kernel, cuts), out_shape=[jax.Sh...  5.77 us
    ppermute x4, waiting for transfers between devices, onward(): return lax.ppermute(block, ('phase', 'ctx'), route)  3.41 us
    ppermute x10, waiting for transfers between devices, across(): lax.ppermute(block, 'ctx', [(i, i ^ 1) for i in range(lax.axis_size('ctx'...  2.3 us
    ppermute x10, starting transfers between devices, across(): lax.ppermute(block, 'ctx', [(i, i ^ 1) for i in range(lax.axis_size('ctx'...  1.76 us
    pallas_call x1, Pallas kernels, attend_home(): pl.pallas_call(attend_home_kernel, grid=(1,), out_shape=(out, out), in_sp...  1.6 us
    pallas_call x1, Pallas kernels, attend_relayed(): pl.pallas_call(attend_relayed_kernel, out_shape=jax.ShapeDtypeStruct((row...  0.99 us
  transfers between devices with their start and end apart: 20, of which 6 were waited for; matrix products, arithmetic and copies ran while one was open for 0% of the time, Pallas kernels for 7%

profile of v7, /device:TPU:0, one launch (start us, length us, event | category | flops | bytes accessed | tf_op | source)
XLA Modules:
  0.0 38.9 jit_solution(4451057798921594811)
XLA Ops:
  0.0 0.0 copy-start
  0.0 5.8 %project.1 = (bf16[128,256]{1,0:T(8,128)(2,1)}, bf16[128,256]{1,0:T(8,128)(2,1)}, bf16[144,768]{1,0:T(8,128)(2,1)}, bf16[128,512]{1,0:T(8,128)(2,1)}, bf16[144,1024]{1,0:T(8,128)(2,1)}) custom-call(bf16[1,128,4096]{2,1,0:T(8,128)(2,1)} %hidden.1, bf16[1,4096,1024]{2,1,0:T(8,128)(2,1)} %weight.1, bf16[1,128,2048]{2,1,0:T(8,128)(2,1)} %queries.3, ...), custom_call_target="tpu_custom_call" | custom-call | tf_op jit(solution)/shard_map/project/pallas_call | solution.py:266
  5.8 3.1 %collective-permute-start = (bf16[144,768]{1,0:T(8,128)(2,1)}, bf16[144,768]{1,0:T(8,128)(2,1)S(1)}, u32[]{:S(2)}, u32[]{:S(2)}) collective-permute-start(bf16[144,768]{1,0:T(8,128)(2,1)} %get-tuple-element.13), channel_id=1, source_target_pairs={{0,2},{1,3},{2,0},{3,1},{4,6},{5,7},{6,4},{7,5},{8,10},{9,11},{10,... | collective-permute-start | bytes 663560 | tf_op jit(solution)/shard_map/ppermute | solution.py:507
  8.9 1.5 %collective-permute-start.11 = (bf16[128,512]{1,0:T(8,128)(2,1)}, bf16[128,512]{1,0:T(8,128)(2,1)S(1)}, u32[]{:S(2)}, u32[]{:S(2)}) collective-permute-start(bf16[128,512]{1,0:T(8,128)(2,1)} %get-tuple-element.19), channel_id=1, source_target_pairs={{0,8},{1,9},{2,10},{3,11},{4,12},{5,13},{6,14},{7,15},{8,16},{9,17... | collective-permute-start | bytes 393224 | tf_op jit(solution)/shard_map/ppermute | solution.py:521
  10.4 0.0 collective-permute-start.1
  10.4 4.5 %collective-permute-start.4 = (bf16[128,256]{1,0:T(8,128)(2,1)}, bf16[128,256]{1,0:T(8,128)(2,1)S(1)}, u32[]{:S(2)}, u32[]{:S(2)}) collective-permute-start(bf16[128,256]{1,0:T(8,128)(2,1)} %get-tuple-element.14), channel_id=1, source_target_pairs={{0,4},{1,5},{2,6},{3,7},{8,12},{9,13},{10,14},{11,15},{16,20},{17,... | collective-permute-start | bytes 196616 | tf_op jit(solution)/shard_map/ppermute | solution.py:507
  14.9 1.3 %collective-permute-start.6 = (bf16[128,256]{1,0:T(8,128)(2,1)}, bf16[128,256]{1,0:T(8,128)(2,1)S(1)}, u32[]{:S(2)}, u32[]{:S(2)}) collective-permute-start(bf16[128,256]{1,0:T(8,128)(2,1)} %get-tuple-element.15), channel_id=1, source_target_pairs={{0,6},{1,7},{2,4},{3,5},{8,14},{9,15},{10,12},{11,13},{16,22},{17,... | collective-permute-start | bytes 196616 | tf_op jit(solution)/shard_map/ppermute | solution.py:507
  16.2 0.0 collective-permute-done.11.refs_0_
  16.2 2.5 %collective-permute-start.13 = (bf16[128,512]{1,0:T(8,128)(2,1)S(1)}, bf16[128,512]{1,0:T(8,128)(2,1)S(1)}, u32[]{:S(2)}, u32[]{:S(2)}) collective-permute-start(bf16[128,512]{1,0:T(8,128)(2,1)S(1)} %collective-permute-done.11.refs_0_), channel_id=1, source_target_pairs={{0,2},{1,3},{2,4},{3,5},{4,6},{5,7},{8,10},{9,11},{10,12},{11,13},... | collective-permute-start | bytes 393224 | tf_op jit(solution)/shard_map/ppermute | solution.py:507
  18.7 0.0 collective-permute-done.1.mine_x
  18.7 0.1 collective-permute-start.2
  18.8 0.0 collective-permute-done.4.far
  18.8 1.5 %collective-permute-start.10 = (bf16[144,1024]{1,0:T(8,128)(2,1)}, bf16[144,1024]{1,0:T(8,128)(2,1)S(1)}, u32[]{:S(2)}, u32[]{:S(2)}) collective-permute-start(bf16[144,1024]{1,0:T(8,128)(2,1)} %get-tuple-element.18), channel_id=1, source_target_pairs={{0,8},{1,9},{2,10},{3,11},{4,12},{5,13},{6,14},{7,15},{8,16},{9,17... | collective-permute-start | bytes 884744 | tf_op jit(solution)/shard_map/ppermute | solution.py:521
  20.3 0.0 collective-permute-done.6.beyond
  20.3 0.2 collective-permute-start.5
  20.5 0.0 collective-permute-done.swap
  20.5 0.4 collective-permute-start.7
  20.8 0.0 collective-permute-done.2.mine
  20.8 0.2 collective-permute-start.3
  21.1 0.5 %collective-permute-done.5.far_x = bf16[128,256]{1,0:T(8,128)(2,1)S(1)} collective-permute-done((bf16[128,256]{1,0:T(8,128)(2,1)S(1)}, bf16[128,256]{1,0:T(8,128)(2,1)S(1)}, u32[]{:S(2)}, u32[]{:S(2)}) %collective-permute-start.5) | collective-permute-done | bytes 65568 | tf_op jit(solution)/shard_map/ppermute | solution.py:511
  21.6 0.2 collective-permute-start.12
  21.7 0.1 collective-permute-done.13.refs_2_
  21.8 0.7 %collective-permute-start.15 = (bf16[128,512]{1,0:T(8,128)(2,1)S(1)}, bf16[128,512]{1,0:T(8,128)(2,1)S(1)}, u32[]{:S(2)}, u32[]{:S(2)}) collective-permute-start(bf16[128,512]{1,0:T(8,128)(2,1)S(1)} %collective-permute-done.13.refs_2_), channel_id=1, source_target_pairs={{2,4},{3,5},{4,6},{5,7},{10,12},{11,13},{12,14},{13,15},{18,20},{1... | collective-permute-start | bytes 393224 | tf_op jit(solution)/shard_map/ppermute | solution.py:507
  22.5 0.0 collective-permute-done.7.beyond_x
  22.5 0.7 %collective-permute-start.18 = (bf16[128,512]{1,0:T(8,128)(2,1)S(1)}, bf16[128,512]{1,0:T(8,128)(2,1)S(1)}, u32[]{:S(2)}, u32[]{:S(2)}) collective-permute-start(bf16[128,512]{1,0:T(8,128)(2,1)S(1)} %collective-permute-done.13.refs_2_), channel_id=1, source_target_pairs={{2,6},{3,7},{10,14},{11,15},{18,22},{19,23},{26,30},{27,31}} | collective-permute-start | bytes 393224 | tf_op jit(solution)/shard_map/ppermute | solution.py:507
  23.1 0.0 collective-permute-done.3.near_x
  23.2 0.0 copy-done
  23.2 0.0 copy-done.1
  23.2 0.0 copy-done.2
  23.2 1.6 %attend_home.1 = (bf16[128,512]{1,0:T(8,128)(2,1)S(1)}, bf16[128,512]{1,0:T(8,128)(2,1)S(1)}) custom-call(bf16[1,128,2048]{2,1,0:T(8,128)(2,1)S(1)} %copy-done, bf16[144,768]{1,0:T(8,128)(2,1)S(1)} %collective-permute-done.swap, bf16[128,256]{1,0:T(8,128)(2,1)S(1)} %collective-permute-done.2.mine, bf16[128,256]{1,0:T(8,128)(2,1)S(1)} %collective-permute-done.1.mine_x, ...), custom_call_target="tpu_custom_call" | custom-call | flops 1900000000 | tf_op jit(solution)/shard_map/attend_home/pallas_call | solution.py:480
  24.8 1.6 %collective-permute-start.9 = (bf16[128,512]{1,0:T(8,128)(2,1)S(1)}, bf16[128,512]{1,0:T(8,128)(2,1)S(1)}, u32[]{:S(2)}, u32[]{:S(2)}) collective-permute-start(bf16[128,512]{1,0:T(8,128)(2,1)S(1)} %get-tuple-element.17), channel_id=1, source_target_pairs={{0,8},{1,9},{2,10},{3,11},{4,12},{5,13},{6,14},{7,15},{8,16},{9,17... | collective-permute-start | bytes 393224 | tf_op jit(solution)/shard_map/ppermute | solution.py:521
  26.3 3.4 %collective-permute-done.10.packed = bf16[144,1024]{1,0:T(8,128)(2,1)S(1)} collective-permute-done((bf16[144,1024]{1,0:T(8,128)(2,1)}, bf16[144,1024]{1,0:T(8,128)(2,1)S(1)}, u32[]{:S(2)}, u32[]{:S(2)}) %collective-permute-start.10) | collective-permute-done | bytes 294944 | tf_op jit(solution)/shard_map/ppermute | solution.py:521
  29.7 4.6 %collective-permute-start.8 = (bf16[128,512]{1,0:T(8,128)(2,1)S(1)}, bf16[128,512]{1,0:T(8,128)(2,1)S(1)}, u32[]{:S(2)}, u32[]{:S(2)}) collective-permute-start(bf16[128,512]{1,0:T(8,128)(2,1)S(1)} %get-tuple-element.16), channel_id=1, source_target_pairs={{0,10},{1,11},{2,8},{3,9},{4,14},{5,15},{6,12},{7,13},{8,18},{9,19... | collective-permute-start | bytes 393224 | tf_op jit(solution)/shard_map/ppermute | solution.py:521
  34.4 0.0 collective-permute-done.15.refs_4_
  34.4 0.0 collective-permute-start.14
  34.4 0.0 collective-permute-done.18.refs_7_
  34.4 0.5 %collective-permute-start.19 = (bf16[128,512]{1,0:T(8,128)(2,1)S(1)}, bf16[128,512]{1,0:T(8,128)(2,1)S(1)}, u32[]{:S(2)}, u32[]{:S(2)}) collective-permute-start(bf16[128,512]{1,0:T(8,128)(2,1)S(1)} %collective-permute-done.18.refs_7_), channel_id=1, source_target_pairs={{0,1},{1,0},{2,3},{3,2},{4,5},{5,4},{6,7},{7,6},{8,9},{9,8},{10,11... | collective-permute-start | bytes 393224 | tf_op jit(solution)/shard_map/ppermute | solution.py:511
  34.9 0.0 collective-permute-done.12.refs_1_
  34.9 0.1 collective-permute-start.16
  35.1 0.7 %collective-permute-done.14.refs_3_ = bf16[128,512]{1,0:T(8,128)(2,1)S(1)} collective-permute-done((bf16[128,512]{1,0:T(8,128)(2,1)S(1)}, bf16[128,512]{1,0:T(8,128)(2,1)S(1)}, u32[]{:S(2)}, u32[]{:S(2)}) %collective-permute-start.14) | collective-permute-done | bytes 131104 | tf_op jit(solution)/shard_map/ppermute | solution.py:511
  35.7 0.1 collective-permute-start.17
  35.9 0.4 collective-permute-done.16.refs_5_
  36.2 0.7 %collective-permute-done.17.refs_6_ = bf16[128,256]{1,0:T(8,128)(2,1)S(1)} collective-permute-done((bf16[128,256]{1,0:T(8,128)(2,1)S(1)}, bf16[128,256]{1,0:T(8,128)(2,1)S(1)}, u32[]{:S(2)}, u32[]{:S(2)}) %collective-permute-start.17) | collective-permute-done | bytes 65568 | tf_op jit(solution)/shard_map/ppermute | solution.py:511
  37.0 0.0 collective-permute-done.19.refs_8_
  37.0 1.0 %attend_relayed.1 = bf16[128,1024]{1,0:T(8,128)(2,1)S(1)} custom-call(bf16[144,1024]{1,0:T(8,128)(2,1)S(1)} %collective-permute-done.10.packed, bf16[128,512]{1,0:T(8,128)(2,1)S(1)} %collective-permute-done.11.refs_0_, bf16[128,512]{1,0:T(8,128)(2,1)S(1)} %collective-permute-done.12.refs_1_, bf16[128,512]{1,0:T(8,128)(2,1)S(1)} %collective-permute-done.13.refs_2_, ...), custom_call_target="tpu_custom_call" | custom-call | tf_op jit(solution)/shard_map/attend_relayed/pallas_call | solution.py:495
  38.0 0.0 collective-permute-done.9
  38.0 0.0 collective-permute-done.8
  38.0 0.9 %fusion = bf16[1,128,2048]{2,1,0:T(8,128)(2,1)} fusion(bf16[1,128,1024]{2,1,0:T(8,128)(2,1)S(1)} %bitcast.3, bf16[1,128,512]{2,1,0:T(8,128)(2,1)S(1)} %bitcast.4, bf16[1,128,512]{2,1,0:T(8,128)(2,1)S(1)} %bitcast.5, pred[]{:T(512)S(6)} %eq.3), kind=kLoop, calls=%fused_computation.2 | loop fusion | flops 3145728 | bytes 1048577 | tf_op jit(solution)/shard_map/jit(_where)/select_n | solution.py:567
  (4 shorter events, 0.0 us)
Async XLA Ops:
  0.0 23.2 %copy-start = (bf16[1,128,2048]{2,1,0:T(8,128)(2,1)S(1)}, bf16[1,128,2048]{2,1,0:T(8,128)(2,1)}, u32[]{:S(2)}) copy-start(bf16[1,128,2048]{2,1,0:T(8,128)(2,1)} %queries.3) | copy-start | bytes 1572868
  0.0 23.2 %copy-start.1 = (s32[1,1024]{1,0:T(1,128)S(1)}, s32[1,1024]{1,0:T(1,128)}, u32[]{:S(2)}) copy-start(s32[1,1024]{1,0:T(1,128)} %docs.3) | copy-start | bytes 12292
  0.0 23.2 %copy-start.2 = (s32[1,128]{1,0:T(1,128)S(1)}, s32[1,128]{1,0:T(1,128)}, u32[]{:S(2)}) copy-start(s32[1,128]{1,0:T(1,128)} %scored.3) | copy-start | bytes 1540
  5.8 14.7 %collective-permute-start = (bf16[144,768]{1,0:T(8,128)(2,1)}, bf16[144,768]{1,0:T(8,128)(2,1)S(1)}, u32[]{:S(2)}, u32[]{:S(2)}) collective-permute-start(bf16[144,768]{1,0:T(8,128)(2,1)} %get-tuple-element.13), channel_id=1, source_target_pairs={{0,2},{1,3},{2,0},{3,1},{4,6},{5,7},{6,4},{7,5},{8,10},{9,11},{10,... | collective-permute-start | bytes 663560 | tf_op jit(solution)/shard_map/ppermute | solution.py:507
  8.9 7.3 %collective-permute-start.11 = (bf16[128,512]{1,0:T(8,128)(2,1)}, bf16[128,512]{1,0:T(8,128)(2,1)S(1)}, u32[]{:S(2)}, u32[]{:S(2)}) collective-permute-start(bf16[128,512]{1,0:T(8,128)(2,1)} %get-tuple-element.19), channel_id=1, source_target_pairs={{0,8},{1,9},{2,10},{3,11},{4,12},{5,13},{6,14},{7,15},{8,16},{9,17... | collective-permute-start | bytes 393224 | tf_op jit(solution)/shard_map/ppermute | solution.py:521
  10.4 8.3 %collective-permute-start.1 = (bf16[128,256]{1,0:T(8,128)(2,1)}, bf16[128,256]{1,0:T(8,128)(2,1)S(1)}, u32[]{:S(2)}, u32[]{:S(2)}) collective-permute-start(bf16[128,256]{1,0:T(8,128)(2,1)} %get-tuple-element.14), channel_id=1, source_target_pairs={{0,1},{1,0},{2,3},{3,2},{4,5},{5,4},{6,7},{7,6},{8,9},{9,8},{10,11... | collective-permute-start | bytes 196616 | tf_op jit(solution)/shard_map/ppermute | solution.py:511
  10.4 8.4 %collective-permute-start.4 = (bf16[128,256]{1,0:T(8,128)(2,1)}, bf16[128,256]{1,0:T(8,128)(2,1)S(1)}, u32[]{:S(2)}, u32[]{:S(2)}) collective-permute-start(bf16[128,256]{1,0:T(8,128)(2,1)} %get-tuple-element.14), channel_id=1, source_target_pairs={{0,4},{1,5},{2,6},{3,7},{8,12},{9,13},{10,14},{11,15},{16,20},{17,... | collective-permute-start | bytes 196616 | tf_op jit(solution)/shard_map/ppermute | solution.py:507
  14.9 5.4 %collective-permute-start.6 = (bf16[128,256]{1,0:T(8,128)(2,1)}, bf16[128,256]{1,0:T(8,128)(2,1)S(1)}, u32[]{:S(2)}, u32[]{:S(2)}) collective-permute-start(bf16[128,256]{1,0:T(8,128)(2,1)} %get-tuple-element.15), channel_id=1, source_target_pairs={{0,6},{1,7},{2,4},{3,5},{8,14},{9,15},{10,12},{11,13},{16,22},{17,... | collective-permute-start | bytes 196616 | tf_op jit(solution)/shard_map/ppermute | solution.py:507
  16.2 5.6 %collective-permute-start.13 = (bf16[128,512]{1,0:T(8,128)(2,1)S(1)}, bf16[128,512]{1,0:T(8,128)(2,1)S(1)}, u32[]{:S(2)}, u32[]{:S(2)}) collective-permute-start(bf16[128,512]{1,0:T(8,128)(2,1)S(1)} %collective-permute-done.11.refs_0_), channel_id=1, source_target_pairs={{0,2},{1,3},{2,4},{3,5},{4,6},{5,7},{8,10},{9,11},{10,12},{11,13},... | collective-permute-start | bytes 393224 | tf_op jit(solution)/shard_map/ppermute | solution.py:507
  18.7 2.2 %collective-permute-start.2 = (bf16[128,256]{1,0:T(8,128)(2,1)S(1)}, bf16[128,256]{1,0:T(8,128)(2,1)S(1)}, u32[]{:S(2)}, u32[]{:S(2)}) collective-permute-start(bf16[128,256]{1,0:T(8,128)(2,1)S(1)} %collective-permute-done.1.mine_x), channel_id=1, source_target_pairs={{0,1},{1,0},{2,3},{3,2},{4,5},{5,4},{6,7},{7,6},{8,9},{9,8},{10,11... | collective-permute-start | bytes 196616 | tf_op jit(solution)/shard_map/ppermute | solution.py:511
  18.8 11.0 %collective-permute-start.10 = (bf16[144,1024]{1,0:T(8,128)(2,1)}, bf16[144,1024]{1,0:T(8,128)(2,1)S(1)}, u32[]{:S(2)}, u32[]{:S(2)}) collective-permute-start(bf16[144,1024]{1,0:T(8,128)(2,1)} %get-tuple-element.18), channel_id=1, source_target_pairs={{0,8},{1,9},{2,10},{3,11},{4,12},{5,13},{6,14},{7,15},{8,16},{9,17... | collective-permute-start | bytes 884744 | tf_op jit(solution)/shard_map/ppermute | solution.py:521
  20.3 1.3 %collective-permute-start.5 = (bf16[128,256]{1,0:T(8,128)(2,1)S(1)}, bf16[128,256]{1,0:T(8,128)(2,1)S(1)}, u32[]{:S(2)}, u32[]{:S(2)}) collective-permute-start(bf16[128,256]{1,0:T(8,128)(2,1)S(1)} %collective-permute-done.4.far), channel_id=1, source_target_pairs={{0,1},{1,0},{2,3},{3,2},{4,5},{5,4},{6,7},{7,6},{8,9},{9,8},{10,11... | collective-permute-start | bytes 196616 | tf_op jit(solution)/shard_map/ppermute | solution.py:511
  20.5 2.0 %collective-permute-start.7 = (bf16[128,256]{1,0:T(8,128)(2,1)S(1)}, bf16[128,256]{1,0:T(8,128)(2,1)S(1)}, u32[]{:S(2)}, u32[]{:S(2)}) collective-permute-start(bf16[128,256]{1,0:T(8,128)(2,1)S(1)} %collective-permute-done.6.beyond), channel_id=1, source_target_pairs={{0,1},{1,0},{2,3},{3,2},{4,5},{5,4},{6,7},{7,6},{8,9},{9,8},{10,11... | collective-permute-start | bytes 196616 | tf_op jit(solution)/shard_map/ppermute | solution.py:511
  20.8 2.3 %collective-permute-start.3 = (bf16[128,256]{1,0:T(8,128)(2,1)S(1)}, bf16[128,256]{1,0:T(8,128)(2,1)S(1)}, u32[]{:S(2)}, u32[]{:S(2)}) collective-permute-start(bf16[128,256]{1,0:T(8,128)(2,1)S(1)} %slice.12), channel_id=1, source_target_pairs={{0,1},{1,0},{2,3},{3,2},{4,5},{5,4},{6,7},{7,6},{8,9},{9,8},{10,11... | collective-permute-start | bytes 196616 | tf_op jit(solution)/shard_map/ppermute | solution.py:511
  21.6 13.3 %collective-permute-start.12 = (bf16[128,512]{1,0:T(8,128)(2,1)S(1)}, bf16[128,512]{1,0:T(8,128)(2,1)S(1)}, u32[]{:S(2)}, u32[]{:S(2)}) collective-permute-start(bf16[128,512]{1,0:T(8,128)(2,1)S(1)} %collective-permute-done.11.refs_0_), channel_id=1, source_target_pairs={{0,1},{1,0},{2,3},{3,2},{4,5},{5,4},{6,7},{7,6},{8,9},{9,8},{10,11... | collective-permute-start | bytes 393224 | tf_op jit(solution)/shard_map/ppermute | solution.py:511
  21.8 12.6 %collective-permute-start.15 = (bf16[128,512]{1,0:T(8,128)(2,1)S(1)}, bf16[128,512]{1,0:T(8,128)(2,1)S(1)}, u32[]{:S(2)}, u32[]{:S(2)}) collective-permute-start(bf16[128,512]{1,0:T(8,128)(2,1)S(1)} %collective-permute-done.13.refs_2_), channel_id=1, source_target_pairs={{2,4},{3,5},{4,6},{5,7},{10,12},{11,13},{12,14},{13,15},{18,20},{1... | collective-permute-start | bytes 393224 | tf_op jit(solution)/shard_map/ppermute | solution.py:507
  22.5 11.9 %collective-permute-start.18 = (bf16[128,512]{1,0:T(8,128)(2,1)S(1)}, bf16[128,512]{1,0:T(8,128)(2,1)S(1)}, u32[]{:S(2)}, u32[]{:S(2)}) collective-permute-start(bf16[128,512]{1,0:T(8,128)(2,1)S(1)} %collective-permute-done.13.refs_2_), channel_id=1, source_target_pairs={{2,6},{3,7},{10,14},{11,15},{18,22},{19,23},{26,30},{27,31}} | collective-permute-start | bytes 393224 | tf_op jit(solution)/shard_map/ppermute | solution.py:507
  24.8 13.2 %collective-permute-start.9 = (bf16[128,512]{1,0:T(8,128)(2,1)S(1)}, bf16[128,512]{1,0:T(8,128)(2,1)S(1)}, u32[]{:S(2)}, u32[]{:S(2)}) collective-permute-start(bf16[128,512]{1,0:T(8,128)(2,1)S(1)} %get-tuple-element.17), channel_id=1, source_target_pairs={{0,8},{1,9},{2,10},{3,11},{4,12},{5,13},{6,14},{7,15},{8,16},{9,17... | collective-permute-start | bytes 393224 | tf_op jit(solution)/shard_map/ppermute | solution.py:521
  29.7 8.3 %collective-permute-start.8 = (bf16[128,512]{1,0:T(8,128)(2,1)S(1)}, bf16[128,512]{1,0:T(8,128)(2,1)S(1)}, u32[]{:S(2)}, u32[]{:S(2)}) collective-permute-start(bf16[128,512]{1,0:T(8,128)(2,1)S(1)} %get-tuple-element.16), channel_id=1, source_target_pairs={{0,10},{1,11},{2,8},{3,9},{4,14},{5,15},{6,12},{7,13},{8,18},{9,19... | collective-permute-start | bytes 393224 | tf_op jit(solution)/shard_map/ppermute | solution.py:521
  34.4 1.3 %collective-permute-start.14 = (bf16[128,512]{1,0:T(8,128)(2,1)S(1)}, bf16[128,512]{1,0:T(8,128)(2,1)S(1)}, u32[]{:S(2)}, u32[]{:S(2)}) collective-permute-start(bf16[128,512]{1,0:T(8,128)(2,1)S(1)} %collective-permute-done.13.refs_2_), channel_id=1, source_target_pairs={{0,1},{1,0},{2,3},{3,2},{4,5},{5,4},{6,7},{7,6},{8,9},{9,8},{10,11... | collective-permute-start | bytes 393224 | tf_op jit(solution)/shard_map/ppermute | solution.py:511
  34.4 2.6 %collective-permute-start.19 = (bf16[128,512]{1,0:T(8,128)(2,1)S(1)}, bf16[128,512]{1,0:T(8,128)(2,1)S(1)}, u32[]{:S(2)}, u32[]{:S(2)}) collective-permute-start(bf16[128,512]{1,0:T(8,128)(2,1)S(1)} %collective-permute-done.18.refs_7_), channel_id=1, source_target_pairs={{0,1},{1,0},{2,3},{3,2},{4,5},{5,4},{6,7},{7,6},{8,9},{9,8},{10,11... | collective-permute-start | bytes 393224 | tf_op jit(solution)/shard_map/ppermute | solution.py:511
  34.9 1.3 %collective-permute-start.16 = (bf16[128,256]{1,0:T(8,128)(2,1)S(1)}, bf16[128,256]{1,0:T(8,128)(2,1)S(1)}, u32[]{:S(2)}, u32[]{:S(2)}) collective-permute-start(bf16[128,256]{1,0:T(8,128)(2,1)S(1)} %get-tuple-element.22), channel_id=1, source_target_pairs={{0,1},{1,0},{2,3},{3,2},{4,5},{5,4},{6,7},{7,6},{8,9},{9,8},{10,11... | collective-permute-start | bytes 196616 | tf_op jit(solution)/shard_map/ppermute | solution.py:511
  35.7 1.3 %collective-permute-start.17 = (bf16[128,256]{1,0:T(8,128)(2,1)S(1)}, bf16[128,256]{1,0:T(8,128)(2,1)S(1)}, u32[]{:S(2)}, u32[]{:S(2)}) collective-permute-start(bf16[128,256]{1,0:T(8,128)(2,1)S(1)} %get-tuple-element.21), channel_id=1, source_target_pairs={{0,1},{1,0},{2,3},{3,2},{4,5},{5,4},{6,7},{7,6},{8,9},{9,8},{10,11... | collective-permute-start | bytes 196616 | tf_op jit(solution)/shard_map/ppermute | solution.py:511
